TPU v7x, 32 devices: a whole 2x2x4 slice. The times are simulated.
32 devices in a mesh: dp: 2 (over y), expert: 16 (over z, x, core).
Axes of the slice: x: 2, y: 2, z: 4, core: 2. Of those that a mesh axis runs over, the one named last changes fastest.
Arguments:
- tokens: bfloat16 [4096, 1920], P(('dp', 'expert')), may hold values from -10 to 10
- assignment: int32 [4096], P(('dp', 'expert')), may hold values from 0 to 15, as said below
- centroids: bfloat16 [16, 1920], P('expert'), may hold values from -0.125 to 0.125
- norm_gain: float32 [16, 1920], P('expert'), may hold values from 0.25 to 1.75
- inner_weight: bfloat16 [16, 4096, 1920], P('expert', 'dp'), may hold values from -0.125 to 0.125
- outer_weight: bfloat16 [16, 4096, 1920], P('expert', 'dp'), may hold values from -0.09375 to 0.09375
Outputs:
- layer_out: bfloat16 [4096, 1920], P(('dp', 'expert'))
Inputs may be any that keep to these rules, and one draw needn't show every extreme that they name: `assignment`: each expert is assigned exactly 128 of the tokens of the devices that share one index of dp. One device assigns at most 16 of its tokens to one expert, and every expert gets exactly 16 tokens from some device of each index of dp.
All inputs are finite; a program needn't handle non-finite values.
Results may differ from a plain program's by a relative error of at most 0.007.
Values may be sent and summed in bfloat16 or wider, within the bound.
No kernel may reach another device: no remote copies, remote signals or barrier semaphores. Data moves between devices by JAX's collectives and lax.ppermute only.
A program may use at most 64 MiB of HBM per device.

v0:
```python
import jax
import jax.numpy as jnp
from jax import lax
from jax.sharding import PartitionSpec as P

epsilon = 1e-05


def normalize(rows_in, gain_row):
    values = rows_in.astype(jnp.float32)
    center = jnp.mean(values, axis=1, keepdims=True)
    spread = jnp.mean(jnp.square(values - center), axis=1, keepdims=True)
    return ((values - center) * lax.rsqrt(spread + epsilon) * gain_row).astype(jnp.bfloat16)


def expert_rows(normed, inner_mat, outer_mat):
    inner_act = lax.dot_general(
        normed, inner_mat, (((1,), (1,)), ((), ())), preferred_element_type=jnp.float32
    )
    hidden = jnp.maximum(inner_act, 0.0).astype(jnp.bfloat16)
    return jnp.dot(hidden, outer_mat, preferred_element_type=jnp.float32)


def body(tokens, assignment, centroids, norm_gain, inner_weight, outer_weight):
    tok_count = tokens.shape[0]
    experts = lax.axis_size("expert")
    capacity = 2 * tok_count // experts
    slot_total = experts * capacity
    expert_ids = jnp.arange(experts, dtype=jnp.int32)
    token_ids = jnp.arange(tok_count, dtype=jnp.int32)
    slot_ids = jnp.arange(slot_total, dtype=jnp.int32)
    onehot = (assignment[:, None] == expert_ids[None, :]).astype(jnp.int32)
    before = jnp.cumsum(onehot, axis=0) - onehot
    position = jnp.sum(before * onehot, axis=1)
    send_counts = jnp.sum(onehot, axis=0)
    slot_of = assignment * capacity + position
    matches = slot_of[None, :] == slot_ids[:, None]
    occupied = jnp.any(matches, axis=1)
    source_row = jnp.sum(jnp.where(matches, token_ids[None, :], 0), axis=1)
    outgoing = jnp.where(
        occupied[:, None], jnp.take(tokens, source_row, axis=0), jnp.zeros((), jnp.bfloat16)
    )
    arrived, arrived_counts = (
        lax.all_to_all(outgoing, "expert", split_axis=0, concat_axis=0, tiled=True),
        lax.all_to_all(send_counts, "expert", split_axis=0, concat_axis=0, tiled=True),
    )
    inclusive = jnp.cumsum(arrived_counts)
    offsets = inclusive - arrived_counts
    sender = jnp.sum((inclusive[None, :] <= token_ids[:, None]).astype(jnp.int32), axis=1)
    within = token_ids - offsets[sender]
    local_rows = jnp.take(arrived, sender * capacity + within, axis=0)
    inner_mat = inner_weight[0]
    outer_mat = outer_weight[0]
    partial_value = expert_rows(
        normalize(lax.all_gather(local_rows, "dp", axis=0, tiled=True), norm_gain),
        inner_mat,
        outer_mat,
    )
    expert_out = lax.psum_scatter(
        partial_value.astype(jnp.bfloat16), "dp", scatter_dimension=0, tiled=True
    )
    slot_sender = slot_ids // capacity
    slot_within = slot_ids % capacity
    slot_live = slot_within < arrived_counts[slot_sender]
    compact = jnp.where(slot_live, offsets[slot_sender] + slot_within, 0)
    returning = jnp.where(
        slot_live[:, None], jnp.take(expert_out, compact, axis=0), jnp.zeros((), jnp.bfloat16)
    )
    local_score = jnp.dot(local_rows, centroids[0], preferred_element_type=jnp.float32)
    local_gate = jax.nn.sigmoid(local_score).astype(jnp.bfloat16)
    gate_slots = jnp.where(slot_live, jnp.take(local_gate, compact), jnp.zeros((), jnp.bfloat16))
    back_rows, back_gate = (
        lax.all_to_all(returning, "expert", split_axis=0, concat_axis=0, tiled=True),
        lax.all_to_all(gate_slots, "expert", split_axis=0, concat_axis=0, tiled=True),
    )
    gate_value = jnp.take(back_gate, slot_of)
    combined = jnp.take(back_rows, slot_of, axis=0)
    mixed_out = tokens.astype(jnp.float32) + gate_value.astype(jnp.float32)[
        :, None
    ] * combined.astype(jnp.float32)
    return mixed_out.astype(jnp.bfloat16)


def solution(mesh):
    in_specs = (
        P(("dp", "expert"), None),
        P(("dp", "expert")),
        P("expert", None),
        P("expert", None),
        P("expert", "dp", None),
        P("expert", "dp", None),
    )
    out_specs = P(("dp", "expert"), None)
    return jax.shard_map(body, mesh=mesh, in_specs=in_specs, out_specs=out_specs, check_vma=False)
```

profile of v0, /device:TPU:1, one launch (start us, length us, event | category | flops | bytes accessed | tf_op | source)
XLA Modules:
  0.0 148.8 jit_solution(3395434690500029310)
XLA Ops:
  6.5 0.0 copy-start
  6.5 0.7 fusion.32
  7.3 0.2 reduce_window_sum.18
  7.5 0.8 fusion.33
  8.3 0.7 copy.15
  9.0 7.3 %all-to-all-start = ((s32[16,1,1]{2,1,0:T(1,128)}), s32[16,1,1]{2,1,0:T(1,128)S(1)}, u32[]{:S(2)}, u32[]{:S(2)}) async-start(s32[16,1,1]{2,1,0:T(1,128)} %copy.15), calls=%async_computation | async-start | bytes 16384 | tf_op jit(solution)/shard_map/all_to_all | solution.py:45
  16.3 0.7 compare_select_fusion.8
  17.0 0.1 select_reduce_fusion
  17.1 0.1 fusion.31
  17.2 3.4 %gather_fusion.2 = bf16[256,1920]{1,0:T(8,128)(2,1)S(1)} fusion(bf16[128,1920]{1,0:T(8,128)(2,1)} %param.10, s32[1024]{0:T(1024)S(1)} %pad_clamp_fusion.4), kind=kCustom, calls=%fused_computation.clone | custom fusion | bytes 1967104 | tf_op jit(solution)/shard_map/jit(_take)/gather | solution.py:41
  20.7 0.0 copy-start.2
  20.7 1.2 select_select_fusion.1
  21.9 0.1 all-to-all-done
  22.0 5.9 %all-to-all-start.1 = ((bf16[16,16,1920]{2,1,0:T(8,128)(2,1)}), bf16[16,16,1920]{2,1,0:T(8,128)(2,1)S(1)}, u32[]{:S(2)}, u32[]{:S(2)}) async-start(bf16[16,16,1920]{2,1,0:T(8,128)(2,1)} %bitcast.47), calls=%async_computation.1 | async-start | bytes 1966080 | tf_op jit(solution)/shard_map/all_to_all | solution.py:44
  27.9 0.0 reduce-scatter.2.cloned.1.call-start
  28.0 0.0 copy-done.2
  28.0 0.1 reduce.9
  28.2 0.4 reduce.10
  28.6 0.7 fusion.45
  29.3 0.1 convert_reduce_fusion.1
  29.4 9.9 %compare_and_fusion.1 = (pred[128]{0:T(512)(128)(4,1)S(1)}, s32[128]{0:T(128)S(1)}) fusion(s32[]{:T(128)} %bitcast.34, s32[]{:T(128)} %bitcast.33, s32[]{:T(128)} %bitcast.32, s32[]{:T(128)} %bitcast.31, s32[]{:T(128)} %bitcast.30, s32[]{:T(128)} %bitcast.29, s32[]{:T(128)} %bitcast.28, s32[]{:T(128)} %bitcast.27, s32[]{:T(128)} %bitcast.26, s32[]{:T(128)} %bitcast.25, ...), kind=kLoop, calls=%fused_computation.100 | loop fusion | flops 5376 | bytes 1216 | tf_op jit(solution)/shard_map/jit(_take)/and | solution.py:51
  39.3 10.6 %all-to-all-done.1 = bf16[16,16,1920]{2,1,0:T(8,128)(2,1)S(1)} async-done(((bf16[16,16,1920]{2,1,0:T(8,128)(2,1)}), bf16[16,16,1920]{2,1,0:T(8,128)(2,1)S(1)}, u32[]{:S(2)}, u32[]{:S(2)}) %all-to-all-start.1) | async-done | bytes 983072 | tf_op jit(solution)/shard_map/all_to_all | solution.py:44
  49.9 0.9 gather_fusion.3
  50.9 0.1 broadcast_select_fusion
  51.0 13.5 %all_gather.3 = bf16[256,1920]{1,0:T(8,128)(2,1)S(1)} all-gather(bf16[128,1920]{1,0:T(8,128)(2,1)S(1)} %broadcast_select_fusion), channel_id=1, replica_groups=mesh['dp'=2,'expert'=16] {'dp'}, dimensions={0}, use_global_device_ids=true | all-gather | bytes 1474560 | tf_op jit(solution)/shard_map/all_gather | solution.py:55
  64.5 0.2 convert_reduce_fusion
  64.7 0.4 fusion.15
  65.2 11.0 %fusion.10 = bf16[256,1920]{1,0:T(8,128)(2,1)} fusion(bf16[1,2048,1920]{2,1,0:T(8,128)(2,1)} %param.15, bf16[1,2048,1920]{2,1,0:T(8,128)(2,1)} %param.14, bf16[256,1920]{1,0:T(8,128)(2,1)S(1)} %all_gather.3, f32[1920]{0:T(1024)S(1)} %reduce.12, f32[256]{0:T(256)S(1)} %add_rsqrt_fusion, f32[256]{0:T(256)S(1)} %broadcast_multiply_fusion), kind=kOutput, calls=%fused_computation.12 | convolution fusion | flops 4030529536 | bytes 17704448 | tf_op jit(solution)/shard_map/dot_general | solution.py:21
  76.2 0.0 reduce-scatter.2.cloned.1.call-update
  76.5 4.4 %compare_select_fusion.10 = s32[256,1]{0,1:T(1,128)S(1)} fusion(s32[]{:T(128)} %bitcast.28, s32[]{:T(128)} %bitcast.29, s32[]{:T(128)} %bitcast.30, s32[]{:T(128)} %bitcast.31, s32[]{:T(128)} %bitcast.32, s32[]{:T(128)} %bitcast.34, s32[]{:T(128)} %bitcast.33), kind=kLoop, calls=%fused_computation.76 | loop fusion | flops 5888 | bytes 1052 | tf_op jit(solution)/shard_map/gather | solution.py:65
  80.9 0.7 fusion.44
  81.5 4.3 %compare_select_fusion.9 = s32[256,1]{0,1:T(1,128)S(1)} fusion(s32[]{:T(128)} %bitcast.10, s32[]{:T(128)} %bitcast.11, s32[]{:T(128)} %bitcast.12, s32[]{:T(128)} %bitcast.13, s32[]{:T(128)} %bitcast.14, s32[]{:T(128)} %bitcast.16, s32[]{:T(128)} %bitcast.15), kind=kLoop, calls=%fused_computation.75 | loop fusion | flops 5888 | bytes 1052 | tf_op jit(solution)/shard_map/gather | solution.py:64
  85.9 11.2 %compare_and_fusion = (pred[256]{0:T(512)(128)(4,1)S(1)}, s32[256]{0:T(256)S(1)}, s32[256]{0:T(256)S(1)}, pred[256]{0:T(512)(128)(4,1)S(1)}, s32[256]{0:T(256)S(1)}) fusion(pred[256]{0:T(512)(128)(4,1)S(1)} %compare_reduce_fusion, pred[256]{0:T(512)(128)(4,1)S(1)} %compare_reduce_fusion.1, pred[256]{0:T(512)(128)(4,1)S(1)} %compare_reduce_fusion.2, ...), kind=kLoop, calls=%fused_computation.99 | loop fusion | flops 8448 | bytes 8008 | tf_op jit(solution)/shard_map/jit(_take)/and | solution.py:67
  97.1 0.1 gather.34
  97.2 0.1 gather.36
  97.3 0.0 copy-done
  97.3 0.2 fusion.22
  97.6 1.9 %gather_fusion = bf16[256]{0:T(256)(128)(2,1)S(1)} fusion(bf16[128]{0:T(256)(128)(2,1)S(1)} %fusion.22, s32[1024]{0:T(1024)S(1)} %pad_clamp_fusion.2), kind=kCustom, calls=%fused_computation.4 | custom fusion | bytes 2048 | tf_op jit(solution)/shard_map/jit(_take)/gather | solution.py:71
  99.5 0.1 gather.41
  99.6 0.6 copy.17
  100.2 7.0 %all-to-all-start.2 = ((bf16[16,16,1]{1,2,0:T(2,128)(2,1)}), bf16[16,16,1]{1,2,0:T(2,128)(2,1)S(1)}, u32[]{:S(2)}, u32[]{:S(2)}) async-start(bf16[16,16,1]{1,2,0:T(2,128)(2,1)} %copy.17), calls=%async_computation.2 | async-start | bytes 16384 | tf_op jit(solution)/shard_map/all_to_all | solution.py:74
  107.2 0.0 reduce-scatter.2.cloned.1.call-done
  107.2 3.4 %gather_fusion.4 = bf16[256,1920]{1,0:T(8,128)(2,1)S(1)} fusion(bf16[128,1920]{1,0:T(8,128)(2,1)} %reduce-scatter.2.cloned.1.call-done, s32[1024]{0:T(1024)S(1)} %pad_clamp_fusion), kind=kCustom, calls=%fused_computation.2.clone | custom fusion | bytes 1967104 | tf_op jit(solution)/shard_map/jit(_take)/gather | solution.py:67
  110.7 1.2 select_select_fusion
  111.9 1.0 all-to-all-done.2
  112.9 5.0 %all-to-all-start.3 = ((bf16[16,16,1920]{2,1,0:T(8,128)(2,1)}), bf16[16,16,1920]{2,1,0:T(8,128)(2,1)S(1)}, u32[]{:S(2)}, u32[]{:S(2)}) async-start(bf16[16,16,1920]{2,1,0:T(8,128)(2,1)} %bitcast.55), calls=%async_computation.4 | async-start | bytes 1966080 | tf_op jit(solution)/shard_map/all_to_all | solution.py:73
  117.9 0.1 all_to_all.37
  118.0 1.2 gather_fusion.1
  119.3 20.6 %all-to-all-done.3 = bf16[16,16,1920]{2,1,0:T(8,128)(2,1)S(1)} async-done(((bf16[16,16,1920]{2,1,0:T(8,128)(2,1)}), bf16[16,16,1920]{2,1,0:T(8,128)(2,1)S(1)}, u32[]{:S(2)}, u32[]{:S(2)}) %all-to-all-start.3) | async-done | bytes 983072 | tf_op jit(solution)/shard_map/all_to_all | solution.py:73
  139.9 0.0 copy-start.1
  139.9 0.9 gather_fusion.5
  140.8 0.1 copy-done.1
  140.9 1.1 add_convert_fusion
  (25 shorter events, 0.5 us)
Async XLA Ops:
  6.5 90.8 %copy-start = (bf16[1,1920]{1,0:T(2,128)(2,1)S(1)}, bf16[1,1920]{1,0:T(2,128)(2,1)}, u32[]{:S(2)}) copy-start(bf16[1,1920]{1,0:T(2,128)(2,1)} %param.12) | copy-start | bytes 11524
  9.0 13.0 %all-to-all-start = ((s32[16,1,1]{2,1,0:T(1,128)}), s32[16,1,1]{2,1,0:T(1,128)S(1)}, u32[]{:S(2)}, u32[]{:S(2)}) async-start(s32[16,1,1]{2,1,0:T(1,128)} %copy.15), calls=%async_computation | async-start | bytes 16384 | tf_op jit(solution)/shard_map/all_to_all | solution.py:45
  20.7 7.3 %copy-start.2 = (f32[1,1920]{1,0:T(1,128)S(1)}, f32[1,1920]{1,0:T(1,128)}, u32[]{:S(2)}) copy-start(f32[1,1920]{1,0:T(1,128)} %param.13) | copy-start | bytes 23044
  22.0 27.9 %all-to-all-start.1 = ((bf16[16,16,1920]{2,1,0:T(8,128)(2,1)}), bf16[16,16,1920]{2,1,0:T(8,128)(2,1)S(1)}, u32[]{:S(2)}, u32[]{:S(2)}) async-start(bf16[16,16,1920]{2,1,0:T(8,128)(2,1)} %bitcast.47), calls=%async_computation.1 | async-start | bytes 1966080 | tf_op jit(solution)/shard_map/all_to_all | solution.py:44
  27.9 79.3 %reduce-scatter.2.cloned.1.call-start = ((), (), s32[]{:S(2)}) async-start(), calls=%async_computation.5 | async-start | bytes 1474560 | tf_op jit(solution)/shard_map/reduce_scatter | solution.py:59
  100.2 12.7 %all-to-all-start.2 = ((bf16[16,16,1]{1,2,0:T(2,128)(2,1)}), bf16[16,16,1]{1,2,0:T(2,128)(2,1)S(1)}, u32[]{:S(2)}, u32[]{:S(2)}) async-start(bf16[16,16,1]{1,2,0:T(2,128)(2,1)} %copy.17), calls=%async_computation.2 | async-start | bytes 16384 | tf_op jit(solution)/shard_map/all_to_all | solution.py:74
  112.9 27.0 %all-to-all-start.3 = ((bf16[16,16,1920]{2,1,0:T(8,128)(2,1)}), bf16[16,16,1920]{2,1,0:T(8,128)(2,1)S(1)}, u32[]{:S(2)}, u32[]{:S(2)}) async-start(bf16[16,16,1920]{2,1,0:T(8,128)(2,1)} %bitcast.55), calls=%async_computation.4 | async-start | bytes 1966080 | tf_op jit(solution)/shard_map/all_to_all | solution.py:73
  139.9 1.0 copy-start.1
Sparse Core Ops, SparseCore 0:
  76.3 21.3 reduce-scatter.1
where the time goes:
time: 151 us; the launch traced here: 149 us
  other arithmetic  37.8 us (25%)
  waiting for transfers between devices  32.4 us (21%)
  starting transfers between devices  25.2 us (17%)
  local copies, waits for them, and re-layouts  15 us (10%)
  between operations  13.6 us (9%)
  blocking collectives  13.5 us (9%)
  matrix products  11.2 us (7%)
    all_to_all x1, waiting for transfers between devices, body(): lax.all_to_all(returning, 'expert', split_axis=0, concat_axis=0, tiled=True)  20.6 us
    all_gather x1, blocking collectives, body(): lax.all_gather(local_rows, 'dp', axis=0, tiled=True)  13.5 us
    and x1, other arithmetic, body(): jnp.take(expert_out, compact, axis=0)  11.2 us
    dot_general x1, matrix products, expert_rows(): return jnp.dot(hidden, outer_mat, preferred_element_type=jnp.float32)  11 us
    all_to_all x1, waiting for transfers between devices, body(): lax.all_to_all(outgoing, 'expert', split_axis=0, concat_axis=0, tiled=True)  10.6 us
    and x1, other arithmetic, body(): local_rows = jnp.take(arrived, sender * capacity + within, axis=0)  9.89 us
    all_to_all x1, starting transfers between devices, body(): lax.all_to_all(send_counts, 'expert', split_axis=0, concat_axis=0, tiled=...  7.32 us
    all_to_all x1, starting transfers between devices, body(): lax.all_to_all(gate_slots, 'expert', split_axis=0, concat_axis=0, tiled=T...  6.98 us
  transfers between devices with their start and end apart: 5, of which 4 were waited for; matrix products, arithmetic and copies ran while one was open for 31% of the time, Pallas kernels for 0%

commit v1 on v0

v1 whole, which is shorter than its diff:
```python
import functools

import jax
import jax.numpy as jnp
from jax import lax
from jax.experimental import pallas as pl
from jax.experimental.pallas import tpu as pltpu
from jax.sharding import PartitionSpec as P

EPSILON = 1e-05
EMPTY = 64.0
VMEM_LIMIT = 48 * 1024 * 1024


def whole(shape):
    return pl.BlockSpec(shape, lambda *_: (0,) * len(shape))


def call(kernel, outs, flops, nbytes, *args):
    return pl.pallas_call(
        kernel,
        out_shape=outs,
        compiler_params=pltpu.CompilerParams(vmem_limit_bytes=VMEM_LIMIT),
        cost_estimate=pl.CostEstimate(flops=flops, bytes_accessed=nbytes, transcendentals=0),
    )(*args)


def earlier(count):
    i = lax.broadcasted_iota(jnp.int32, (count, count), 0)
    j = lax.broadcasted_iota(jnp.int32, (count, count), 1)
    return (i < j).astype(jnp.bfloat16)


def pack_kernel(experts, capacity, assign_ref, tokens_ref, slots_ref, place_ref):
    tok_count = tokens_ref.shape[0]
    slot_total = slots_ref.shape[0]
    assign = assign_ref[...]
    ids = lax.broadcasted_iota(jnp.int32, (experts, tok_count), 0)
    onehot = (assign == ids).astype(jnp.float32)
    before = jnp.dot(
        onehot.astype(jnp.bfloat16), earlier(tok_count), preferred_element_type=jnp.float32
    )
    position = jnp.sum(before * onehot, axis=0, keepdims=True).astype(jnp.int32)
    slot_of = assign * capacity + position
    rows = lax.broadcasted_iota(jnp.int32, (slot_total, tok_count), 0)
    place = (rows == slot_of).astype(jnp.float32)
    taken = jnp.sum(place, axis=1, keepdims=True)
    place = place.astype(jnp.bfloat16)
    place_ref[...] = place
    packed = jnp.dot(place, tokens_ref[...], preferred_element_type=jnp.float32)
    slots_ref[...] = jnp.where(taken > 0.5, packed, EMPTY).astype(jnp.bfloat16)


def compact_kernel(slots_ref, gain_ref, centroid_ref, normed_ref, gate_ref, select_ref):
    slot_total = slots_ref.shape[0]
    rows = normed_ref.shape[0]
    first = (lax.broadcasted_iota(jnp.int32, (8, 128), 1) == 0).astype(jnp.bfloat16)
    mark = lax.dot_general(
        first, slots_ref[:, :128], (((1,), (1,)), ((), ())), preferred_element_type=jnp.float32
    )
    live = mark < 0.5 * EMPTY
    rank = jnp.dot(
        live.astype(jnp.bfloat16), earlier(slot_total), preferred_element_type=jnp.float32
    )
    rank = jnp.where(live, rank, -1.0)[:1].astype(jnp.int32)
    select = (lax.broadcasted_iota(jnp.int32, (rows, slot_total), 0) == rank).astype(jnp.bfloat16)
    select_ref[...] = select
    values = jnp.dot(select, slots_ref[...], preferred_element_type=jnp.float32)
    center = jnp.mean(values, axis=1, keepdims=True)
    shifted = values - center
    spread = jnp.mean(jnp.square(shifted), axis=1, keepdims=True)
    normed_ref[...] = (shifted * lax.rsqrt(spread + EPSILON) * gain_ref[...]).astype(jnp.bfloat16)
    score = jnp.sum(values * centroid_ref[...].astype(jnp.float32), axis=1, keepdims=True)
    gate = (1.0 / (1.0 + jnp.exp(-score))).astype(jnp.bfloat16).astype(jnp.float32)
    gate_ref[...] = jnp.broadcast_to(gate, gate_ref.shape)


def ffn_kernel(rows_ref, inner_ref, outer_ref, out_ref, total_ref):
    step = pl.program_id(0)

    @pl.when(step == 0)
    def _():
        total_ref[...] = jnp.zeros_like(total_ref)

    act = lax.dot_general(
        rows_ref[...], inner_ref[...], (((1,), (1,)), ((), ())), preferred_element_type=jnp.float32
    )
    hidden = jnp.maximum(act, 0.0).astype(jnp.bfloat16)
    total_ref[...] += jnp.dot(hidden, outer_ref[...], preferred_element_type=jnp.float32)

    @pl.when(step == pl.num_programs(0) - 1)
    def _():
        out_ref[...] = total_ref[...].astype(out_ref.dtype)


def ffn(rows, inner, outer):
    count, features = rows.shape
    units = inner.shape[0]
    tile = min(units, 256)
    return pl.pallas_call(
        ffn_kernel,
        out_shape=jax.ShapeDtypeStruct((count, features), jnp.bfloat16),
        grid=(units // tile,),
        in_specs=[
            whole((count, features)),
            pl.BlockSpec((tile, features), lambda i: (i, 0)),
            pl.BlockSpec((tile, features), lambda i: (i, 0)),
        ],
        out_specs=whole((count, features)),
        scratch_shapes=[pltpu.VMEM((count, features), jnp.float32)],
        compiler_params=pltpu.CompilerParams(vmem_limit_bytes=VMEM_LIMIT),
        cost_estimate=pl.CostEstimate(
            flops=4 * count * features * units,
            bytes_accessed=4 * units * features,
            transcendentals=0,
        ),
    )(rows, inner, outer)


def spread_kernel(parts, *refs):
    part_refs, gate_ref, select_ref, slots_ref = refs[:parts], refs[parts], refs[parts + 1], refs[parts + 2]
    total = part_refs[0][...].astype(jnp.float32)
    for ref in part_refs[1:]:
        total = total + ref[...].astype(jnp.float32)
    gated = (gate_ref[:, :1] * total).astype(jnp.bfloat16)
    slots_ref[...] = lax.dot_general(
        select_ref[...], gated, (((0,), (0,)), ((), ())), preferred_element_type=jnp.float32
    ).astype(jnp.bfloat16)


def final_kernel(tokens_ref, slots_ref, place_ref, out_ref):
    added = lax.dot_general(
        place_ref[...], slots_ref[...], (((0,), (0,)), ((), ())), preferred_element_type=jnp.float32
    )
    out_ref[...] = (tokens_ref[...].astype(jnp.float32) + added).astype(jnp.bfloat16)


def body(tokens, assignment, centroids, norm_gain, inner_weight, outer_weight):
    tok_count, features = tokens.shape
    experts = lax.axis_size("expert")
    groups = lax.axis_size("dp")
    capacity = 2 * tok_count // experts
    slot_total = experts * capacity
    shape = jax.ShapeDtypeStruct
    bf16 = jnp.bfloat16
    slot_bytes = 2 * slot_total * features
    move_flops = 2 * slot_total * tok_count * features
    outgoing, place = call(
        functools.partial(pack_kernel, experts, capacity),
        (shape((slot_total, features), bf16), shape((slot_total, tok_count), bf16)),
        move_flops,
        2 * slot_bytes,
        assignment.reshape(1, tok_count),
        tokens,
    )
    arrived = lax.all_to_all(outgoing, "expert", split_axis=0, concat_axis=0, tiled=True)
    normed, gate, select = call(
        compact_kernel,
        (
            shape((tok_count, features), bf16),
            shape((tok_count, 128), jnp.float32),
            shape((tok_count, slot_total), bf16),
        ),
        move_flops,
        2 * slot_bytes,
        arrived,
        norm_gain,
        centroids,
    )
    inner = inner_weight[0]
    outer = outer_weight[0]
    guests = []
    for k in range(1, groups):
        there = [(i, (i + k) % groups) for i in range(groups)]
        guests.append(lax.ppermute(normed, "dp", there))
    parts = [ffn(normed, inner, outer)]
    for k in range(1, groups):
        back = [((i + k) % groups, i) for i in range(groups)]
        parts.append(lax.ppermute(ffn(guests[k - 1], inner, outer), "dp", back))
    returning = call(
        functools.partial(spread_kernel, groups),
        shape((slot_total, features), bf16),
        move_flops,
        2 * slot_bytes,
        *parts,
        gate,
        select,
    )
    back_rows = lax.all_to_all(returning, "expert", split_axis=0, concat_axis=0, tiled=True)
    return call(
        final_kernel,
        shape((tok_count, features), bf16),
        move_flops,
        2 * slot_bytes,
        tokens,
        back_rows,
        place,
    )


def solution(mesh):
    in_specs = (
        P(("dp", "expert"), None),
        P(("dp", "expert")),
        P("expert", None),
        P("expert", None),
        P("expert", "dp", None),
        P("expert", "dp", None),
    )
    out_specs = P(("dp", "expert"), None)
    return jax.shard_map(body, mesh=mesh, in_specs=in_specs, out_specs=out_specs, check_vma=False)
```

time: 151 us -> 103 us (0.68); the launches traced: 149 us -> 103 us
  blocking collectives: 13.5 us -> 60.2 us
  other arithmetic: 37.8 us -> 0 us
  Pallas kernels: 0 us -> 24.8 us
  starting transfers between devices: 25.2 us -> 2.61 us
  waiting for transfers between devices: 32.4 us -> 11.8 us
  between operations: 13.6 us -> 0.05 us
  local copies, waits for them, and re-layouts: 15 us -> 3.08 us
  matrix products: 11.2 us -> 0 us
    all_to_all x0 -> x2, blocking collectives: none -> 60.2 us  [the longest x1 31.2 us: body(): lax.all_to_all(outgoing, 'expert', split_axis=0, concat_axis=0, tiled=True)]
    all_to_all x4 -> x0, waiting for transfers between devices: 32.4 us -> none  [the longest x1 20.6 us: body(): lax.all_to_all(returning, 'expert', split_axis=0, concat_axis=0, tiled=True)]
    all_to_all x4 -> x0, starting transfers between devices: 25.2 us -> none  [the longest x1 7.32 us: body(): lax.all_to_all(send_counts, 'expert', split_axis=0, concat_axis=0, tiled=...]
    pallas_call x0 -> x6, Pallas kernels: none -> 24.8 us  [the longest x2 21.8 us: ffn(): pl.pallas_call(ffn_kernel, out_shape=jax.ShapeDtypeStruct((count, feature...]
    and x3 -> x0, other arithmetic: 21.1 us -> none  [the longest x1 11.2 us: body(): jnp.take(expert_out, compact, axis=0)]
    all_gather x1 -> x0, blocking collectives: 13.5 us -> none  [body(): lax.all_gather(local_rows, 'dp', axis=0, tiled=True)]
    gather x11 -> x0, local copies, waits for them, and re-layouts: 13.5 us -> none  [the longest x1 3.44 us: body(): jnp.take(tokens, source_row, axis=0)]
    ppermute x0 -> x2, waiting for transfers between devices: none -> 11.8 us  [the longest x1 11.8 us: body(): guests.append(lax.ppermute(normed, 'dp', there))]
  transfers between devices with their start and end apart: 5 -> 2, of which waited for: 4 -> 1; matrix products, arithmetic and copies ran while one was open for 31% -> 0% of each run, Pallas kernels for 0% -> 11%
where the time goes in v1:
time: 103 us
  blocking collectives  60.2 us (58%)
  Pallas kernels  24.8 us (24%)
  waiting for transfers between devices  11.8 us (11%)
  local copies, waits for them, and re-layouts  3.08 us (3%)
  starting transfers between devices  2.61 us (3%)
    all_to_all x1, blocking collectives, body(): lax.all_to_all(outgoing, 'expert', split_axis=0, concat_axis=0, tiled=True)  31.2 us
    all_to_all x1, blocking collectives, body(): lax.all_to_all(returning, 'expert', split_axis=0, concat_axis=0, tiled=True)  29.1 us
    pallas_call x2, Pallas kernels, ffn(): pl.pallas_call(ffn_kernel, out_shape=jax.ShapeDtypeStruct((count, feature...  21.8 us
    ppermute x1, waiting for transfers between devices, body(): guests.append(lax.ppermute(normed, 'dp', there))  11.8 us
    unnamed x10, local copies, waits for them, and re-layouts  3.08 us
    pallas_call x4, Pallas kernels, call(): pl.pallas_call(kernel, out_shape=outs, compiler_params=pltpu.CompilerPara...  2.98 us
  transfers between devices with their start and end apart: 2, of which 1 were waited for; matrix products, arithmetic and copies ran while one was open for 0% of the time, Pallas kernels for 11%

profile of v1, /device:TPU:1, one launch (start us, length us, event | category | flops | bytes accessed | tf_op | source)
XLA Modules:
  0.0 102.6 jit_solution(17882407287149050716)
XLA Ops:
  0.0 0.0 copy-start
  0.0 1.0 %copy-done = bf16[128,1920]{1,0:T(8,128)(2,1)S(1)} copy-done((bf16[128,1920]{1,0:T(8,128)(2,1)S(1)}, bf16[128,1920]{1,0:T(8,128)(2,1)}, u32[]{:S(2)}) %copy-start) | copy-done | bytes 491544
  1.0 0.0 copy-start.4
  1.0 0.7 copy-done.4
  1.7 0.6 shard_map.64
  2.2 31.2 %all_to_all.22 = bf16[16,16,1920]{2,1,0:T(8,128)(2,1)S(1)} all-to-all(bf16[16,16,1920]{2,1,0:T(8,128)(2,1)S(1)} %bitcast.10), channel_id=1, replica_groups=mesh['dp'=2,'expert'=16] {'expert'}, dimensions={0} | all-to-all | bytes 1966080 | tf_op jit(solution)/shard_map/all_to_all | solution.py:156
  33.4 0.0 copy-start.2
  33.4 0.7 copy-done.2
  34.1 0.0 copy-start.3
  34.1 0.7 copy-done.3
  34.8 0.8 shard_map.65
  35.7 1.3 %collective-permute-start = (bf16[128,1920]{1,0:T(8,128)(2,1)S(1)}, bf16[128,1920]{1,0:T(8,128)(2,1)S(1)}, u32[]{:S(2)}, u32[]{:S(2)}) collective-permute-start(bf16[128,1920]{1,0:T(8,128)(2,1)S(1)} %get-tuple-element.11.rows_ref), channel_id=1, source_target_pairs={{0,16},{16,0},{1,17},{17,1},{2,18},{18,2},{3,19},{19,3},{4,20},{20... | collective-permute-start | bytes 1474568 | tf_op jit(solution)/shard_map/ppermute | solution.py:175
  37.0 11.8 %collective-permute-done.rows_ref = bf16[128,1920]{1,0:T(8,128)(2,1)S(1)} collective-permute-done((bf16[128,1920]{1,0:T(8,128)(2,1)S(1)}, bf16[128,1920]{1,0:T(8,128)(2,1)S(1)}, u32[]{:S(2)}, u32[]{:S(2)}) %collective-permute-start) | collective-permute-done | bytes 491552 | tf_op jit(solution)/shard_map/ppermute | solution.py:175
  48.8 10.9 %shard_map.67 = bf16[128,1920]{1,0:T(8,128)(2,1)S(1)} custom-call(bf16[128,1920]{1,0:T(8,128)(2,1)S(1)} %collective-permute-done.rows_ref, bf16[2048,1920]{1,0:T(8,128)(2,1)} %bitcast.12, bf16[2048,1920]{1,0:T(8,128)(2,1)} %bitcast.14), custom_call_target="tpu_custom_call" | custom-call | flops 2013265920 | bytes 15728640 | tf_op jit(solution)/shard_map/pallas_call | solution.py:100
  59.7 0.0 copy-start.1
  59.7 1.3 %collective-permute-start.1 = (bf16[128,1920]{1,0:T(8,128)(2,1)S(1)}, bf16[128,1920]{1,0:T(8,128)(2,1)S(1)}, u32[]{:S(2)}, u32[]{:S(2)}) collective-permute-start(bf16[128,1920]{1,0:T(8,128)(2,1)S(1)} %shard_map.67), channel_id=1, source_target_pairs={{16,0},{0,16},{17,1},{1,17},{18,2},{2,18},{19,3},{3,19},{20,4},{4,... | collective-permute-start | bytes 1474568 | tf_op jit(solution)/shard_map/ppermute | solution.py:179
  61.0 10.9 %shard_map.66.refs_0_ = bf16[128,1920]{1,0:T(8,128)(2,1)S(1)} custom-call(bf16[128,1920]{1,0:T(8,128)(2,1)S(1)} %get-tuple-element.11.rows_ref, bf16[2048,1920]{1,0:T(8,128)(2,1)} %bitcast.13, bf16[2048,1920]{1,0:T(8,128)(2,1)} %bitcast.15), custom_call_target="tpu_custom_call" | custom-call | flops 2013265920 | bytes 15728640 | tf_op jit(solution)/shard_map/pallas_call | solution.py:100
  71.9 0.0 collective-permute-done.1.refs_1_
  71.9 0.5 shard_map.68
  72.4 29.1 %all_to_all.23 = bf16[16,16,1920]{2,1,0:T(8,128)(2,1)S(1)} all-to-all(bf16[16,16,1920]{2,1,0:T(8,128)(2,1)S(1)} %bitcast.8), channel_id=1, replica_groups=mesh['dp'=2,'expert'=16] {'expert'}, dimensions={0} | all-to-all | bytes 1966080 | tf_op jit(solution)/shard_map/all_to_all | solution.py:189
  101.5 0.0 copy-done.1
  101.5 1.1 %shard_map.69 = bf16[128,1920]{1,0:T(8,128)(2,1)} custom-call(bf16[128,1920]{1,0:T(8,128)(2,1)S(1)} %copy-done.1, bf16[256,1920]{1,0:T(8,128)(2,1)S(1)} %bitcast.9, bf16[256,128]{1,0:T(8,128)(2,1)S(1)} %get-tuple-element.14.place_ref), custom_call_target="tpu_custom_call" | custom-call | flops 125829120 | bytes 1966080 | tf_op jit(solution)/shard_map/pallas_call | solution.py:20
Async XLA Ops:
  0.0 1.0 %copy-start = (bf16[128,1920]{1,0:T(8,128)(2,1)S(1)}, bf16[128,1920]{1,0:T(8,128)(2,1)}, u32[]{:S(2)}) copy-start(bf16[128,1920]{1,0:T(8,128)(2,1)} %tokens_ref.3) | copy-start | bytes 1474564
  1.0 0.7 copy-start.4
  33.4 0.7 copy-start.2
  34.1 0.7 copy-start.3
  35.7 13.1 %collective-permute-start = (bf16[128,1920]{1,0:T(8,128)(2,1)S(1)}, bf16[128,1920]{1,0:T(8,128)(2,1)S(1)}, u32[]{:S(2)}, u32[]{:S(2)}) collective-permute-start(bf16[128,1920]{1,0:T(8,128)(2,1)S(1)} %get-tuple-element.11.rows_ref), channel_id=1, source_target_pairs={{0,16},{16,0},{1,17},{17,1},{2,18},{18,2},{3,19},{19,3},{4,20},{20... | collective-permute-start | bytes 1474568 | tf_op jit(solution)/shard_map/ppermute | solution.py:175
  59.7 41.8 %copy-start.1 = (bf16[128,1920]{1,0:T(8,128)(2,1)S(1)}, bf16[128,1920]{1,0:T(8,128)(2,1)}, u32[]{:S(2)}) copy-start(bf16[128,1920]{1,0:T(8,128)(2,1)} %tokens_ref.3) | copy-start | bytes 1474564
  59.7 12.2 %collective-permute-start.1 = (bf16[128,1920]{1,0:T(8,128)(2,1)S(1)}, bf16[128,1920]{1,0:T(8,128)(2,1)S(1)}, u32[]{:S(2)}, u32[]{:S(2)}) collective-permute-start(bf16[128,1920]{1,0:T(8,128)(2,1)S(1)} %shard_map.67), channel_id=1, source_target_pairs={{16,0},{0,16},{17,1},{1,17},{18,2},{2,18},{19,3},{3,19},{20,4},{4,... | collective-permute-start | bytes 1474568 | tf_op jit(solution)/shard_map/ppermute | solution.py:179

commit v2 on v1

--- a/solution.py
+++ b/solution.py
@@ -9,7 +9,8 @@
 
 EPSILON = 1e-05
 EMPTY = 64.0
-VMEM_LIMIT = 48 * 1024 * 1024
+VMEM_LIMIT = 24 * 1024 * 1024
+CHUNKS = 2
 
 
 def whole(shape):
@@ -31,10 +32,40 @@
     return (i < j).astype(jnp.bfloat16)
 
 
-def pack_kernel(experts, capacity, assign_ref, tokens_ref, slots_ref, place_ref):
+def fetch(sources, targets, sems):
+    copies = [
+        pltpu.make_async_copy(source, target, sems.at[i])
+        for i, (source, target) in enumerate(zip(sources, targets))
+    ]
+    for copy in copies:
+        copy.start()
+    return copies
+
+
+def pack_kernel(
+    experts,
+    capacity,
+    assign_ref,
+    tokens_ref,
+    gain_ref,
+    centroid_ref,
+    slots_ref,
+    place_ref,
+    gain_out,
+    centroid_out,
+    assign_buf,
+    tokens_buf,
+    sems,
+):
     tok_count = tokens_ref.shape[0]
     slot_total = slots_ref.shape[0]
-    assign = assign_ref[...]
+    get_assign, *others = fetch(
+        (assign_ref, tokens_ref, gain_ref, centroid_ref),
+        (assign_buf, tokens_buf, gain_out, centroid_out),
+        sems,
+    )
+    get_assign.wait()
+    assign = assign_buf[...]
     ids = lax.broadcasted_iota(jnp.int32, (experts, tok_count), 0)
     onehot = (assign == ids).astype(jnp.float32)
     before = jnp.dot(
@@ -47,13 +78,21 @@
     taken = jnp.sum(place, axis=1, keepdims=True)
     place = place.astype(jnp.bfloat16)
     place_ref[...] = place
-    packed = jnp.dot(place, tokens_ref[...], preferred_element_type=jnp.float32)
+    for copy in others:
+        copy.wait()
+    packed = jnp.dot(place, tokens_buf[...], preferred_element_type=jnp.float32)
     slots_ref[...] = jnp.where(taken > 0.5, packed, EMPTY).astype(jnp.bfloat16)
 
 
-def compact_kernel(slots_ref, gain_ref, centroid_ref, normed_ref, gate_ref, select_ref):
+def load_kernel(inner_ref, outer_ref, _, inner_out, outer_out, sems):
+    for copy in fetch((inner_ref, outer_ref), (inner_out, outer_out), sems):
+        copy.wait()
+
+
+def compact_kernel(slots_ref, gain_ref, centroid_ref, *refs):
+    chunk_refs, (normed_ref, gate_ref, select_ref) = refs[:-3], refs[-3:]
     slot_total = slots_ref.shape[0]
-    rows = normed_ref.shape[0]
+    rows = gate_ref.shape[0]
     first = (lax.broadcasted_iota(jnp.int32, (8, 128), 1) == 0).astype(jnp.bfloat16)
     mark = lax.dot_general(
         first, slots_ref[:, :128], (((1,), (1,)), ((), ())), preferred_element_type=jnp.float32
@@ -69,59 +108,64 @@
     center = jnp.mean(values, axis=1, keepdims=True)
     shifted = values - center
     spread = jnp.mean(jnp.square(shifted), axis=1, keepdims=True)
-    normed_ref[...] = (shifted * lax.rsqrt(spread + EPSILON) * gain_ref[...]).astype(jnp.bfloat16)
+    normed = (shifted * lax.rsqrt(spread + EPSILON) * gain_ref[...]).astype(jnp.bfloat16)
+    normed_ref[...] = normed
+    done = 0
+    for ref in chunk_refs:
+        ref[...] = normed[done : done + ref.shape[0]]
+        done += ref.shape[0]
     score = jnp.sum(values * centroid_ref[...].astype(jnp.float32), axis=1, keepdims=True)
     gate = (1.0 / (1.0 + jnp.exp(-score))).astype(jnp.bfloat16).astype(jnp.float32)
     gate_ref[...] = jnp.broadcast_to(gate, gate_ref.shape)
 
 
-def ffn_kernel(rows_ref, inner_ref, outer_ref, out_ref, total_ref):
-    step = pl.program_id(0)
-
-    @pl.when(step == 0)
-    def _():
-        total_ref[...] = jnp.zeros_like(total_ref)
-
-    act = lax.dot_general(
-        rows_ref[...], inner_ref[...], (((1,), (1,)), ((), ())), preferred_element_type=jnp.float32
-    )
-    hidden = jnp.maximum(act, 0.0).astype(jnp.bfloat16)
-    total_ref[...] += jnp.dot(hidden, outer_ref[...], preferred_element_type=jnp.float32)
-
-    @pl.when(step == pl.num_programs(0) - 1)
-    def _():
-        out_ref[...] = total_ref[...].astype(out_ref.dtype)
-
-
-def ffn(rows, inner, outer):
+def ffn_kernel(rows_ref, inner_ref, outer_ref, _, out_ref, total_ref):
+    units = inner_ref.shape[0]
+    tile = min(units, 1024)
+    for start in range(0, units, tile):
+        act = lax.dot_general(
+            rows_ref[...],
+            inner_ref[start : start + tile],
+            (((1,), (1,)), ((), ())),
+            preferred_element_type=jnp.float32,
+        )
+        hidden = jnp.maximum(act, 0.0).astype(jnp.bfloat16)
+        more = jnp.dot(
+            hidden, outer_ref[start : start + tile], preferred_element_type=jnp.float32
+        )
+        if start == 0:
+            total_ref[...] = more
+        else:
+            total_ref[...] += more
+    out_ref[...] = total_ref[...].astype(out_ref.dtype)
+
+
+def ffn(rows, inner, outer, after):
     count, features = rows.shape
     units = inner.shape[0]
-    tile = min(units, 256)
     return pl.pallas_call(
         ffn_kernel,
         out_shape=jax.ShapeDtypeStruct((count, features), jnp.bfloat16),
-        grid=(units // tile,),
-        in_specs=[
-            whole((count, features)),
-            pl.BlockSpec((tile, features), lambda i: (i, 0)),
-            pl.BlockSpec((tile, features), lambda i: (i, 0)),
-        ],
-        out_specs=whole((count, features)),
+        in_specs=[pl.BlockSpec(memory_space=pltpu.VMEM)] * 3 + [pl.BlockSpec(memory_space=pl.ANY)],
+        out_specs=pl.BlockSpec(memory_space=pltpu.VMEM),
         scratch_shapes=[pltpu.VMEM((count, features), jnp.float32)],
         compiler_params=pltpu.CompilerParams(vmem_limit_bytes=VMEM_LIMIT),
         cost_estimate=pl.CostEstimate(
-            flops=4 * count * features * units,
-            bytes_accessed=4 * units * features,
+            flops=4 * max(count, 256) * features * units,
+            bytes_accessed=4 * count * features,
             transcendentals=0,
         ),
-    )(rows, inner, outer)
-
-
-def spread_kernel(parts, *refs):
-    part_refs, gate_ref, select_ref, slots_ref = refs[:parts], refs[parts], refs[parts + 1], refs[parts + 2]
-    total = part_refs[0][...].astype(jnp.float32)
-    for ref in part_refs[1:]:
-        total = total + ref[...].astype(jnp.float32)
+    )(rows, inner, outer, after)
+
+
+def spread_kernel(groups, *refs):
+    gate_ref, select_ref, slots_ref = refs[-3:]
+    chunks = (len(refs) - 4) // (groups - 1)
+    total = refs[0][...].astype(jnp.float32)
+    for g in range(1, groups):
+        first = 1 + (g - 1) * chunks
+        rows = [ref[...].astype(jnp.float32) for ref in refs[first : first + chunks]]
+        total = total + jnp.concatenate(rows, axis=0)
     gated = (gate_ref[:, :1] * total).astype(jnp.bfloat16)
     slots_ref[...] = lax.dot_general(
         select_ref[...], gated, (((0,), (0,)), ((), ())), preferred_element_type=jnp.float32
@@ -145,38 +189,70 @@
     bf16 = jnp.bfloat16
     slot_bytes = 2 * slot_total * features
     move_flops = 2 * slot_total * tok_count * features
-    outgoing, place = call(
+    local = pl.BlockSpec(memory_space=pltpu.VMEM)
+    far = pl.BlockSpec(memory_space=pltpu.HBM)
+    stay = lambda x: pltpu.with_memory_space_constraint(x, pltpu.HBM)
+    outgoing, place, gain, centroid = pl.pallas_call(
         functools.partial(pack_kernel, experts, capacity),
-        (shape((slot_total, features), bf16), shape((slot_total, tok_count), bf16)),
-        move_flops,
-        2 * slot_bytes,
-        assignment.reshape(1, tok_count),
-        tokens,
-    )
+        out_shape=(
+            shape((slot_total, features), bf16),
+            shape((slot_total, tok_count), bf16),
+            pltpu.VMEM((1, features), jnp.float32),
+            pltpu.VMEM((1, features), bf16),
+        ),
+        in_specs=[far] * 4,
+        out_specs=(local,) * 4,
+        scratch_shapes=[
+            pltpu.VMEM((1, tok_count), jnp.int32),
+            pltpu.VMEM((tok_count, features), bf16),
+            pltpu.SemaphoreType.DMA((4,)),
+        ],
+        compiler_params=pltpu.CompilerParams(vmem_limit_bytes=VMEM_LIMIT),
+        cost_estimate=pl.CostEstimate(
+            flops=move_flops, bytes_accessed=2 * slot_bytes, transcendentals=0
+        ),
+    )(stay(assignment.reshape(1, tok_count)), stay(tokens), stay(norm_gain), stay(centroids))
     arrived = lax.all_to_all(outgoing, "expert", split_axis=0, concat_axis=0, tiled=True)
-    normed, gate, select = call(
+    half = tok_count // CHUNKS
+    *chunks, normed, gate, select = pl.pallas_call(
         compact_kernel,
-        (
+        out_shape=(shape((half, features), bf16),) * CHUNKS
+        + (
             shape((tok_count, features), bf16),
             shape((tok_count, 128), jnp.float32),
             shape((tok_count, slot_total), bf16),
         ),
-        move_flops,
-        2 * slot_bytes,
-        arrived,
-        norm_gain,
-        centroids,
-    )
-    inner = inner_weight[0]
-    outer = outer_weight[0]
+        in_specs=[local] * 3,
+        out_specs=(local,) * (CHUNKS + 3),
+        compiler_params=pltpu.CompilerParams(vmem_limit_bytes=VMEM_LIMIT),
+        cost_estimate=pl.CostEstimate(
+            flops=move_flops, bytes_accessed=2 * slot_bytes, transcendentals=0
+        ),
+    )(arrived, gain, centroid)
+    weights = (inner_weight[0], outer_weight[0])
+    inner, outer = pl.pallas_call(
+        load_kernel,
+        out_shape=tuple(pltpu.VMEM(w.shape, bf16) for w in weights),
+        in_specs=[far, far, pl.BlockSpec(memory_space=pl.ANY)],
+        out_specs=(local, local),
+        scratch_shapes=[pltpu.SemaphoreType.DMA((2,))],
+        compiler_params=pltpu.CompilerParams(vmem_limit_bytes=VMEM_LIMIT),
+        cost_estimate=pl.CostEstimate(
+            flops=0, bytes_accessed=4 * weights[0].size, transcendentals=0
+        ),
+    )(*map(stay, weights), gate)
     guests = []
     for k in range(1, groups):
         there = [(i, (i + k) % groups) for i in range(groups)]
-        guests.append(lax.ppermute(normed, "dp", there))
-    parts = [ffn(normed, inner, outer)]
+        guests.append([lax.ppermute(rows, "dp", there) for rows in chunks])
+    visits = []
     for k in range(1, groups):
         back = [((i + k) % groups, i) for i in range(groups)]
-        parts.append(lax.ppermute(ffn(guests[k - 1], inner, outer), "dp", back))
+        sums = [ffn(rows, inner, outer, gate) for rows in guests[k - 1]]
+        visits.append([lax.ppermute(rows, "dp", back) for rows in sums])
+    parts = [ffn(normed, inner, outer, sums[-1])]
+    for visit in visits:
+        parts += visit
     returning = call(
         functools.partial(spread_kernel, groups),
         shape((slot_total, features), bf16),

time: 103 us -> 88.1 us (0.86)
  waiting for transfers between devices: 11.8 us -> 2.98 us
  Pallas kernels: 24.8 us -> 20.4 us
  local copies, waits for them, and re-layouts: 3.08 us -> 0.01 us
  starting transfers between devices: 2.61 us -> 4.13 us
    pallas_call x2 -> x3, Pallas kernels: 21.8 us -> 10.9 us  [ffn(): pl.pallas_call(ffn_kernel, out_shape=jax.ShapeDtypeStruct((count, feature...]
    ppermute x2 -> x4, waiting for transfers between devices: 11.8 us -> 2.98 us  [the longest x2 1.76 us: body(): visits.append([lax.ppermute(rows, 'dp', back) for rows in sums])]
    pallas_call x0 -> x3, Pallas kernels: none -> 7.84 us  [the longest x1 5.49 us: body(): pl.pallas_call(load_kernel, out_shape=tuple((pltpu.VMEM(w.shape, bf16) fo...]
    unnamed x10 -> x2, local copies, waits for them, and re-layouts: 3.08 us -> 0.01 us
    ppermute x2 -> x4, starting transfers between devices: 2.61 us -> 4.13 us  [the longest x2 2.6 us: body(): visits.append([lax.ppermute(rows, 'dp', back) for rows in sums])]
    pallas_call x4 -> x2, Pallas kernels: 2.98 us -> 1.6 us  [call(): pl.pallas_call(kernel, out_shape=outs, compiler_params=pltpu.CompilerPara...]
  transfers between devices with their start and end apart: 2 -> 4, of which waited for: 1 -> 3; matrix products, arithmetic and copies ran while one was open for 0% -> 0% of each run, Pallas kernels for 11% -> 19%
where the time goes in v2:
time: 88.1 us; the launch traced here: 87.9 us
  blocking collectives  60.3 us (68%)
  Pallas kernels  20.4 us (23%)
  starting transfers between devices  4.13 us (5%)
  waiting for transfers between devices  2.98 us (3%)
    all_to_all x1, blocking collectives, body(): lax.all_to_all(outgoing, 'expert', split_axis=0, concat_axis=0, tiled=True)  31.2 us
    all_to_all x1, blocking collectives, body(): lax.all_to_all(returning, 'expert', split_axis=0, concat_axis=0, tiled=True)  29.2 us
    pallas_call x3, Pallas kernels, ffn(): pl.pallas_call(ffn_kernel, out_shape=jax.ShapeDtypeStruct((count, feature...  10.9 us
    pallas_call x1, Pallas kernels, body(): pl.pallas_call(load_kernel, out_shape=tuple((pltpu.VMEM(w.shape, bf16) fo...  5.49 us
    ppermute x2, starting transfers between devices, body(): visits.append([lax.ppermute(rows, 'dp', back) for rows in sums])  2.6 us
    ppermute x2, waiting for transfers between devices, body(): visits.append([lax.ppermute(rows, 'dp', back) for rows in sums])  1.76 us
  transfers between devices with their start and end apart: 4, of which 3 were waited for; matrix products, arithmetic and copies ran while one was open for 0% of the time, Pallas kernels for 19%

profile of v2, /device:TPU:1, one launch (start us, length us, event | category | flops | bytes accessed | tf_op | source)
XLA Modules:
  0.0 87.9 jit_solution(13106577398992109946)
XLA Ops:
  0.0 1.5 %shard_map.64 = (bf16[256,1920]{1,0:T(8,128)(2,1)S(1)}, bf16[256,128]{1,0:T(8,128)(2,1)S(1)}, f32[1,1920]{1,0:T(1,128)S(1)}, bf16[1,1920]{1,0:T(2,128)(2,1)S(1)}) custom-call(s32[1,128]{1,0:T(1,128)} %bitcast.13, bf16[128,1920]{1,0:T(8,128)(2,1)} %tokens_ref.3, f32[1,1920]{1,0:T(1,128)} %gain_ref.1, bf16[1,1920]{1,0:T(2,128)(2,1)} %centroid_ref.1), custom_call_target="tpu_custom_call" | custom-call | flops 125829120 | bytes 1966080 | tf_op jit(solution)/shard_map/pallas_call | solution.py:195
  1.5 31.2 %all_to_all.22 = bf16[16,16,1920]{2,1,0:T(8,128)(2,1)S(1)} all-to-all(bf16[16,16,1920]{2,1,0:T(8,128)(2,1)S(1)} %bitcast.10), channel_id=1, replica_groups=mesh['dp'=2,'expert'=16] {'expert'}, dimensions={0} | all-to-all | bytes 1966080 | tf_op jit(solution)/shard_map/all_to_all | solution.py:215
  32.7 0.8 shard_map.65
  33.5 1.3 %collective-permute-start.1 = (bf16[64,1920]{1,0:T(8,128)(2,1)S(1)}, bf16[64,1920]{1,0:T(8,128)(2,1)S(1)}, u32[]{:S(2)}, u32[]{:S(2)}) collective-permute-start(bf16[64,1920]{1,0:T(8,128)(2,1)S(1)} %get-tuple-element.24), channel_id=1, source_target_pairs={{0,16},{16,0},{1,17},{17,1},{2,18},{18,2},{3,19},{19,3},{4,20},{20... | collective-permute-start | bytes 737288 | tf_op jit(solution)/shard_map/ppermute | solution.py:247
  34.9 0.2 collective-permute-start
  35.1 5.5 %shard_map.66 = (bf16[2048,1920]{1,0:T(8,128)(2,1)S(1)}, bf16[2048,1920]{1,0:T(8,128)(2,1)S(1)}) custom-call(bf16[2048,1920]{1,0:T(8,128)(2,1)} %bitcast.11, bf16[2048,1920]{1,0:T(8,128)(2,1)} %bitcast.12, f32[128,128]{1,0:T(8,128)S(1)} %get-tuple-element.20._.refs_3_), custom_call_target="tpu_custom_call" | custom-call | bytes 15728640 | tf_op jit(solution)/shard_map/pallas_call | solution.py:233
  40.6 0.8 collective-permute-done.1.rows_ref
  41.4 3.6 %shard_map.69 = bf16[64,1920]{1,0:T(8,128)(2,1)S(1)} custom-call(bf16[64,1920]{1,0:T(8,128)(2,1)S(1)} %collective-permute-done.1.rows_ref, bf16[2048,1920]{1,0:T(8,128)(2,1)S(1)} %get-tuple-element.21.inner_ref, bf16[2048,1920]{1,0:T(8,128)(2,1)S(1)} %get-tuple-element.22.outer_ref, f32[128,128]{1,0:T(8,128)S(1)} %get-tuple-element.20._.refs_3_), custom_call_target="tpu_custom_call" | custom-call | flops 4026531840 | bytes 491520 | tf_op jit(solution)/shard_map/pallas_call | solution.py:146
  45.0 1.3 %collective-permute-start.2 = (bf16[64,1920]{1,0:T(8,128)(2,1)S(1)}, bf16[64,1920]{1,0:T(8,128)(2,1)S(1)}, u32[]{:S(2)}, u32[]{:S(2)}) collective-permute-start(bf16[64,1920]{1,0:T(8,128)(2,1)S(1)} %shard_map.69), channel_id=1, source_target_pairs={{16,0},{0,16},{17,1},{1,17},{18,2},{2,18},{19,3},{3,19},{20,4},{4,... | collective-permute-start | bytes 737288 | tf_op jit(solution)/shard_map/ppermute | solution.py:252
  46.2 0.4 collective-permute-done.rows_ref
  46.7 3.6 %shard_map.67._ = bf16[64,1920]{1,0:T(8,128)(2,1)S(1)} custom-call(bf16[64,1920]{1,0:T(8,128)(2,1)S(1)} %collective-permute-done.rows_ref, bf16[2048,1920]{1,0:T(8,128)(2,1)S(1)} %get-tuple-element.21.inner_ref, bf16[2048,1920]{1,0:T(8,128)(2,1)S(1)} %get-tuple-element.22.outer_ref, f32[128,128]{1,0:T(8,128)S(1)} %get-tuple-element.20._.refs_3_), custom_call_target="tpu_custom_call" | custom-call | flops 4026531840 | bytes 491520 | tf_op jit(solution)/shard_map/pallas_call | solution.py:146
  50.2 1.3 %collective-permute-start.3 = (bf16[64,1920]{1,0:T(8,128)(2,1)S(1)}, bf16[64,1920]{1,0:T(8,128)(2,1)S(1)}, u32[]{:S(2)}, u32[]{:S(2)}) collective-permute-start(bf16[64,1920]{1,0:T(8,128)(2,1)S(1)} %shard_map.67._), channel_id=1, source_target_pairs={{16,0},{0,16},{17,1},{1,17},{18,2},{2,18},{19,3},{3,19},{20,4},{4,... | collective-permute-start | bytes 737288 | tf_op jit(solution)/shard_map/ppermute | solution.py:252
  51.5 0.0 copy-start
  51.5 3.8 %shard_map.68.refs_0_ = bf16[128,1920]{1,0:T(8,128)(2,1)S(1)} custom-call(bf16[128,1920]{1,0:T(8,128)(2,1)S(1)} %get-tuple-element.19.rows_ref, bf16[2048,1920]{1,0:T(8,128)(2,1)S(1)} %get-tuple-element.21.inner_ref, bf16[2048,1920]{1,0:T(8,128)(2,1)S(1)} %get-tuple-element.22.outer_ref, bf16[64,1920]{1,0:T(8,128)(2,1)S(1)} %shard_map.67._), custom_call_target="tpu_custom_call" | custom-call | flops 4026531840 | bytes 983040 | tf_op jit(solution)/shard_map/pallas_call | solution.py:146
  55.3 0.0 collective-permute-done.2.refs_1_
  55.3 1.8 %collective-permute-done.3.refs_2_ = bf16[64,1920]{1,0:T(8,128)(2,1)S(1)} collective-permute-done((bf16[64,1920]{1,0:T(8,128)(2,1)S(1)}, bf16[64,1920]{1,0:T(8,128)(2,1)S(1)}, u32[]{:S(2)}, u32[]{:S(2)}) %collective-permute-start.3) | collective-permute-done | bytes 245792 | tf_op jit(solution)/shard_map/ppermute | solution.py:252
  57.1 0.5 shard_map.70
  57.6 29.2 %all_to_all.23 = bf16[16,16,1920]{2,1,0:T(8,128)(2,1)S(1)} all-to-all(bf16[16,16,1920]{2,1,0:T(8,128)(2,1)S(1)} %bitcast.8), channel_id=1, replica_groups=mesh['dp'=2,'expert'=16] {'expert'}, dimensions={0} | all-to-all | bytes 1966080 | tf_op jit(solution)/shard_map/all_to_all | solution.py:265
  86.8 0.0 copy-done
  86.8 1.1 %shard_map.71 = bf16[128,1920]{1,0:T(8,128)(2,1)} custom-call(bf16[128,1920]{1,0:T(8,128)(2,1)S(1)} %copy-done, bf16[256,1920]{1,0:T(8,128)(2,1)S(1)} %bitcast.9, bf16[256,128]{1,0:T(8,128)(2,1)S(1)} %get-tuple-element.26.place_ref), custom_call_target="tpu_custom_call" | custom-call | flops 125829120 | bytes 1966080 | tf_op jit(solution)/shard_map/pallas_call | solution.py:21
Async XLA Ops:
  33.5 7.8 %collective-permute-start.1 = (bf16[64,1920]{1,0:T(8,128)(2,1)S(1)}, bf16[64,1920]{1,0:T(8,128)(2,1)S(1)}, u32[]{:S(2)}, u32[]{:S(2)}) collective-permute-start(bf16[64,1920]{1,0:T(8,128)(2,1)S(1)} %get-tuple-element.24), channel_id=1, source_target_pairs={{0,16},{16,0},{1,17},{17,1},{2,18},{18,2},{3,19},{19,3},{4,20},{20... | collective-permute-start | bytes 737288 | tf_op jit(solution)/shard_map/ppermute | solution.py:247
  34.9 11.8 %collective-permute-start = (bf16[64,1920]{1,0:T(8,128)(2,1)S(1)}, bf16[64,1920]{1,0:T(8,128)(2,1)S(1)}, u32[]{:S(2)}, u32[]{:S(2)}) collective-permute-start(bf16[64,1920]{1,0:T(8,128)(2,1)S(1)} %get-tuple-element.23), channel_id=1, source_target_pairs={{0,16},{16,0},{1,17},{17,1},{2,18},{18,2},{3,19},{19,3},{4,20},{20... | collective-permute-start | bytes 737288 | tf_op jit(solution)/shard_map/ppermute | solution.py:247
  45.0 10.4 %collective-permute-start.2 = (bf16[64,1920]{1,0:T(8,128)(2,1)S(1)}, bf16[64,1920]{1,0:T(8,128)(2,1)S(1)}, u32[]{:S(2)}, u32[]{:S(2)}) collective-permute-start(bf16[64,1920]{1,0:T(8,128)(2,1)S(1)} %shard_map.69), channel_id=1, source_target_pairs={{16,0},{0,16},{17,1},{1,17},{18,2},{2,18},{19,3},{3,19},{20,4},{4,... | collective-permute-start | bytes 737288 | tf_op jit(solution)/shard_map/ppermute | solution.py:252
  50.2 6.9 %collective-permute-start.3 = (bf16[64,1920]{1,0:T(8,128)(2,1)S(1)}, bf16[64,1920]{1,0:T(8,128)(2,1)S(1)}, u32[]{:S(2)}, u32[]{:S(2)}) collective-permute-start(bf16[64,1920]{1,0:T(8,128)(2,1)S(1)} %shard_map.67._), channel_id=1, source_target_pairs={{16,0},{0,16},{17,1},{1,17},{18,2},{2,18},{19,3},{3,19},{20,4},{4,... | collective-permute-start | bytes 737288 | tf_op jit(solution)/shard_map/ppermute | solution.py:252
  51.5 35.2 %copy-start = (bf16[128,1920]{1,0:T(8,128)(2,1)S(1)}, bf16[128,1920]{1,0:T(8,128)(2,1)}, u32[]{:S(2)}) copy-start(bf16[128,1920]{1,0:T(8,128)(2,1)} %tokens_ref.3) | copy-start | bytes 1474564

commit v3 on v0

v3 whole, which is shorter than its diff:
```python
import functools

import jax
import jax.numpy as jnp
from jax import lax
from jax.experimental import pallas as pl
from jax.experimental.pallas import tpu as pltpu
from jax.sharding import PartitionSpec as P

EPSILON = 1e-05
EMPTY = 64.0
VMEM_LIMIT = 24 * 1024 * 1024
FIRST_SHARE = 9
LOCAL = pl.BlockSpec(memory_space=pltpu.VMEM)
FAR = pl.BlockSpec(memory_space=pltpu.HBM)
ANYWHERE = pl.BlockSpec(memory_space=pl.ANY)
BF16 = jnp.bfloat16
F32 = jnp.float32


def shape(*dims, dtype=BF16):
    return jax.ShapeDtypeStruct(dims, dtype)


def call(kernel, outs, args, flops, nbytes, in_specs=None, scratch=()):
    return pl.pallas_call(
        kernel,
        out_shape=tuple(outs),
        in_specs=[LOCAL] * len(args) if in_specs is None else in_specs,
        out_specs=(LOCAL,) * len(outs),
        scratch_shapes=list(scratch),
        compiler_params=pltpu.CompilerParams(vmem_limit_bytes=VMEM_LIMIT),
        cost_estimate=pl.CostEstimate(flops=flops, bytes_accessed=nbytes, transcendentals=0),
    )(*args)


def stay(array):
    return pltpu.with_memory_space_constraint(array, pltpu.HBM)


def fetch(sources, targets, sems):
    copies = [
        pltpu.make_async_copy(source, target, sems.at[i])
        for i, (source, target) in enumerate(zip(sources, targets))
    ]
    for copy in copies:
        copy.start()
    return copies


def earlier(count):
    i = lax.broadcasted_iota(jnp.int32, (count, count), 0)
    j = lax.broadcasted_iota(jnp.int32, (count, count), 1)
    return (i < j).astype(BF16)


def dot(a, b, dims=((1,), (0,))):
    return lax.dot_general(a, b, (dims, ((), ())), preferred_element_type=F32)


def put_slots(slots, refs, capacity):
    if len(refs) == 1:
        refs[0][...] = slots
        return
    for block in range(slots.shape[0] // capacity):
        row = block // 2 * capacity
        refs[block % 2][row : row + capacity] = slots[block * capacity : (block + 1) * capacity]


def get_blocks(refs):
    return jnp.concatenate([ref[...] for ref in refs], axis=0)


def pair_kernel(capacity, stay_ref, crossed_ref, _, *pair_refs):
    pairs = stay_ref.shape[0] // capacity
    for i in range(pairs):
        source = slice(i * capacity, (i + 1) * capacity)
        ref = pair_refs[i % len(pair_refs)]
        row = i // len(pair_refs) * 2 * capacity
        ref[row : row + capacity] = stay_ref[source]
        ref[row + capacity : row + 2 * capacity] = crossed_ref[source]


def pack_kernel(targets, experts, capacity, cut, *refs):
    assign_ref, tokens_ref, gain_ref, centroid_ref = refs[:4]
    halves = refs[4 : 4 + targets], refs[4 + targets : 4 + 2 * targets]
    place_ref, gain_out, centroid_out, assign_buf, tokens_buf, sems = refs[4 + 2 * targets :]
    tok_count = tokens_ref.shape[0]
    slot_total = place_ref.shape[0]
    get_assign, *others = fetch(
        (assign_ref, tokens_ref, gain_ref, centroid_ref),
        (assign_buf, tokens_buf, gain_out, centroid_out),
        sems,
    )
    get_assign.wait()
    assign = assign_buf[...]
    if targets == 2:
        assign = assign ^ lax.axis_index("expert")
    ids = lax.broadcasted_iota(jnp.int32, (experts, tok_count), 0)
    onehot = (assign == ids).astype(F32)
    before = dot(onehot.astype(BF16), earlier(tok_count))
    position = jnp.sum(before * onehot, axis=0, keepdims=True).astype(jnp.int32)
    rows = lax.broadcasted_iota(jnp.int32, (slot_total, tok_count), 0)
    place_ref[...] = (rows == assign_buf[...] * capacity + position).astype(F32).astype(BF16)
    place = (rows == assign * capacity + position).astype(F32)
    taken = jnp.sum(place, axis=1, keepdims=True)
    place = place.astype(BF16)
    for copy in others:
        copy.wait()
    packed = dot(place, tokens_buf[...])
    packed = jnp.where(taken > 0.5, packed, EMPTY).astype(BF16)
    put_slots(packed[:, :cut], halves[0], capacity)
    put_slots(packed[:, cut:], halves[1], capacity)


def load_kernel(inner_ref, outer_ref, _, inner_out, outer_out, sems):
    for copy in fetch((inner_ref, outer_ref), (inner_out, outer_out), sems):
        copy.wait()


def first_kernel(*refs):
    block_refs, (rows_ref, select_ref) = refs[:-2], refs[-2:]
    slots = get_blocks(block_refs)
    first = (lax.broadcasted_iota(jnp.int32, (8, 128), 1) == 0).astype(BF16)
    live = dot(first, slots[:, :128], ((1,), (1,))) < 0.5 * EMPTY
    rank = dot(live.astype(BF16), earlier(slots.shape[0]))
    rank = jnp.where(live, rank, -1.0)[:1].astype(jnp.int32)
    ids = lax.broadcasted_iota(jnp.int32, select_ref.shape, 0)
    select = (ids == rank).astype(BF16)
    select_ref[...] = select
    rows_ref[...] = dot(select, slots).astype(BF16)


def second_kernel(*refs):
    block_refs, (select_ref, rows_ref) = refs[:-2], refs[-2:]
    rows_ref[...] = dot(select_ref[...], get_blocks(block_refs)).astype(BF16)


def normalize(left, right, gain):
    count = left.shape[1] + right.shape[1]
    center = (
        jnp.sum(left, axis=1, keepdims=True) + jnp.sum(right, axis=1, keepdims=True)
    ) / count
    left, right = left - center, right - center
    spread = (
        jnp.sum(jnp.square(left), axis=1, keepdims=True)
        + jnp.sum(jnp.square(right), axis=1, keepdims=True)
    ) / count
    scale = lax.rsqrt(spread + EPSILON)
    cut = left.shape[1]
    left = (left * scale * gain[:, :cut]).astype(BF16)
    right = (right * scale * gain[:, cut:]).astype(BF16)
    return jnp.concatenate([left, right], axis=1)


def project(normed_ref, inner_ref, hidden_ref):
    units = inner_ref.shape[0]
    tile = min(units, 1024)
    for start in range(0, units, tile):
        act = dot(normed_ref[...], inner_ref[start : start + tile], ((1,), (1,)))
        hidden_ref[:, start : start + tile] = jnp.maximum(act, 0.0).astype(BF16)


def own_kernel(
    left_ref,
    right_ref,
    gain_ref,
    centroid_ref,
    inner_ref,
    outer_ref,
    left_out,
    right_out,
    gate_ref,
    normed_ref,
    hidden_ref,
):
    cut = left_ref.shape[1]
    left, right = left_ref[...].astype(F32), right_ref[...].astype(F32)
    centroid = centroid_ref[...].astype(F32)
    score = jnp.sum(left * centroid[:, :cut], axis=1, keepdims=True)
    score = score + jnp.sum(right * centroid[:, cut:], axis=1, keepdims=True)
    gate = (1.0 / (1.0 + jnp.exp(-score))).astype(BF16).astype(F32)
    gate_ref[...] = jnp.broadcast_to(gate, gate_ref.shape)
    normed_ref[...] = normalize(left, right, gain_ref[...])
    project(normed_ref, inner_ref, hidden_ref)
    cut = left_out.shape[1]
    left_out[...] = dot(hidden_ref[...], outer_ref[:, :cut]).astype(BF16)
    right_out[...] = dot(hidden_ref[...], outer_ref[:, cut:]).astype(BF16)


def guest_kernel(
    left_ref, right_ref, gain_ref, inner_ref, outer_ref, left_out, hidden_ref, normed_ref
):
    cut = left_out.shape[1]
    normed_ref[...] = normalize(
        left_ref[...].astype(F32), right_ref[...].astype(F32), gain_ref[...]
    )
    project(normed_ref, inner_ref, hidden_ref)
    left_out[...] = dot(hidden_ref[...], outer_ref[:, :cut]).astype(BF16)


def rest_kernel(hidden_ref, outer_ref, right_out):
    cut = outer_ref.shape[1] - right_out.shape[1]
    right_out[...] = dot(hidden_ref[...], outer_ref[:, cut:]).astype(BF16)


def spread_kernel(groups, capacity, relative, *refs):
    gate_ref, select_ref, slots_ref = refs[2 * groups :]
    sums = []
    for part_refs in (refs[:groups], refs[groups : 2 * groups]):
        total = part_refs[0][...].astype(F32)
        for ref in part_refs[1:]:
            total = total + ref[...].astype(F32)
        sums.append((gate_ref[:, :1] * total).astype(BF16))
    slots = dot(select_ref[...], jnp.concatenate(sums, axis=1), ((0,), (0,))).astype(BF16)
    if not relative:
        slots_ref[...] = slots
        return
    me = lax.axis_index("expert")
    for j in range(slots.shape[0] // capacity):
        row = pl.multiple_of((me ^ j) * capacity, capacity)
        slots_ref[pl.ds(row, capacity)] = slots[j * capacity : (j + 1) * capacity]


def final_kernel(tokens_ref, slots_ref, place_ref, out_ref):
    added = dot(place_ref[...], slots_ref[...], ((0,), (0,)))
    out_ref[...] = (tokens_ref[...].astype(F32) + added).astype(BF16)


def swap(array, axis_mask, experts):
    return lax.ppermute(array, "expert", [(i, i ^ axis_mask) for i in range(experts)])


def pair(stay, crossed, targets, capacity, after):
    rows, width = stay.shape
    return call(
        functools.partial(pair_kernel, capacity),
        [shape(2 * rows // targets, width) for _ in range(targets)],
        [stay, crossed, after],
        0,
        8 * rows * width,
        [LOCAL, LOCAL, ANYWHERE],
    )


def exchange(halves, experts, capacity, after=None):
    crossed = swap(halves[1], 1, experts)
    after = halves[0] if after is None else after
    blocks = list(pair(halves[0], crossed, experts // 2, capacity, after))
    for j in reversed(range(1, experts // 2)):
        blocks[j] = swap(blocks[j], 2 * j, experts)
    return blocks


def together(rows):
    return lax.all_to_all(rows, "expert", split_axis=0, concat_axis=0, tiled=True)


def body(tokens, assignment, centroids, norm_gain, inner_weight, outer_weight):
    tok_count, features = tokens.shape
    experts = lax.axis_size("expert")
    groups = lax.axis_size("dp")
    capacity = 2 * tok_count // experts
    slot_total = experts * capacity
    units = inner_weight.shape[1]
    targets = 2 if capacity % 16 == 0 and experts & (experts - 1) == 0 and experts >= 8 else 1
    cut = features // 128 * FIRST_SHARE // 16 * 128
    widths = (cut, features - cut)
    back_cut = (features // 128 + 1) // 2 * 128
    back_widths = (back_cut, features - back_cut)
    move_flops = slot_total * tok_count * features
    half_bytes = 2 * slot_total * features
    *packed, place, gain, centroid = call(
        functools.partial(pack_kernel, targets, experts, capacity, cut),
        [shape(slot_total // targets, w) for w in widths for _ in range(targets)]
        + [
            shape(slot_total, tok_count),
            pltpu.VMEM((1, features), F32),
            pltpu.VMEM((1, features), BF16),
        ],
        [stay(a) for a in (assignment.reshape(1, tok_count), tokens, norm_gain, centroids)],
        2 * move_flops,
        2 * half_bytes,
        [FAR] * 4,
        [
            pltpu.VMEM((1, tok_count), jnp.int32),
            pltpu.VMEM((tok_count, features), BF16),
            pltpu.SemaphoreType.DMA((4,)),
        ],
    )
    if targets == 2:
        first = exchange(packed[:targets], experts, capacity)
        second = exchange(packed[targets:], experts, capacity, first[1])
    else:
        first, second = [together(packed[0])], [together(packed[1])]
    rows, select = call(
        first_kernel,
        [shape(tok_count, cut), shape(tok_count, slot_total)],
        first,
        move_flops,
        half_bytes,
    )
    there = [[(i, (i + k) % groups) for i in range(groups)] for k in range(groups)]
    back = [[(t, s) for s, t in pairs] for pairs in there]
    left_guests = [lax.ppermute(rows, "dp", there[k]) for k in range(1, groups)]
    weights = (inner_weight[0], outer_weight[0])
    inner, outer = call(
        load_kernel,
        [pltpu.VMEM(w.shape, BF16) for w in weights],
        [stay(w) for w in weights] + [select],
        0,
        8 * units * features,
        [FAR, FAR, ANYWHERE],
        [pltpu.SemaphoreType.DMA((2,))],
    )
    (right_rows,) = call(
        second_kernel,
        [shape(tok_count, widths[1])],
        [*second, select],
        move_flops,
        half_bytes,
    )
    right_guests = [lax.ppermute(right_rows, "dp", there[k]) for k in range(1, groups)]
    ffn_flops = 4 * 2 * tok_count * units * features
    wide = [pltpu.VMEM((tok_count, features), BF16)]
    own_left, own_right, gate = call(
        own_kernel,
        [shape(tok_count, w) for w in back_widths] + [shape(tok_count, 128, dtype=F32)],
        [rows, right_rows, gain, centroid, inner, outer],
        ffn_flops,
        half_bytes,
        scratch=wide + [pltpu.VMEM((tok_count, units), BF16)],
    )
    left_parts, right_parts = [own_left], [own_right]
    for k in range(1, groups):
        left_part, hidden = call(
            guest_kernel,
            [shape(tok_count, back_cut), shape(tok_count, units)],
            [left_guests[k - 1], right_guests[k - 1], gain, inner, outer],
            ffn_flops * 3 // 4,
            half_bytes,
            scratch=wide,
        )
        left_parts.append(lax.ppermute(left_part, "dp", back[k]))
        (right_part,) = call(
            rest_kernel,
            [shape(tok_count, back_widths[1])],
            [hidden, outer],
            ffn_flops // 4,
            half_bytes,
        )
        right_parts.append(lax.ppermute(right_part, "dp", back[k]))
    (leaving,) = call(
        functools.partial(spread_kernel, groups, capacity, targets == 2),
        [shape(slot_total, features)],
        [*left_parts, *right_parts, gate, select],
        2 * move_flops,
        2 * half_bytes,
    )
    (out,) = call(
        final_kernel,
        [shape(tok_count, features)],
        [tokens, together(leaving), place],
        2 * move_flops,
        2 * half_bytes,
    )
    return out


def solution(mesh):
    in_specs = (
        P(("dp", "expert"), None),
        P(("dp", "expert")),
        P("expert", None),
        P("expert", None),
        P("expert", "dp", None),
        P("expert", "dp", None),
    )
    out_specs = P(("dp", "expert"), None)
    return jax.shard_map(body, mesh=mesh, in_specs=in_specs, out_specs=out_specs, check_vma=False)
```

time: 151 us -> 86.9 us (0.58); the launches traced: 149 us -> 86.7 us
  other arithmetic: 37.8 us -> 0 us
  waiting for transfers between devices: 32.4 us -> 8.87 us
  blocking collectives: 13.5 us -> 33.2 us
  Pallas kernels: 0 us -> 17.6 us
  local copies, waits for them, and re-layouts: 15 us -> 0.01 us
  between operations: 13.6 us -> 0.13 us
  matrix products: 11.2 us -> 0 us
  starting transfers between devices: 25.2 us -> 26.9 us
    all_to_all x0 -> x1, blocking collectives: none -> 33.2 us  [together(): lax.all_to_all(rows, 'expert', split_axis=0, concat_axis=0, tiled=True)]
    all_to_all x4 -> x0, waiting for transfers between devices: 32.4 us -> none  [the longest x1 20.6 us: body(): lax.all_to_all(returning, 'expert', split_axis=0, concat_axis=0, tiled=True)]
    ppermute x0 -> x20, starting transfers between devices: none -> 26.9 us  [the longest x16 22.7 us: swap(): lax.ppermute(array, 'expert', [(i, i ^ axis_mask) for i in range(experts)])]
    all_to_all x4 -> x0, starting transfers between devices: 25.2 us -> none  [the longest x1 7.32 us: body(): lax.all_to_all(send_counts, 'expert', split_axis=0, concat_axis=0, tiled=...]
    and x3 -> x0, other arithmetic: 21.1 us -> none  [the longest x1 11.2 us: body(): jnp.take(expert_out, compact, axis=0)]
    pallas_call x0 -> x11, Pallas kernels: none -> 17.6 us  [call(): pl.pallas_call(kernel, out_shape=tuple(outs), in_specs=[LOCAL] * len(args...]
    all_gather x1 -> x0, blocking collectives: 13.5 us -> none  [body(): lax.all_gather(local_rows, 'dp', axis=0, tiled=True)]
    gather x11 -> x0, local copies, waits for them, and re-layouts: 13.5 us -> none  [the longest x1 3.44 us: body(): jnp.take(tokens, source_row, axis=0)]
  transfers between devices with their start and end apart: 5 -> 20, of which waited for: 4 -> 5; matrix products, arithmetic and copies ran while one was open for 31% -> 0% of each run, Pallas kernels for 0% -> 12%
where the time goes in v3:
time: 86.9 us; the launch traced here: 86.7 us
  blocking collectives  33.2 us (38%)
  starting transfers between devices  26.9 us (31%)
  Pallas kernels  17.6 us (20%)
  waiting for transfers between devices  8.87 us (10%)
    all_to_all x1, blocking collectives, together(): lax.all_to_all(rows, 'expert', split_axis=0, concat_axis=0, tiled=True)  33.2 us
    ppermute x16, starting transfers between devices, swap(): lax.ppermute(array, 'expert', [(i, i ^ axis_mask) for i in range(experts)])  22.7 us
    pallas_call x11, Pallas kernels, call(): pl.pallas_call(kernel, out_shape=tuple(outs), in_specs=[LOCAL] * len(args...  17.6 us
    ppermute x16, waiting for transfers between devices, swap(): lax.ppermute(array, 'expert', [(i, i ^ axis_mask) for i in range(experts)])  4.21 us
    ppermute x1, waiting for transfers between devices, body(): left_parts.append(lax.ppermute(left_part, 'dp', back[k]))  3.6 us
  transfers between devices with their start and end apart: 20, of which 5 were waited for; matrix products, arithmetic and copies ran while one was open for 0% of the time, Pallas kernels for 12%

profile of v3, /device:TPU:1, one launch (start us, length us, event | category | flops | bytes accessed | tf_op | source)
XLA Modules:
  0.0 86.7 jit_solution(11263165461418544203)
XLA Ops:
  0.0 1.5 %shard_map.64 = (bf16[128,1024]{1,0:T(8,128)(2,1)S(1)}, bf16[128,1024]{1,0:T(8,128)(2,1)S(1)}, bf16[128,896]{1,0:T(8,128)(2,1)S(1)}, bf16[128,896]{1,0:T(8,128)(...) custom-call(s32[1,128]{1,0:T(1,128)} %bitcast.9, ...), custom_call_target="tpu_custom_call" | custom-call | flops 125829120 | bytes 1966080 | tf_op jit(solution)/shard_map/pallas_call | solution.py:26
  1.5 0.1 collective-permute-start
  1.6 0.5 collective-permute-start.8
  2.1 1.0 %collective-permute-done.crossed_ref = bf16[128,1024]{1,0:T(8,128)(2,1)S(1)} collective-permute-done((bf16[128,1024]{1,0:T(8,128)(2,1)S(1)}, bf16[128,1024]{1,0:T(8,128)(2,1)S(1)}, u32[]{:S(2)}, u32[]{:S(2)}) %collective-permute-start) | collective-permute-done | bytes 262176 | tf_op jit(solution)/shard_map/ppermute | solution.py:231
  3.2 2.4 %collective-permute-start.1 = (bf16[32,1024]{1,0:T(8,128)(2,1)S(1)}, bf16[32,1024]{1,0:T(8,128)(2,1)S(1)}, u32[]{:S(2)}, u32[]{:S(2)}) collective-permute-start(bf16[32,1024]{1,0:T(8,128)(2,1)S(1)} %get-tuple-element.40), channel_id=1, source_target_pairs={{0,2},{1,3},{2,0},{3,1},{4,6},{5,7},{6,4},{7,5},{8,10},{9,11},{10,... | collective-permute-start | bytes 196616 | tf_op jit(solution)/shard_map/ppermute | solution.py:231
  5.6 1.3 %collective-permute-start.2 = (bf16[32,1024]{1,0:T(8,128)(2,1)S(1)}, bf16[32,1024]{1,0:T(8,128)(2,1)S(1)}, u32[]{:S(2)}, u32[]{:S(2)}) collective-permute-start(bf16[32,1024]{1,0:T(8,128)(2,1)S(1)} %get-tuple-element.41), channel_id=1, source_target_pairs={{0,4},{1,5},{2,6},{3,7},{4,0},{5,1},{6,2},{7,3},{8,12},{9,13},{10,... | collective-permute-start | bytes 196616 | tf_op jit(solution)/shard_map/ppermute | solution.py:231
  6.9 0.0 collective-permute-start.3
  6.9 2.4 %collective-permute-start.4 = (bf16[32,1024]{1,0:T(8,128)(2,1)S(1)}, bf16[32,1024]{1,0:T(8,128)(2,1)S(1)}, u32[]{:S(2)}, u32[]{:S(2)}) collective-permute-start(bf16[32,1024]{1,0:T(8,128)(2,1)S(1)} %get-tuple-element.43), channel_id=1, source_target_pairs={{0,8},{1,9},{2,10},{3,11},{4,12},{5,13},{6,14},{7,15},{8,0},{9,1},... | collective-permute-start | bytes 196616 | tf_op jit(solution)/shard_map/ppermute | solution.py:231
  9.3 0.0 collective-permute-done.8.crossed_ref
  9.3 1.0 %collective-permute-start.5 = (bf16[32,1024]{1,0:T(8,128)(2,1)S(1)}, bf16[32,1024]{1,0:T(8,128)(2,1)S(1)}, u32[]{:S(2)}, u32[]{:S(2)}) collective-permute-start(bf16[32,1024]{1,0:T(8,128)(2,1)S(1)} %get-tuple-element.44), channel_id=1, source_target_pairs={{0,10},{1,11},{2,8},{3,9},{4,14},{5,15},{6,12},{7,13},{8,2},{9,3},... | collective-permute-start | bytes 196616 | tf_op jit(solution)/shard_map/ppermute | solution.py:231
  10.3 0.0 collective-permute-done.1.refs_1_._
  10.3 3.3 %collective-permute-start.6 = (bf16[32,1024]{1,0:T(8,128)(2,1)S(1)}, bf16[32,1024]{1,0:T(8,128)(2,1)S(1)}, u32[]{:S(2)}, u32[]{:S(2)}) collective-permute-start(bf16[32,1024]{1,0:T(8,128)(2,1)S(1)} %get-tuple-element.45), channel_id=1, source_target_pairs={{0,12},{1,13},{2,14},{3,15},{4,8},{5,9},{6,10},{7,11},{8,4},{9,5},... | collective-permute-start | bytes 196616 | tf_op jit(solution)/shard_map/ppermute | solution.py:231
  13.6 0.0 collective-permute-done.2.refs_2_
  13.6 0.0 collective-permute-start.7
  13.7 0.0 collective-permute-done.3.refs_3_
  13.7 0.1 collective-permute-start.10
  13.8 0.0 collective-permute-done.4.refs_4_
  13.8 2.6 %collective-permute-start.11 = (bf16[32,896]{1,0:T(8,128)(2,1)S(1)}, bf16[32,896]{1,0:T(8,128)(2,1)S(1)}, u32[]{:S(2)}, u32[]{:S(2)}) collective-permute-start(bf16[32,896]{1,0:T(8,128)(2,1)S(1)} %get-tuple-element.53), channel_id=1, source_target_pairs={{0,6},{1,7},{2,4},{3,5},{4,2},{5,3},{6,0},{7,1},{8,14},{9,15},{10,... | collective-permute-start | bytes 172040 | tf_op jit(solution)/shard_map/ppermute | solution.py:231
  16.4 2.5 %collective-permute-done.5.refs_5_ = bf16[32,1024]{1,0:T(8,128)(2,1)S(1)} collective-permute-done((bf16[32,1024]{1,0:T(8,128)(2,1)S(1)}, bf16[32,1024]{1,0:T(8,128)(2,1)S(1)}, u32[]{:S(2)}, u32[]{:S(2)}) %collective-permute-start.5) | collective-permute-done | bytes 65568 | tf_op jit(solution)/shard_map/ppermute | solution.py:231
  18.9 1.5 %collective-permute-start.12 = (bf16[32,896]{1,0:T(8,128)(2,1)S(1)}, bf16[32,896]{1,0:T(8,128)(2,1)S(1)}, u32[]{:S(2)}, u32[]{:S(2)}) collective-permute-start(bf16[32,896]{1,0:T(8,128)(2,1)S(1)} %get-tuple-element.54), channel_id=1, source_target_pairs={{0,8},{1,9},{2,10},{3,11},{4,12},{5,13},{6,14},{7,15},{8,0},{9,1},... | collective-permute-start | bytes 172040 | tf_op jit(solution)/shard_map/ppermute | solution.py:231
  20.4 0.0 collective-permute-done.6.refs_6_
  20.4 3.1 %collective-permute-start.13 = (bf16[32,896]{1,0:T(8,128)(2,1)S(1)}, bf16[32,896]{1,0:T(8,128)(2,1)S(1)}, u32[]{:S(2)}, u32[]{:S(2)}) collective-permute-start(bf16[32,896]{1,0:T(8,128)(2,1)S(1)} %get-tuple-element.55), channel_id=1, source_target_pairs={{0,10},{1,11},{2,8},{3,9},{4,14},{5,15},{6,12},{7,13},{8,2},{9,3},... | collective-permute-start | bytes 172040 | tf_op jit(solution)/shard_map/ppermute | solution.py:231
  23.4 0.0 collective-permute-done.7.refs_7_
  23.4 0.9 %collective-permute-start.14 = (bf16[32,896]{1,0:T(8,128)(2,1)S(1)}, bf16[32,896]{1,0:T(8,128)(2,1)S(1)}, u32[]{:S(2)}, u32[]{:S(2)}) collective-permute-start(bf16[32,896]{1,0:T(8,128)(2,1)S(1)} %get-tuple-element.56), channel_id=1, source_target_pairs={{0,12},{1,13},{2,14},{3,15},{4,8},{5,9},{6,10},{7,11},{8,4},{9,5},... | collective-permute-start | bytes 172040 | tf_op jit(solution)/shard_map/ppermute | solution.py:231
  24.4 0.0 collective-permute-done.10.refs_2_
  24.4 2.2 %collective-permute-start.15 = (bf16[32,896]{1,0:T(8,128)(2,1)S(1)}, bf16[32,896]{1,0:T(8,128)(2,1)S(1)}, u32[]{:S(2)}, u32[]{:S(2)}) collective-permute-start(bf16[32,896]{1,0:T(8,128)(2,1)S(1)} %get-tuple-element.57), channel_id=1, source_target_pairs={{0,14},{1,15},{2,12},{3,13},{4,10},{5,11},{6,8},{7,9},{8,6},{9,7},... | collective-permute-start | bytes 172040 | tf_op jit(solution)/shard_map/ppermute | solution.py:231
  26.6 0.0 collective-permute-done.11.refs_3_
  26.6 1.3 %collective-permute-start.9 = (bf16[32,896]{1,0:T(8,128)(2,1)S(1)}, bf16[32,896]{1,0:T(8,128)(2,1)S(1)}, u32[]{:S(2)}, u32[]{:S(2)}) collective-permute-start(bf16[32,896]{1,0:T(8,128)(2,1)S(1)} %get-tuple-element.51), channel_id=1, source_target_pairs={{0,2},{1,3},{2,0},{3,1},{4,6},{5,7},{6,4},{7,5},{8,10},{9,11},{10,... | collective-permute-start | bytes 172040 | tf_op jit(solution)/shard_map/ppermute | solution.py:231
  27.9 0.5 shard_map.66
  28.4 0.0 collective-permute-done.12.refs_4_
  28.4 1.3 %collective-permute-start.16 = (bf16[128,1024]{1,0:T(8,128)(2,1)S(1)}, bf16[128,1024]{1,0:T(8,128)(2,1)S(1)}, u32[]{:S(2)}, u32[]{:S(2)}) collective-permute-start(bf16[128,1024]{1,0:T(8,128)(2,1)S(1)} %get-tuple-element.47.left_ref), channel_id=1, source_target_pairs={{0,16},{16,0},{1,17},{17,1},{2,18},{18,2},{3,19},{19,3},{4,20},{20... | collective-permute-start | bytes 786440 | tf_op jit(solution)/shard_map/ppermute | solution.py:305
  29.7 0.0 collective-permute-done.13.refs_5_
  29.7 0.0 collective-permute-done.14.refs_6_
  29.7 0.7 collective-permute-done.15.refs_7_
  30.4 0.0 collective-permute-done.9.refs_1_
  30.4 0.2 shard_map.68.right_ref
  30.6 1.3 %collective-permute-start.17 = (bf16[128,896]{1,0:T(8,128)(2,1)S(1)}, bf16[128,896]{1,0:T(8,128)(2,1)S(1)}, u32[]{:S(2)}, u32[]{:S(2)}) collective-permute-start(bf16[128,896]{1,0:T(8,128)(2,1)S(1)} %shard_map.68.right_ref), channel_id=1, source_target_pairs={{0,16},{16,0},{1,17},{17,1},{2,18},{18,2},{3,19},{19,3},{4,20},{20... | collective-permute-start | bytes 688136 | tf_op jit(solution)/shard_map/ppermute | solution.py:323
  31.9 5.5 %shard_map.69 = (bf16[2048,1920]{1,0:T(8,128)(2,1)S(1)}, bf16[2048,1920]{1,0:T(8,128)(2,1)S(1)}) custom-call(bf16[2048,1920]{1,0:T(8,128)(2,1)} %bitcast.7, bf16[2048,1920]{1,0:T(8,128)(2,1)} %bitcast.8, bf16[128,256]{1,0:T(8,128)(2,1)S(1)} %get-tuple-element.58.refs_8_._.refs_5_), custom_call_target="tpu_custom_call" | custom-call | bytes 31457280 | tf_op jit(solution)/shard_map/pallas_call | solution.py:26
  37.4 0.0 collective-permute-done.16.left_ref
  37.4 1.1 %collective-permute-done.17.right_ref = bf16[128,896]{1,0:T(8,128)(2,1)S(1)} collective-permute-done((bf16[128,896]{1,0:T(8,128)(2,1)S(1)}, bf16[128,896]{1,0:T(8,128)(2,1)S(1)}, u32[]{:S(2)}, u32[]{:S(2)}) %collective-permute-start.17) | collective-permute-done | bytes 229408 | tf_op jit(solution)/shard_map/ppermute | solution.py:323
  38.5 3.4 %shard_map.71 = (bf16[128,1024]{1,0:T(8,128)(2,1)S(1)}, bf16[128,2048]{1,0:T(8,128)(2,1)S(1)}) custom-call(bf16[128,1024]{1,0:T(8,128)(2,1)S(1)} %collective-permute-done.16.left_ref, bf16[128,896]{1,0:T(8,128)(2,1)S(1)} %collective-permute-done.17.right_ref, f32[1,1920]{1,0:T(1,128)S(1)} %get-tuple-element.59.gain_ref, ...), custom_call_target="tpu_custom_call" | custom-call | flops 3019898880 | bytes 983040 | tf_op jit(solution)/shard_map/pallas_call | solution.py:26
  41.9 0.7 shard_map.72
  42.7 1.3 %collective-permute-start.19 = (bf16[128,896]{1,0:T(8,128)(2,1)S(1)}, bf16[128,896]{1,0:T(8,128)(2,1)S(1)}, u32[]{:S(2)}, u32[]{:S(2)}) collective-permute-start(bf16[128,896]{1,0:T(8,128)(2,1)S(1)} %shard_map.72), channel_id=1, source_target_pairs={{16,0},{0,16},{17,1},{1,17},{18,2},{2,18},{19,3},{3,19},{20,4},{4,... | collective-permute-start | bytes 688136 | tf_op jit(solution)/shard_map/ppermute | solution.py:352
  44.0 0.2 collective-permute-start.18
  44.2 0.0 copy-start
  44.2 4.0 %shard_map.70 = (bf16[128,1024]{1,0:T(8,128)(2,1)S(1)}, bf16[128,896]{1,0:T(8,128)(2,1)S(1)}, f32[128,128]{1,0:T(8,128)S(1)}) custom-call(bf16[128,1024]{1,0:T(8,128)(2,1)S(1)} %get-tuple-element.47.left_ref, bf16[128,896]{1,0:T(8,128)(2,1)S(1)} %shard_map.68.right_ref, f32[1,1920]{1,0:T(1,128)S(1)} %get-tuple-element.59.gain_ref, ...), custom_call_target="tpu_custom_call" | custom-call | flops 4026531840 | bytes 983040 | tf_op jit(solution)/shard_map/pallas_call | solution.py:26
  48.3 0.0 collective-permute-done.19.refs_3_
  48.3 3.6 %collective-permute-done.18.refs_1_ = bf16[128,1024]{1,0:T(8,128)(2,1)S(1)} collective-permute-done((bf16[128,1024]{1,0:T(8,128)(2,1)S(1)}, bf16[128,1024]{1,0:T(8,128)(2,1)S(1)}, u32[]{:S(2)}, u32[]{:S(2)}) %collective-permute-start.18) | collective-permute-done | bytes 262176 | tf_op jit(solution)/shard_map/ppermute | solution.py:344
  51.9 0.5 shard_map.73
  52.4 33.2 %all_to_all.11 = bf16[16,16,1920]{2,1,0:T(8,128)(2,1)S(1)} all-to-all(bf16[16,16,1920]{2,1,0:T(8,128)(2,1)S(1)} %bitcast.5), channel_id=1, replica_groups=mesh['dp'=2,'expert'=16] {'expert'}, dimensions={0} | all-to-all | bytes 1966080 | tf_op jit(solution)/shard_map/all_to_all | solution.py:256
  85.6 0.0 copy-done
  85.6 1.1 %shard_map.74 = bf16[128,1920]{1,0:T(8,128)(2,1)} custom-call(bf16[128,1920]{1,0:T(8,128)(2,1)S(1)} %copy-done, bf16[256,1920]{1,0:T(8,128)(2,1)S(1)} %bitcast.6, bf16[256,128]{1,0:T(8,128)(2,1)S(1)} %get-tuple-element.68.place_ref), custom_call_target="tpu_custom_call" | custom-call | flops 125829120 | bytes 1966080 | tf_op jit(solution)/shard_map/pallas_call | solution.py:26
  (2 shorter events, 0.1 us)
Async XLA Ops:
  1.5 1.6 %collective-permute-start = (bf16[128,1024]{1,0:T(8,128)(2,1)S(1)}, bf16[128,1024]{1,0:T(8,128)(2,1)S(1)}, u32[]{:S(2)}, u32[]{:S(2)}) collective-permute-start(bf16[128,1024]{1,0:T(8,128)(2,1)S(1)} %get-tuple-element.38), channel_id=1, source_target_pairs={{0,1},{1,0},{2,3},{3,2},{4,5},{5,4},{6,7},{7,6},{8,9},{9,8},{10,11... | collective-permute-start | bytes 786440 | tf_op jit(solution)/shard_map/ppermute | solution.py:231
  1.6 7.7 %collective-permute-start.8 = (bf16[128,896]{1,0:T(8,128)(2,1)S(1)}, bf16[128,896]{1,0:T(8,128)(2,1)S(1)}, u32[]{:S(2)}, u32[]{:S(2)}) collective-permute-start(bf16[128,896]{1,0:T(8,128)(2,1)S(1)} %get-tuple-element.49), channel_id=1, source_target_pairs={{0,1},{1,0},{2,3},{3,2},{4,5},{5,4},{6,7},{7,6},{8,9},{9,8},{10,11... | collective-permute-start | bytes 688136 | tf_op jit(solution)/shard_map/ppermute | solution.py:231
  3.2 7.1 %collective-permute-start.1 = (bf16[32,1024]{1,0:T(8,128)(2,1)S(1)}, bf16[32,1024]{1,0:T(8,128)(2,1)S(1)}, u32[]{:S(2)}, u32[]{:S(2)}) collective-permute-start(bf16[32,1024]{1,0:T(8,128)(2,1)S(1)} %get-tuple-element.40), channel_id=1, source_target_pairs={{0,2},{1,3},{2,0},{3,1},{4,6},{5,7},{6,4},{7,5},{8,10},{9,11},{10,... | collective-permute-start | bytes 196616 | tf_op jit(solution)/shard_map/ppermute | solution.py:231
  5.6 8.1 %collective-permute-start.2 = (bf16[32,1024]{1,0:T(8,128)(2,1)S(1)}, bf16[32,1024]{1,0:T(8,128)(2,1)S(1)}, u32[]{:S(2)}, u32[]{:S(2)}) collective-permute-start(bf16[32,1024]{1,0:T(8,128)(2,1)S(1)} %get-tuple-element.41), channel_id=1, source_target_pairs={{0,4},{1,5},{2,6},{3,7},{4,0},{5,1},{6,2},{7,3},{8,12},{9,13},{10,... | collective-permute-start | bytes 196616 | tf_op jit(solution)/shard_map/ppermute | solution.py:231
  6.9 6.9 %collective-permute-start.3 = (bf16[32,1024]{1,0:T(8,128)(2,1)S(1)}, bf16[32,1024]{1,0:T(8,128)(2,1)S(1)}, u32[]{:S(2)}, u32[]{:S(2)}) collective-permute-start(bf16[32,1024]{1,0:T(8,128)(2,1)S(1)} %get-tuple-element.42), channel_id=1, source_target_pairs={{0,6},{1,7},{2,4},{3,5},{4,2},{5,3},{6,0},{7,1},{8,14},{9,15},{10,... | collective-permute-start | bytes 196616 | tf_op jit(solution)/shard_map/ppermute | solution.py:231
  6.9 6.9 %collective-permute-start.4 = (bf16[32,1024]{1,0:T(8,128)(2,1)S(1)}, bf16[32,1024]{1,0:T(8,128)(2,1)S(1)}, u32[]{:S(2)}, u32[]{:S(2)}) collective-permute-start(bf16[32,1024]{1,0:T(8,128)(2,1)S(1)} %get-tuple-element.43), channel_id=1, source_target_pairs={{0,8},{1,9},{2,10},{3,11},{4,12},{5,13},{6,14},{7,15},{8,0},{9,1},... | collective-permute-start | bytes 196616 | tf_op jit(solution)/shard_map/ppermute | solution.py:231
  9.3 9.6 %collective-permute-start.5 = (bf16[32,1024]{1,0:T(8,128)(2,1)S(1)}, bf16[32,1024]{1,0:T(8,128)(2,1)S(1)}, u32[]{:S(2)}, u32[]{:S(2)}) collective-permute-start(bf16[32,1024]{1,0:T(8,128)(2,1)S(1)} %get-tuple-element.44), channel_id=1, source_target_pairs={{0,10},{1,11},{2,8},{3,9},{4,14},{5,15},{6,12},{7,13},{8,2},{9,3},... | collective-permute-start | bytes 196616 | tf_op jit(solution)/shard_map/ppermute | solution.py:231
  10.3 10.1 %collective-permute-start.6 = (bf16[32,1024]{1,0:T(8,128)(2,1)S(1)}, bf16[32,1024]{1,0:T(8,128)(2,1)S(1)}, u32[]{:S(2)}, u32[]{:S(2)}) collective-permute-start(bf16[32,1024]{1,0:T(8,128)(2,1)S(1)} %get-tuple-element.45), channel_id=1, source_target_pairs={{0,12},{1,13},{2,14},{3,15},{4,8},{5,9},{6,10},{7,11},{8,4},{9,5},... | collective-permute-start | bytes 196616 | tf_op jit(solution)/shard_map/ppermute | solution.py:231
  13.6 9.8 %collective-permute-start.7 = (bf16[32,1024]{1,0:T(8,128)(2,1)S(1)}, bf16[32,1024]{1,0:T(8,128)(2,1)S(1)}, u32[]{:S(2)}, u32[]{:S(2)}) collective-permute-start(bf16[32,1024]{1,0:T(8,128)(2,1)S(1)} %get-tuple-element.46), channel_id=1, source_target_pairs={{0,14},{1,15},{2,12},{3,13},{4,10},{5,11},{6,8},{7,9},{8,6},{9,7},... | collective-permute-start | bytes 196616 | tf_op jit(solution)/shard_map/ppermute | solution.py:231
  13.7 10.6 %collective-permute-start.10 = (bf16[32,896]{1,0:T(8,128)(2,1)S(1)}, bf16[32,896]{1,0:T(8,128)(2,1)S(1)}, u32[]{:S(2)}, u32[]{:S(2)}) collective-permute-start(bf16[32,896]{1,0:T(8,128)(2,1)S(1)} %get-tuple-element.52), channel_id=1, source_target_pairs={{0,4},{1,5},{2,6},{3,7},{4,0},{5,1},{6,2},{7,3},{8,12},{9,13},{10,... | collective-permute-start | bytes 172040 | tf_op jit(solution)/shard_map/ppermute | solution.py:231
  13.8 12.7 %collective-permute-start.11 = (bf16[32,896]{1,0:T(8,128)(2,1)S(1)}, bf16[32,896]{1,0:T(8,128)(2,1)S(1)}, u32[]{:S(2)}, u32[]{:S(2)}) collective-permute-start(bf16[32,896]{1,0:T(8,128)(2,1)S(1)} %get-tuple-element.53), channel_id=1, source_target_pairs={{0,6},{1,7},{2,4},{3,5},{4,2},{5,3},{6,0},{7,1},{8,14},{9,15},{10,... | collective-permute-start | bytes 172040 | tf_op jit(solution)/shard_map/ppermute | solution.py:231
  18.9 9.5 %collective-permute-start.12 = (bf16[32,896]{1,0:T(8,128)(2,1)S(1)}, bf16[32,896]{1,0:T(8,128)(2,1)S(1)}, u32[]{:S(2)}, u32[]{:S(2)}) collective-permute-start(bf16[32,896]{1,0:T(8,128)(2,1)S(1)} %get-tuple-element.54), channel_id=1, source_target_pairs={{0,8},{1,9},{2,10},{3,11},{4,12},{5,13},{6,14},{7,15},{8,0},{9,1},... | collective-permute-start | bytes 172040 | tf_op jit(solution)/shard_map/ppermute | solution.py:231
  20.4 9.3 %collective-permute-start.13 = (bf16[32,896]{1,0:T(8,128)(2,1)S(1)}, bf16[32,896]{1,0:T(8,128)(2,1)S(1)}, u32[]{:S(2)}, u32[]{:S(2)}) collective-permute-start(bf16[32,896]{1,0:T(8,128)(2,1)S(1)} %get-tuple-element.55), channel_id=1, source_target_pairs={{0,10},{1,11},{2,8},{3,9},{4,14},{5,15},{6,12},{7,13},{8,2},{9,3},... | collective-permute-start | bytes 172040 | tf_op jit(solution)/shard_map/ppermute | solution.py:231
  23.4 6.3 %collective-permute-start.14 = (bf16[32,896]{1,0:T(8,128)(2,1)S(1)}, bf16[32,896]{1,0:T(8,128)(2,1)S(1)}, u32[]{:S(2)}, u32[]{:S(2)}) collective-permute-start(bf16[32,896]{1,0:T(8,128)(2,1)S(1)} %get-tuple-element.56), channel_id=1, source_target_pairs={{0,12},{1,13},{2,14},{3,15},{4,8},{5,9},{6,10},{7,11},{8,4},{9,5},... | collective-permute-start | bytes 172040 | tf_op jit(solution)/shard_map/ppermute | solution.py:231
  24.4 6.0 %collective-permute-start.15 = (bf16[32,896]{1,0:T(8,128)(2,1)S(1)}, bf16[32,896]{1,0:T(8,128)(2,1)S(1)}, u32[]{:S(2)}, u32[]{:S(2)}) collective-permute-start(bf16[32,896]{1,0:T(8,128)(2,1)S(1)} %get-tuple-element.57), channel_id=1, source_target_pairs={{0,14},{1,15},{2,12},{3,13},{4,10},{5,11},{6,8},{7,9},{8,6},{9,7},... | collective-permute-start | bytes 172040 | tf_op jit(solution)/shard_map/ppermute | solution.py:231
  26.6 3.8 %collective-permute-start.9 = (bf16[32,896]{1,0:T(8,128)(2,1)S(1)}, bf16[32,896]{1,0:T(8,128)(2,1)S(1)}, u32[]{:S(2)}, u32[]{:S(2)}) collective-permute-start(bf16[32,896]{1,0:T(8,128)(2,1)S(1)} %get-tuple-element.51), channel_id=1, source_target_pairs={{0,2},{1,3},{2,0},{3,1},{4,6},{5,7},{6,4},{7,5},{8,10},{9,11},{10,... | collective-permute-start | bytes 172040 | tf_op jit(solution)/shard_map/ppermute | solution.py:231
  28.4 9.0 %collective-permute-start.16 = (bf16[128,1024]{1,0:T(8,128)(2,1)S(1)}, bf16[128,1024]{1,0:T(8,128)(2,1)S(1)}, u32[]{:S(2)}, u32[]{:S(2)}) collective-permute-start(bf16[128,1024]{1,0:T(8,128)(2,1)S(1)} %get-tuple-element.47.left_ref), channel_id=1, source_target_pairs={{0,16},{16,0},{1,17},{17,1},{2,18},{18,2},{3,19},{19,3},{4,20},{20... | collective-permute-start | bytes 786440 | tf_op jit(solution)/shard_map/ppermute | solution.py:305
  30.6 7.9 %collective-permute-start.17 = (bf16[128,896]{1,0:T(8,128)(2,1)S(1)}, bf16[128,896]{1,0:T(8,128)(2,1)S(1)}, u32[]{:S(2)}, u32[]{:S(2)}) collective-permute-start(bf16[128,896]{1,0:T(8,128)(2,1)S(1)} %shard_map.68.right_ref), channel_id=1, source_target_pairs={{0,16},{16,0},{1,17},{17,1},{2,18},{18,2},{3,19},{19,3},{4,20},{20... | collective-permute-start | bytes 688136 | tf_op jit(solution)/shard_map/ppermute | solution.py:323
  42.7 5.6 %collective-permute-start.19 = (bf16[128,896]{1,0:T(8,128)(2,1)S(1)}, bf16[128,896]{1,0:T(8,128)(2,1)S(1)}, u32[]{:S(2)}, u32[]{:S(2)}) collective-permute-start(bf16[128,896]{1,0:T(8,128)(2,1)S(1)} %shard_map.72), channel_id=1, source_target_pairs={{16,0},{0,16},{17,1},{1,17},{18,2},{2,18},{19,3},{3,19},{20,4},{4,... | collective-permute-start | bytes 688136 | tf_op jit(solution)/shard_map/ppermute | solution.py:352
  44.0 7.9 %collective-permute-start.18 = (bf16[128,1024]{1,0:T(8,128)(2,1)S(1)}, bf16[128,1024]{1,0:T(8,128)(2,1)S(1)}, u32[]{:S(2)}, u32[]{:S(2)}) collective-permute-start(bf16[128,1024]{1,0:T(8,128)(2,1)S(1)} %get-tuple-element.64), channel_id=1, source_target_pairs={{16,0},{0,16},{17,1},{1,17},{18,2},{2,18},{19,3},{3,19},{20,4},{4,... | collective-permute-start | bytes 786440 | tf_op jit(solution)/shard_map/ppermute | solution.py:344
  44.2 41.4 %copy-start = (bf16[128,1920]{1,0:T(8,128)(2,1)S(1)}, bf16[128,1920]{1,0:T(8,128)(2,1)}, u32[]{:S(2)}) copy-start(bf16[128,1920]{1,0:T(8,128)(2,1)} %tokens_ref.1) | copy-start | bytes 1474564

commit v4 on v3

--- a/solution.py
+++ b/solution.py
@@ -266,7 +266,7 @@
     targets = 2 if capacity % 16 == 0 and experts & (experts - 1) == 0 and experts >= 8 else 1
     cut = features // 128 * FIRST_SHARE // 16 * 128
     widths = (cut, features - cut)
-    back_cut = (features // 128 + 1) // 2 * 128
+    back_cut = (features // 128 * 3 + 3) // 4 * 128
     back_widths = (back_cut, features - back_cut)
     move_flops = slot_total * tok_count * features
     half_bytes = 2 * slot_total * features
@@ -290,7 +290,7 @@
     )
     if targets == 2:
         first = exchange(packed[:targets], experts, capacity)
-        second = exchange(packed[targets:], experts, capacity, first[1])
+        second = exchange(packed[targets:], experts, capacity, first[experts // 4])
     else:
         first, second = [together(packed[0])], [together(packed[1])]
     rows, select = call(

time: 86.9 us -> 83.3 us (0.959)
  blocking collectives: 33.2 us -> 31.7 us
  starting transfers between devices: 26.9 us -> 25.7 us
    ppermute x1, waiting for transfers between devices: 3.6 us -> 0.01 us  [body(): left_parts.append(lax.ppermute(left_part, 'dp', back[k]))]
    ppermute x1, waiting for transfers between devices: 0.01 us -> 3.19 us  [body(): right_parts.append(lax.ppermute(right_part, 'dp', back[k]))]
    all_to_all x1, blocking collectives: 33.2 us -> 31.7 us  [together(): lax.all_to_all(rows, 'expert', split_axis=0, concat_axis=0, tiled=True)]
    ppermute x16, starting transfers between devices: 22.7 us -> 21.5 us  [swap(): lax.ppermute(array, 'expert', [(i, i ^ axis_mask) for i in range(experts)])]
    ppermute x1, starting transfers between devices: 0.23 us -> 1.31 us  [body(): left_parts.append(lax.ppermute(left_part, 'dp', back[k]))]
    ppermute x1, starting transfers between devices: 1.3 us -> 0.28 us  [body(): right_parts.append(lax.ppermute(right_part, 'dp', back[k]))]
  transfers between devices with their start and end apart: 20 -> 20, of which waited for: 5 -> 5; matrix products, arithmetic and copies ran while one was open for 0% -> 0% of each run, Pallas kernels for 12% -> 13%
where the time goes in v4:
time: 83.3 us; the launch traced here: 83.1 us
  blocking collectives  31.7 us (38%)
  starting transfers between devices  25.7 us (31%)
  Pallas kernels  17.6 us (21%)
  waiting for transfers between devices  8.04 us (10%)
    all_to_all x1, blocking collectives, together(): lax.all_to_all(rows, 'expert', split_axis=0, concat_axis=0, tiled=True)  31.7 us
    ppermute x16, starting transfers between devices, swap(): lax.ppermute(array, 'expert', [(i, i ^ axis_mask) for i in range(experts)])  21.5 us
    pallas_call x11, Pallas kernels, call(): pl.pallas_call(kernel, out_shape=tuple(outs), in_specs=[LOCAL] * len(args...  17.6 us
    ppermute x16, waiting for transfers between devices, swap(): lax.ppermute(array, 'expert', [(i, i ^ axis_mask) for i in range(experts)])  4.28 us
    ppermute x1, waiting for transfers between devices, body(): right_parts.append(lax.ppermute(right_part, 'dp', back[k]))  3.19 us
  transfers between devices with their start and end apart: 20, of which 5 were waited for; matrix products, arithmetic and copies ran while one was open for 0% of the time, Pallas kernels for 13%

profile of v4, /device:TPU:1, one launch (start us, length us, event | category | flops | bytes accessed | tf_op | source)
XLA Modules:
  0.0 83.1 jit_solution(1688524843107972445)
XLA Ops:
  0.0 1.5 %shard_map.64 = (bf16[128,1024]{1,0:T(8,128)(2,1)S(1)}, bf16[128,1024]{1,0:T(8,128)(2,1)S(1)}, bf16[128,896]{1,0:T(8,128)(2,1)S(1)}, bf16[128,896]{1,0:T(8,128)(...) custom-call(s32[1,128]{1,0:T(1,128)} %bitcast.9, ...), custom_call_target="tpu_custom_call" | custom-call | flops 125829120 | bytes 1966080 | tf_op jit(solution)/shard_map/pallas_call | solution.py:26
  1.5 0.1 collective-permute-start
  1.6 0.5 collective-permute-start.8
  2.1 1.0 %collective-permute-done.crossed_ref = bf16[128,1024]{1,0:T(8,128)(2,1)S(1)} collective-permute-done((bf16[128,1024]{1,0:T(8,128)(2,1)S(1)}, bf16[128,1024]{1,0:T(8,128)(2,1)S(1)}, u32[]{:S(2)}, u32[]{:S(2)}) %collective-permute-start) | collective-permute-done | bytes 262176 | tf_op jit(solution)/shard_map/ppermute | solution.py:231
  3.2 3.5 %collective-permute-start.4 = (bf16[32,1024]{1,0:T(8,128)(2,1)S(1)}, bf16[32,1024]{1,0:T(8,128)(2,1)S(1)}, u32[]{:S(2)}, u32[]{:S(2)}) collective-permute-start(bf16[32,1024]{1,0:T(8,128)(2,1)S(1)} %get-tuple-element.43), channel_id=1, source_target_pairs={{0,8},{1,9},{2,10},{3,11},{4,12},{5,13},{6,14},{7,15},{8,0},{9,1},... | collective-permute-start | bytes 196616 | tf_op jit(solution)/shard_map/ppermute | solution.py:231
  6.7 1.2 %collective-permute-start.1 = (bf16[32,1024]{1,0:T(8,128)(2,1)S(1)}, bf16[32,1024]{1,0:T(8,128)(2,1)S(1)}, u32[]{:S(2)}, u32[]{:S(2)}) collective-permute-start(bf16[32,1024]{1,0:T(8,128)(2,1)S(1)} %get-tuple-element.40), channel_id=1, source_target_pairs={{0,2},{1,3},{2,0},{3,1},{4,6},{5,7},{6,4},{7,5},{8,10},{9,11},{10,... | collective-permute-start | bytes 196616 | tf_op jit(solution)/shard_map/ppermute | solution.py:231
  7.9 1.3 %collective-permute-start.2 = (bf16[32,1024]{1,0:T(8,128)(2,1)S(1)}, bf16[32,1024]{1,0:T(8,128)(2,1)S(1)}, u32[]{:S(2)}, u32[]{:S(2)}) collective-permute-start(bf16[32,1024]{1,0:T(8,128)(2,1)S(1)} %get-tuple-element.41), channel_id=1, source_target_pairs={{0,4},{1,5},{2,6},{3,7},{4,0},{5,1},{6,2},{7,3},{8,12},{9,13},{10,... | collective-permute-start | bytes 196616 | tf_op jit(solution)/shard_map/ppermute | solution.py:231
  9.2 0.1 collective-permute-start.3
  9.3 0.0 collective-permute-done.8.crossed_ref
  9.3 1.0 %collective-permute-start.5 = (bf16[32,1024]{1,0:T(8,128)(2,1)S(1)}, bf16[32,1024]{1,0:T(8,128)(2,1)S(1)}, u32[]{:S(2)}, u32[]{:S(2)}) collective-permute-start(bf16[32,1024]{1,0:T(8,128)(2,1)S(1)} %get-tuple-element.44), channel_id=1, source_target_pairs={{0,10},{1,11},{2,8},{3,9},{4,14},{5,15},{6,12},{7,13},{8,2},{9,3},... | collective-permute-start | bytes 196616 | tf_op jit(solution)/shard_map/ppermute | solution.py:231
  10.3 0.0 collective-permute-done.4.refs_4_._
  10.3 3.6 %collective-permute-start.6 = (bf16[32,1024]{1,0:T(8,128)(2,1)S(1)}, bf16[32,1024]{1,0:T(8,128)(2,1)S(1)}, u32[]{:S(2)}, u32[]{:S(2)}) collective-permute-start(bf16[32,1024]{1,0:T(8,128)(2,1)S(1)} %get-tuple-element.45), channel_id=1, source_target_pairs={{0,12},{1,13},{2,14},{3,15},{4,8},{5,9},{6,10},{7,11},{8,4},{9,5},... | collective-permute-start | bytes 196616 | tf_op jit(solution)/shard_map/ppermute | solution.py:231
  13.9 0.0 collective-permute-done.1.refs_1_
  13.9 0.9 %collective-permute-start.7 = (bf16[32,1024]{1,0:T(8,128)(2,1)S(1)}, bf16[32,1024]{1,0:T(8,128)(2,1)S(1)}, u32[]{:S(2)}, u32[]{:S(2)}) collective-permute-start(bf16[32,1024]{1,0:T(8,128)(2,1)S(1)} %get-tuple-element.46), channel_id=1, source_target_pairs={{0,14},{1,15},{2,12},{3,13},{4,10},{5,11},{6,8},{7,9},{8,6},{9,7},... | collective-permute-start | bytes 196616 | tf_op jit(solution)/shard_map/ppermute | solution.py:231
  14.9 0.0 collective-permute-done.2.refs_2_
  14.9 0.1 collective-permute-start.10
  15.0 0.0 collective-permute-done.3.refs_3_
  15.0 1.4 %collective-permute-start.11 = (bf16[32,896]{1,0:T(8,128)(2,1)S(1)}, bf16[32,896]{1,0:T(8,128)(2,1)S(1)}, u32[]{:S(2)}, u32[]{:S(2)}) collective-permute-start(bf16[32,896]{1,0:T(8,128)(2,1)S(1)} %get-tuple-element.53), channel_id=1, source_target_pairs={{0,6},{1,7},{2,4},{3,5},{4,2},{5,3},{6,0},{7,1},{8,14},{9,15},{10,... | collective-permute-start | bytes 172040 | tf_op jit(solution)/shard_map/ppermute | solution.py:231
  16.4 0.0 collective-permute-done.5.refs_5_
  16.4 2.1 %collective-permute-start.12 = (bf16[32,896]{1,0:T(8,128)(2,1)S(1)}, bf16[32,896]{1,0:T(8,128)(2,1)S(1)}, u32[]{:S(2)}, u32[]{:S(2)}) collective-permute-start(bf16[32,896]{1,0:T(8,128)(2,1)S(1)} %get-tuple-element.54), channel_id=1, source_target_pairs={{0,8},{1,9},{2,10},{3,11},{4,12},{5,13},{6,14},{7,15},{8,0},{9,1},... | collective-permute-start | bytes 172040 | tf_op jit(solution)/shard_map/ppermute | solution.py:231
  18.6 0.0 collective-permute-done.6.refs_6_
  18.6 1.1 %collective-permute-start.13 = (bf16[32,896]{1,0:T(8,128)(2,1)S(1)}, bf16[32,896]{1,0:T(8,128)(2,1)S(1)}, u32[]{:S(2)}, u32[]{:S(2)}) collective-permute-start(bf16[32,896]{1,0:T(8,128)(2,1)S(1)} %get-tuple-element.55), channel_id=1, source_target_pairs={{0,10},{1,11},{2,8},{3,9},{4,14},{5,15},{6,12},{7,13},{8,2},{9,3},... | collective-permute-start | bytes 172040 | tf_op jit(solution)/shard_map/ppermute | solution.py:231
  19.7 0.1 collective-permute-done.7.refs_7_
  19.8 3.1 %collective-permute-start.14 = (bf16[32,896]{1,0:T(8,128)(2,1)S(1)}, bf16[32,896]{1,0:T(8,128)(2,1)S(1)}, u32[]{:S(2)}, u32[]{:S(2)}) collective-permute-start(bf16[32,896]{1,0:T(8,128)(2,1)S(1)} %get-tuple-element.56), channel_id=1, source_target_pairs={{0,12},{1,13},{2,14},{3,15},{4,8},{5,9},{6,10},{7,11},{8,4},{9,5},... | collective-permute-start | bytes 172040 | tf_op jit(solution)/shard_map/ppermute | solution.py:231
  22.9 0.0 collective-permute-done.10.refs_2_
  22.9 1.1 %collective-permute-start.15 = (bf16[32,896]{1,0:T(8,128)(2,1)S(1)}, bf16[32,896]{1,0:T(8,128)(2,1)S(1)}, u32[]{:S(2)}, u32[]{:S(2)}) collective-permute-start(bf16[32,896]{1,0:T(8,128)(2,1)S(1)} %get-tuple-element.57), channel_id=1, source_target_pairs={{0,14},{1,15},{2,12},{3,13},{4,10},{5,11},{6,8},{7,9},{8,6},{9,7},... | collective-permute-start | bytes 172040 | tf_op jit(solution)/shard_map/ppermute | solution.py:231
  24.1 0.0 collective-permute-done.11.refs_3_
  24.1 0.2 collective-permute-start.9
  24.3 0.5 shard_map.66
  24.7 0.0 collective-permute-done.12.refs_4_
  24.8 1.3 %collective-permute-start.16 = (bf16[128,1024]{1,0:T(8,128)(2,1)S(1)}, bf16[128,1024]{1,0:T(8,128)(2,1)S(1)}, u32[]{:S(2)}, u32[]{:S(2)}) collective-permute-start(bf16[128,1024]{1,0:T(8,128)(2,1)S(1)} %get-tuple-element.47.left_ref), channel_id=1, source_target_pairs={{0,16},{16,0},{1,17},{17,1},{2,18},{18,2},{3,19},{19,3},{4,20},{20... | collective-permute-start | bytes 786440 | tf_op jit(solution)/shard_map/ppermute | solution.py:305
  26.1 0.0 collective-permute-done.13.refs_5_
  26.1 0.0 collective-permute-done.14.refs_6_
  26.1 3.1 %collective-permute-done.15.refs_7_ = bf16[32,896]{1,0:T(8,128)(2,1)S(1)} collective-permute-done((bf16[32,896]{1,0:T(8,128)(2,1)S(1)}, bf16[32,896]{1,0:T(8,128)(2,1)S(1)}, u32[]{:S(2)}, u32[]{:S(2)}) %collective-permute-start.15) | collective-permute-done | bytes 57376 | tf_op jit(solution)/shard_map/ppermute | solution.py:231
  29.2 0.0 collective-permute-done.9.refs_1_
  29.2 0.2 shard_map.68.right_ref
  29.4 1.3 %collective-permute-start.17 = (bf16[128,896]{1,0:T(8,128)(2,1)S(1)}, bf16[128,896]{1,0:T(8,128)(2,1)S(1)}, u32[]{:S(2)}, u32[]{:S(2)}) collective-permute-start(bf16[128,896]{1,0:T(8,128)(2,1)S(1)} %shard_map.68.right_ref), channel_id=1, source_target_pairs={{0,16},{16,0},{1,17},{17,1},{2,18},{18,2},{3,19},{19,3},{4,20},{20... | collective-permute-start | bytes 688136 | tf_op jit(solution)/shard_map/ppermute | solution.py:323
  30.7 5.5 %shard_map.69 = (bf16[2048,1920]{1,0:T(8,128)(2,1)S(1)}, bf16[2048,1920]{1,0:T(8,128)(2,1)S(1)}) custom-call(bf16[2048,1920]{1,0:T(8,128)(2,1)} %bitcast.7, bf16[2048,1920]{1,0:T(8,128)(2,1)} %bitcast.8, bf16[128,256]{1,0:T(8,128)(2,1)S(1)} %get-tuple-element.58.refs_8_._.refs_5_), custom_call_target="tpu_custom_call" | custom-call | bytes 31457280 | tf_op jit(solution)/shard_map/pallas_call | solution.py:26
  36.2 0.0 collective-permute-done.16.left_ref
  36.2 0.6 collective-permute-done.17.right_ref
  36.8 3.7 %shard_map.71 = (bf16[128,1536]{1,0:T(8,128)(2,1)S(1)}, bf16[128,2048]{1,0:T(8,128)(2,1)S(1)}) custom-call(bf16[128,1024]{1,0:T(8,128)(2,1)S(1)} %collective-permute-done.16.left_ref, bf16[128,896]{1,0:T(8,128)(2,1)S(1)} %collective-permute-done.17.right_ref, f32[1,1920]{1,0:T(1,128)S(1)} %get-tuple-element.59.gain_ref, ...), custom_call_target="tpu_custom_call" | custom-call | flops 3019898880 | bytes 983040 | tf_op jit(solution)/shard_map/pallas_call | solution.py:26
  40.5 1.3 %collective-permute-start.18 = (bf16[128,1536]{1,0:T(8,128)(2,1)S(1)}, bf16[128,1536]{1,0:T(8,128)(2,1)S(1)}, u32[]{:S(2)}, u32[]{:S(2)}) collective-permute-start(bf16[128,1536]{1,0:T(8,128)(2,1)S(1)} %get-tuple-element.64), channel_id=1, source_target_pairs={{16,0},{0,16},{17,1},{1,17},{18,2},{2,18},{19,3},{3,19},{20,4},{4,... | collective-permute-start | bytes 1179656 | tf_op jit(solution)/shard_map/ppermute | solution.py:344
  41.8 0.4 shard_map.72
  42.3 0.3 collective-permute-start.19
  42.5 0.0 copy-start
  42.5 4.0 %shard_map.70 = (bf16[128,1536]{1,0:T(8,128)(2,1)S(1)}, bf16[128,384]{1,0:T(8,128)(2,1)S(1)}, f32[128,128]{1,0:T(8,128)S(1)}) custom-call(bf16[128,1024]{1,0:T(8,128)(2,1)S(1)} %get-tuple-element.47.left_ref, bf16[128,896]{1,0:T(8,128)(2,1)S(1)} %shard_map.68.right_ref, f32[1,1920]{1,0:T(1,128)S(1)} %get-tuple-element.59.gain_ref, ...), custom_call_target="tpu_custom_call" | custom-call | flops 4026531840 | bytes 983040 | tf_op jit(solution)/shard_map/pallas_call | solution.py:26
  46.6 3.2 %collective-permute-done.19.refs_3_ = bf16[128,384]{1,0:T(8,128)(2,1)S(1)} collective-permute-done((bf16[128,384]{1,0:T(8,128)(2,1)S(1)}, bf16[128,384]{1,0:T(8,128)(2,1)S(1)}, u32[]{:S(2)}, u32[]{:S(2)}) %collective-permute-start.19) | collective-permute-done | bytes 98336 | tf_op jit(solution)/shard_map/ppermute | solution.py:352
  49.8 0.0 collective-permute-done.18.refs_1_
  49.8 0.5 shard_map.73
  50.3 31.7 %all_to_all.11 = bf16[16,16,1920]{2,1,0:T(8,128)(2,1)S(1)} all-to-all(bf16[16,16,1920]{2,1,0:T(8,128)(2,1)S(1)} %bitcast.5), channel_id=1, replica_groups=mesh['dp'=2,'expert'=16] {'expert'}, dimensions={0} | all-to-all | bytes 1966080 | tf_op jit(solution)/shard_map/all_to_all | solution.py:256
  82.0 0.0 copy-done
  82.0 1.1 %shard_map.74 = bf16[128,1920]{1,0:T(8,128)(2,1)} custom-call(bf16[128,1920]{1,0:T(8,128)(2,1)S(1)} %copy-done, bf16[256,1920]{1,0:T(8,128)(2,1)S(1)} %bitcast.6, bf16[256,128]{1,0:T(8,128)(2,1)S(1)} %get-tuple-element.68.place_ref), custom_call_target="tpu_custom_call" | custom-call | flops 125829120 | bytes 1966080 | tf_op jit(solution)/shard_map/pallas_call | solution.py:26
  (2 shorter events, 0.1 us)
Async XLA Ops:
  1.5 1.6 %collective-permute-start = (bf16[128,1024]{1,0:T(8,128)(2,1)S(1)}, bf16[128,1024]{1,0:T(8,128)(2,1)S(1)}, u32[]{:S(2)}, u32[]{:S(2)}) collective-permute-start(bf16[128,1024]{1,0:T(8,128)(2,1)S(1)} %get-tuple-element.38), channel_id=1, source_target_pairs={{0,1},{1,0},{2,3},{3,2},{4,5},{5,4},{6,7},{7,6},{8,9},{9,8},{10,11... | collective-permute-start | bytes 786440 | tf_op jit(solution)/shard_map/ppermute | solution.py:231
  1.6 7.7 %collective-permute-start.8 = (bf16[128,896]{1,0:T(8,128)(2,1)S(1)}, bf16[128,896]{1,0:T(8,128)(2,1)S(1)}, u32[]{:S(2)}, u32[]{:S(2)}) collective-permute-start(bf16[128,896]{1,0:T(8,128)(2,1)S(1)} %get-tuple-element.49), channel_id=1, source_target_pairs={{0,1},{1,0},{2,3},{3,2},{4,5},{5,4},{6,7},{7,6},{8,9},{9,8},{10,11... | collective-permute-start | bytes 688136 | tf_op jit(solution)/shard_map/ppermute | solution.py:231
  3.2 7.2 %collective-permute-start.4 = (bf16[32,1024]{1,0:T(8,128)(2,1)S(1)}, bf16[32,1024]{1,0:T(8,128)(2,1)S(1)}, u32[]{:S(2)}, u32[]{:S(2)}) collective-permute-start(bf16[32,1024]{1,0:T(8,128)(2,1)S(1)} %get-tuple-element.43), channel_id=1, source_target_pairs={{0,8},{1,9},{2,10},{3,11},{4,12},{5,13},{6,14},{7,15},{8,0},{9,1},... | collective-permute-start | bytes 196616 | tf_op jit(solution)/shard_map/ppermute | solution.py:231
  6.7 7.2 %collective-permute-start.1 = (bf16[32,1024]{1,0:T(8,128)(2,1)S(1)}, bf16[32,1024]{1,0:T(8,128)(2,1)S(1)}, u32[]{:S(2)}, u32[]{:S(2)}) collective-permute-start(bf16[32,1024]{1,0:T(8,128)(2,1)S(1)} %get-tuple-element.40), channel_id=1, source_target_pairs={{0,2},{1,3},{2,0},{3,1},{4,6},{5,7},{6,4},{7,5},{8,10},{9,11},{10,... | collective-permute-start | bytes 196616 | tf_op jit(solution)/shard_map/ppermute | solution.py:231
  7.9 7.0 %collective-permute-start.2 = (bf16[32,1024]{1,0:T(8,128)(2,1)S(1)}, bf16[32,1024]{1,0:T(8,128)(2,1)S(1)}, u32[]{:S(2)}, u32[]{:S(2)}) collective-permute-start(bf16[32,1024]{1,0:T(8,128)(2,1)S(1)} %get-tuple-element.41), channel_id=1, source_target_pairs={{0,4},{1,5},{2,6},{3,7},{4,0},{5,1},{6,2},{7,3},{8,12},{9,13},{10,... | collective-permute-start | bytes 196616 | tf_op jit(solution)/shard_map/ppermute | solution.py:231
  9.2 5.8 %collective-permute-start.3 = (bf16[32,1024]{1,0:T(8,128)(2,1)S(1)}, bf16[32,1024]{1,0:T(8,128)(2,1)S(1)}, u32[]{:S(2)}, u32[]{:S(2)}) collective-permute-start(bf16[32,1024]{1,0:T(8,128)(2,1)S(1)} %get-tuple-element.42), channel_id=1, source_target_pairs={{0,6},{1,7},{2,4},{3,5},{4,2},{5,3},{6,0},{7,1},{8,14},{9,15},{10,... | collective-permute-start | bytes 196616 | tf_op jit(solution)/shard_map/ppermute | solution.py:231
  9.3 7.1 %collective-permute-start.5 = (bf16[32,1024]{1,0:T(8,128)(2,1)S(1)}, bf16[32,1024]{1,0:T(8,128)(2,1)S(1)}, u32[]{:S(2)}, u32[]{:S(2)}) collective-permute-start(bf16[32,1024]{1,0:T(8,128)(2,1)S(1)} %get-tuple-element.44), channel_id=1, source_target_pairs={{0,10},{1,11},{2,8},{3,9},{4,14},{5,15},{6,12},{7,13},{8,2},{9,3},... | collective-permute-start | bytes 196616 | tf_op jit(solution)/shard_map/ppermute | solution.py:231
  10.3 8.2 %collective-permute-start.6 = (bf16[32,1024]{1,0:T(8,128)(2,1)S(1)}, bf16[32,1024]{1,0:T(8,128)(2,1)S(1)}, u32[]{:S(2)}, u32[]{:S(2)}) collective-permute-start(bf16[32,1024]{1,0:T(8,128)(2,1)S(1)} %get-tuple-element.45), channel_id=1, source_target_pairs={{0,12},{1,13},{2,14},{3,15},{4,8},{5,9},{6,10},{7,11},{8,4},{9,5},... | collective-permute-start | bytes 196616 | tf_op jit(solution)/shard_map/ppermute | solution.py:231
  13.9 5.9 %collective-permute-start.7 = (bf16[32,1024]{1,0:T(8,128)(2,1)S(1)}, bf16[32,1024]{1,0:T(8,128)(2,1)S(1)}, u32[]{:S(2)}, u32[]{:S(2)}) collective-permute-start(bf16[32,1024]{1,0:T(8,128)(2,1)S(1)} %get-tuple-element.46), channel_id=1, source_target_pairs={{0,14},{1,15},{2,12},{3,13},{4,10},{5,11},{6,8},{7,9},{8,6},{9,7},... | collective-permute-start | bytes 196616 | tf_op jit(solution)/shard_map/ppermute | solution.py:231
  14.9 8.1 %collective-permute-start.10 = (bf16[32,896]{1,0:T(8,128)(2,1)S(1)}, bf16[32,896]{1,0:T(8,128)(2,1)S(1)}, u32[]{:S(2)}, u32[]{:S(2)}) collective-permute-start(bf16[32,896]{1,0:T(8,128)(2,1)S(1)} %get-tuple-element.52), channel_id=1, source_target_pairs={{0,4},{1,5},{2,6},{3,7},{4,0},{5,1},{6,2},{7,3},{8,12},{9,13},{10,... | collective-permute-start | bytes 172040 | tf_op jit(solution)/shard_map/ppermute | solution.py:231
  15.0 9.1 %collective-permute-start.11 = (bf16[32,896]{1,0:T(8,128)(2,1)S(1)}, bf16[32,896]{1,0:T(8,128)(2,1)S(1)}, u32[]{:S(2)}, u32[]{:S(2)}) collective-permute-start(bf16[32,896]{1,0:T(8,128)(2,1)S(1)} %get-tuple-element.53), channel_id=1, source_target_pairs={{0,6},{1,7},{2,4},{3,5},{4,2},{5,3},{6,0},{7,1},{8,14},{9,15},{10,... | collective-permute-start | bytes 172040 | tf_op jit(solution)/shard_map/ppermute | solution.py:231
  16.4 8.3 %collective-permute-start.12 = (bf16[32,896]{1,0:T(8,128)(2,1)S(1)}, bf16[32,896]{1,0:T(8,128)(2,1)S(1)}, u32[]{:S(2)}, u32[]{:S(2)}) collective-permute-start(bf16[32,896]{1,0:T(8,128)(2,1)S(1)} %get-tuple-element.54), channel_id=1, source_target_pairs={{0,8},{1,9},{2,10},{3,11},{4,12},{5,13},{6,14},{7,15},{8,0},{9,1},... | collective-permute-start | bytes 172040 | tf_op jit(solution)/shard_map/ppermute | solution.py:231
  18.6 7.5 %collective-permute-start.13 = (bf16[32,896]{1,0:T(8,128)(2,1)S(1)}, bf16[32,896]{1,0:T(8,128)(2,1)S(1)}, u32[]{:S(2)}, u32[]{:S(2)}) collective-permute-start(bf16[32,896]{1,0:T(8,128)(2,1)S(1)} %get-tuple-element.55), channel_id=1, source_target_pairs={{0,10},{1,11},{2,8},{3,9},{4,14},{5,15},{6,12},{7,13},{8,2},{9,3},... | collective-permute-start | bytes 172040 | tf_op jit(solution)/shard_map/ppermute | solution.py:231
  19.8 6.3 %collective-permute-start.14 = (bf16[32,896]{1,0:T(8,128)(2,1)S(1)}, bf16[32,896]{1,0:T(8,128)(2,1)S(1)}, u32[]{:S(2)}, u32[]{:S(2)}) collective-permute-start(bf16[32,896]{1,0:T(8,128)(2,1)S(1)} %get-tuple-element.56), channel_id=1, source_target_pairs={{0,12},{1,13},{2,14},{3,15},{4,8},{5,9},{6,10},{7,11},{8,4},{9,5},... | collective-permute-start | bytes 172040 | tf_op jit(solution)/shard_map/ppermute | solution.py:231
  22.9 6.2 %collective-permute-start.15 = (bf16[32,896]{1,0:T(8,128)(2,1)S(1)}, bf16[32,896]{1,0:T(8,128)(2,1)S(1)}, u32[]{:S(2)}, u32[]{:S(2)}) collective-permute-start(bf16[32,896]{1,0:T(8,128)(2,1)S(1)} %get-tuple-element.57), channel_id=1, source_target_pairs={{0,14},{1,15},{2,12},{3,13},{4,10},{5,11},{6,8},{7,9},{8,6},{9,7},... | collective-permute-start | bytes 172040 | tf_op jit(solution)/shard_map/ppermute | solution.py:231
  24.1 5.1 %collective-permute-start.9 = (bf16[32,896]{1,0:T(8,128)(2,1)S(1)}, bf16[32,896]{1,0:T(8,128)(2,1)S(1)}, u32[]{:S(2)}, u32[]{:S(2)}) collective-permute-start(bf16[32,896]{1,0:T(8,128)(2,1)S(1)} %get-tuple-element.51), channel_id=1, source_target_pairs={{0,2},{1,3},{2,0},{3,1},{4,6},{5,7},{6,4},{7,5},{8,10},{9,11},{10,... | collective-permute-start | bytes 172040 | tf_op jit(solution)/shard_map/ppermute | solution.py:231
  24.8 11.5 %collective-permute-start.16 = (bf16[128,1024]{1,0:T(8,128)(2,1)S(1)}, bf16[128,1024]{1,0:T(8,128)(2,1)S(1)}, u32[]{:S(2)}, u32[]{:S(2)}) collective-permute-start(bf16[128,1024]{1,0:T(8,128)(2,1)S(1)} %get-tuple-element.47.left_ref), channel_id=1, source_target_pairs={{0,16},{16,0},{1,17},{17,1},{2,18},{18,2},{3,19},{19,3},{4,20},{20... | collective-permute-start | bytes 786440 | tf_op jit(solution)/shard_map/ppermute | solution.py:305
  29.4 7.4 %collective-permute-start.17 = (bf16[128,896]{1,0:T(8,128)(2,1)S(1)}, bf16[128,896]{1,0:T(8,128)(2,1)S(1)}, u32[]{:S(2)}, u32[]{:S(2)}) collective-permute-start(bf16[128,896]{1,0:T(8,128)(2,1)S(1)} %shard_map.68.right_ref), channel_id=1, source_target_pairs={{0,16},{16,0},{1,17},{17,1},{2,18},{18,2},{3,19},{19,3},{4,20},{20... | collective-permute-start | bytes 688136 | tf_op jit(solution)/shard_map/ppermute | solution.py:323
  40.5 9.3 %collective-permute-start.18 = (bf16[128,1536]{1,0:T(8,128)(2,1)S(1)}, bf16[128,1536]{1,0:T(8,128)(2,1)S(1)}, u32[]{:S(2)}, u32[]{:S(2)}) collective-permute-start(bf16[128,1536]{1,0:T(8,128)(2,1)S(1)} %get-tuple-element.64), channel_id=1, source_target_pairs={{16,0},{0,16},{17,1},{1,17},{18,2},{2,18},{19,3},{3,19},{20,4},{4,... | collective-permute-start | bytes 1179656 | tf_op jit(solution)/shard_map/ppermute | solution.py:344
  42.3 7.5 %collective-permute-start.19 = (bf16[128,384]{1,0:T(8,128)(2,1)S(1)}, bf16[128,384]{1,0:T(8,128)(2,1)S(1)}, u32[]{:S(2)}, u32[]{:S(2)}) collective-permute-start(bf16[128,384]{1,0:T(8,128)(2,1)S(1)} %shard_map.72), channel_id=1, source_target_pairs={{16,0},{0,16},{17,1},{1,17},{18,2},{2,18},{19,3},{3,19},{20,4},{4,... | collective-permute-start | bytes 294920 | tf_op jit(solution)/shard_map/ppermute | solution.py:352
  42.5 39.4 %copy-start = (bf16[128,1920]{1,0:T(8,128)(2,1)S(1)}, bf16[128,1920]{1,0:T(8,128)(2,1)}, u32[]{:S(2)}) copy-start(bf16[128,1920]{1,0:T(8,128)(2,1)} %tokens_ref.1) | copy-start | bytes 1474564

commit v5 on v4

--- a/solution.py
+++ b/solution.py
@@ -82,14 +82,14 @@
 
 
 def pack_kernel(targets, experts, capacity, cut, *refs):
-    assign_ref, tokens_ref, gain_ref, centroid_ref = refs[:4]
-    halves = refs[4 : 4 + targets], refs[4 + targets : 4 + 2 * targets]
-    place_ref, gain_out, centroid_out, assign_buf, tokens_buf, sems = refs[4 + 2 * targets :]
+    assign_ref, tokens_ref, gain_ref = refs[:3]
+    halves = refs[3 : 3 + targets], refs[3 + targets : 3 + 2 * targets]
+    place_ref, gain_out, assign_buf, tokens_buf, sems = refs[3 + 2 * targets :]
     tok_count = tokens_ref.shape[0]
     slot_total = place_ref.shape[0]
     get_assign, *others = fetch(
-        (assign_ref, tokens_ref, gain_ref, centroid_ref),
-        (assign_buf, tokens_buf, gain_out, centroid_out),
+        (assign_ref, tokens_ref, gain_ref),
+        (assign_buf, tokens_buf, gain_out),
         sems,
     )
     get_assign.wait()
@@ -270,22 +270,21 @@
     back_widths = (back_cut, features - back_cut)
     move_flops = slot_total * tok_count * features
     half_bytes = 2 * slot_total * features
-    *packed, place, gain, centroid = call(
+    *packed, place, gain = call(
         functools.partial(pack_kernel, targets, experts, capacity, cut),
         [shape(slot_total // targets, w) for w in widths for _ in range(targets)]
         + [
             shape(slot_total, tok_count),
             pltpu.VMEM((1, features), F32),
-            pltpu.VMEM((1, features), BF16),
         ],
-        [stay(a) for a in (assignment.reshape(1, tok_count), tokens, norm_gain, centroids)],
+        [stay(a) for a in (assignment.reshape(1, tok_count), tokens, norm_gain)],
         2 * move_flops,
         2 * half_bytes,
-        [FAR] * 4,
+        [FAR] * 3,
         [
             pltpu.VMEM((1, tok_count), jnp.int32),
             pltpu.VMEM((tok_count, features), BF16),
-            pltpu.SemaphoreType.DMA((4,)),
+            pltpu.SemaphoreType.DMA((3,)),
         ],
     )
     if targets == 2:
@@ -326,7 +325,7 @@
     own_left, own_right, gate = call(
         own_kernel,
         [shape(tok_count, w) for w in back_widths] + [shape(tok_count, 128, dtype=F32)],
-        [rows, right_rows, gain, centroid, inner, outer],
+        [rows, right_rows, gain, centroids, inner, outer],
         ffn_flops,
         half_bytes,
         scratch=wide + [pltpu.VMEM((tok_count, units), BF16)],

time: 83.3 us -> 83.3 us (level)
  no operation moved by 1% of the time
where the time goes in v5:
time: 83.3 us; the launch traced here: 83.1 us
  blocking collectives  31.6 us (38%)
  starting transfers between devices  25.7 us (31%)
  Pallas kernels  17.6 us (21%)
  waiting for transfers between devices  8.04 us (10%)
    all_to_all x1, blocking collectives, together(): lax.all_to_all(rows, 'expert', split_axis=0, concat_axis=0, tiled=True)  31.6 us
    ppermute x16, starting transfers between devices, swap(): lax.ppermute(array, 'expert', [(i, i ^ axis_mask) for i in range(experts)])  21.5 us
    pallas_call x11, Pallas kernels, call(): pl.pallas_call(kernel, out_shape=tuple(outs), in_specs=[LOCAL] * len(args...  17.6 us
    ppermute x16, waiting for transfers between devices, swap(): lax.ppermute(array, 'expert', [(i, i ^ axis_mask) for i in range(experts)])  4.28 us
    ppermute x1, waiting for transfers between devices, body(): right_parts.append(lax.ppermute(right_part, 'dp', back[k]))  3.18 us
  transfers between devices with their start and end apart: 20, of which 5 were waited for; matrix products, arithmetic and copies ran while one was open for 0% of the time, Pallas kernels for 13%

profile of v5, /device:TPU:1, one launch (start us, length us, event | category | flops | bytes accessed | tf_op | source)
XLA Modules:
  0.0 83.1 jit_solution(3190868488504100244)
XLA Ops:
  0.0 1.5 %shard_map.64 = (bf16[128,1024]{1,0:T(8,128)(2,1)S(1)}, bf16[128,1024]{1,0:T(8,128)(2,1)S(1)}, bf16[128,896]{1,0:T(8,128)(2,1)S(1)}, bf16[128,896]{1,0:T(8,128)(...) custom-call(s32[1,128]{1,0:T(1,128)} %bitcast.9, bf16[128,1920]{1,0:T(8,128)(2,1)} %tokens_ref.1, ...), custom_call_target="tpu_custom_call" | custom-call | flops 125829120 | bytes 1966080 | tf_op jit(solution)/shard_map/pallas_call | solution.py:26
  1.5 0.1 collective-permute-start
  1.6 0.5 collective-permute-start.8
  2.1 1.0 %collective-permute-done.crossed_ref = bf16[128,1024]{1,0:T(8,128)(2,1)S(1)} collective-permute-done((bf16[128,1024]{1,0:T(8,128)(2,1)S(1)}, bf16[128,1024]{1,0:T(8,128)(2,1)S(1)}, u32[]{:S(2)}, u32[]{:S(2)}) %collective-permute-start) | collective-permute-done | bytes 262176 | tf_op jit(solution)/shard_map/ppermute | solution.py:231
  3.1 3.5 %collective-permute-start.4 = (bf16[32,1024]{1,0:T(8,128)(2,1)S(1)}, bf16[32,1024]{1,0:T(8,128)(2,1)S(1)}, u32[]{:S(2)}, u32[]{:S(2)}) collective-permute-start(bf16[32,1024]{1,0:T(8,128)(2,1)S(1)} %get-tuple-element.42), channel_id=1, source_target_pairs={{0,8},{1,9},{2,10},{3,11},{4,12},{5,13},{6,14},{7,15},{8,0},{9,1},... | collective-permute-start | bytes 196616 | tf_op jit(solution)/shard_map/ppermute | solution.py:231
  6.6 1.2 %collective-permute-start.1 = (bf16[32,1024]{1,0:T(8,128)(2,1)S(1)}, bf16[32,1024]{1,0:T(8,128)(2,1)S(1)}, u32[]{:S(2)}, u32[]{:S(2)}) collective-permute-start(bf16[32,1024]{1,0:T(8,128)(2,1)S(1)} %get-tuple-element.39), channel_id=1, source_target_pairs={{0,2},{1,3},{2,0},{3,1},{4,6},{5,7},{6,4},{7,5},{8,10},{9,11},{10,... | collective-permute-start | bytes 196616 | tf_op jit(solution)/shard_map/ppermute | solution.py:231
  7.9 1.3 %collective-permute-start.2 = (bf16[32,1024]{1,0:T(8,128)(2,1)S(1)}, bf16[32,1024]{1,0:T(8,128)(2,1)S(1)}, u32[]{:S(2)}, u32[]{:S(2)}) collective-permute-start(bf16[32,1024]{1,0:T(8,128)(2,1)S(1)} %get-tuple-element.40), channel_id=1, source_target_pairs={{0,4},{1,5},{2,6},{3,7},{4,0},{5,1},{6,2},{7,3},{8,12},{9,13},{10,... | collective-permute-start | bytes 196616 | tf_op jit(solution)/shard_map/ppermute | solution.py:231
  9.2 0.1 collective-permute-start.3
  9.3 0.0 collective-permute-done.8.crossed_ref
  9.3 1.0 %collective-permute-start.5 = (bf16[32,1024]{1,0:T(8,128)(2,1)S(1)}, bf16[32,1024]{1,0:T(8,128)(2,1)S(1)}, u32[]{:S(2)}, u32[]{:S(2)}) collective-permute-start(bf16[32,1024]{1,0:T(8,128)(2,1)S(1)} %get-tuple-element.43), channel_id=1, source_target_pairs={{0,10},{1,11},{2,8},{3,9},{4,14},{5,15},{6,12},{7,13},{8,2},{9,3},... | collective-permute-start | bytes 196616 | tf_op jit(solution)/shard_map/ppermute | solution.py:231
  10.3 0.0 collective-permute-done.4.refs_4_._
  10.3 3.6 %collective-permute-start.6 = (bf16[32,1024]{1,0:T(8,128)(2,1)S(1)}, bf16[32,1024]{1,0:T(8,128)(2,1)S(1)}, u32[]{:S(2)}, u32[]{:S(2)}) collective-permute-start(bf16[32,1024]{1,0:T(8,128)(2,1)S(1)} %get-tuple-element.44), channel_id=1, source_target_pairs={{0,12},{1,13},{2,14},{3,15},{4,8},{5,9},{6,10},{7,11},{8,4},{9,5},... | collective-permute-start | bytes 196616 | tf_op jit(solution)/shard_map/ppermute | solution.py:231
  13.9 0.0 collective-permute-done.1.refs_1_
  13.9 0.9 %collective-permute-start.7 = (bf16[32,1024]{1,0:T(8,128)(2,1)S(1)}, bf16[32,1024]{1,0:T(8,128)(2,1)S(1)}, u32[]{:S(2)}, u32[]{:S(2)}) collective-permute-start(bf16[32,1024]{1,0:T(8,128)(2,1)S(1)} %get-tuple-element.45), channel_id=1, source_target_pairs={{0,14},{1,15},{2,12},{3,13},{4,10},{5,11},{6,8},{7,9},{8,6},{9,7},... | collective-permute-start | bytes 196616 | tf_op jit(solution)/shard_map/ppermute | solution.py:231
  14.9 0.0 collective-permute-done.2.refs_2_
  14.9 0.1 collective-permute-start.10
  14.9 0.0 collective-permute-done.3.refs_3_
  15.0 1.4 %collective-permute-start.11 = (bf16[32,896]{1,0:T(8,128)(2,1)S(1)}, bf16[32,896]{1,0:T(8,128)(2,1)S(1)}, u32[]{:S(2)}, u32[]{:S(2)}) collective-permute-start(bf16[32,896]{1,0:T(8,128)(2,1)S(1)} %get-tuple-element.52), channel_id=1, source_target_pairs={{0,6},{1,7},{2,4},{3,5},{4,2},{5,3},{6,0},{7,1},{8,14},{9,15},{10,... | collective-permute-start | bytes 172040 | tf_op jit(solution)/shard_map/ppermute | solution.py:231
  16.4 0.0 collective-permute-done.5.refs_5_
  16.4 2.1 %collective-permute-start.12 = (bf16[32,896]{1,0:T(8,128)(2,1)S(1)}, bf16[32,896]{1,0:T(8,128)(2,1)S(1)}, u32[]{:S(2)}, u32[]{:S(2)}) collective-permute-start(bf16[32,896]{1,0:T(8,128)(2,1)S(1)} %get-tuple-element.53), channel_id=1, source_target_pairs={{0,8},{1,9},{2,10},{3,11},{4,12},{5,13},{6,14},{7,15},{8,0},{9,1},... | collective-permute-start | bytes 172040 | tf_op jit(solution)/shard_map/ppermute | solution.py:231
  18.6 0.0 collective-permute-done.6.refs_6_
  18.6 1.1 %collective-permute-start.13 = (bf16[32,896]{1,0:T(8,128)(2,1)S(1)}, bf16[32,896]{1,0:T(8,128)(2,1)S(1)}, u32[]{:S(2)}, u32[]{:S(2)}) collective-permute-start(bf16[32,896]{1,0:T(8,128)(2,1)S(1)} %get-tuple-element.54), channel_id=1, source_target_pairs={{0,10},{1,11},{2,8},{3,9},{4,14},{5,15},{6,12},{7,13},{8,2},{9,3},... | collective-permute-start | bytes 172040 | tf_op jit(solution)/shard_map/ppermute | solution.py:231
  19.7 0.1 collective-permute-done.7.refs_7_
  19.8 3.1 %collective-permute-start.14 = (bf16[32,896]{1,0:T(8,128)(2,1)S(1)}, bf16[32,896]{1,0:T(8,128)(2,1)S(1)}, u32[]{:S(2)}, u32[]{:S(2)}) collective-permute-start(bf16[32,896]{1,0:T(8,128)(2,1)S(1)} %get-tuple-element.55), channel_id=1, source_target_pairs={{0,12},{1,13},{2,14},{3,15},{4,8},{5,9},{6,10},{7,11},{8,4},{9,5},... | collective-permute-start | bytes 172040 | tf_op jit(solution)/shard_map/ppermute | solution.py:231
  22.9 0.0 collective-permute-done.10.refs_2_
  22.9 1.1 %collective-permute-start.15 = (bf16[32,896]{1,0:T(8,128)(2,1)S(1)}, bf16[32,896]{1,0:T(8,128)(2,1)S(1)}, u32[]{:S(2)}, u32[]{:S(2)}) collective-permute-start(bf16[32,896]{1,0:T(8,128)(2,1)S(1)} %get-tuple-element.56), channel_id=1, source_target_pairs={{0,14},{1,15},{2,12},{3,13},{4,10},{5,11},{6,8},{7,9},{8,6},{9,7},... | collective-permute-start | bytes 172040 | tf_op jit(solution)/shard_map/ppermute | solution.py:231
  24.1 0.0 collective-permute-done.11.refs_3_
  24.1 0.2 collective-permute-start.9
  24.2 0.5 shard_map.66
  24.7 0.0 collective-permute-done.12.refs_4_
  24.7 1.3 %collective-permute-start.16 = (bf16[128,1024]{1,0:T(8,128)(2,1)S(1)}, bf16[128,1024]{1,0:T(8,128)(2,1)S(1)}, u32[]{:S(2)}, u32[]{:S(2)}) collective-permute-start(bf16[128,1024]{1,0:T(8,128)(2,1)S(1)} %get-tuple-element.46.left_ref), channel_id=1, source_target_pairs={{0,16},{16,0},{1,17},{17,1},{2,18},{18,2},{3,19},{19,3},{4,20},{20... | collective-permute-start | bytes 786440 | tf_op jit(solution)/shard_map/ppermute | solution.py:304
  26.1 0.0 collective-permute-done.13.refs_5_
  26.1 0.0 collective-permute-done.14.refs_6_
  26.1 3.1 %collective-permute-done.15.refs_7_ = bf16[32,896]{1,0:T(8,128)(2,1)S(1)} collective-permute-done((bf16[32,896]{1,0:T(8,128)(2,1)S(1)}, bf16[32,896]{1,0:T(8,128)(2,1)S(1)}, u32[]{:S(2)}, u32[]{:S(2)}) %collective-permute-start.15) | collective-permute-done | bytes 57376 | tf_op jit(solution)/shard_map/ppermute | solution.py:231
  29.2 0.0 collective-permute-done.9.refs_1_
  29.2 0.2 shard_map.68.right_ref
  29.4 1.3 %collective-permute-start.17 = (bf16[128,896]{1,0:T(8,128)(2,1)S(1)}, bf16[128,896]{1,0:T(8,128)(2,1)S(1)}, u32[]{:S(2)}, u32[]{:S(2)}) collective-permute-start(bf16[128,896]{1,0:T(8,128)(2,1)S(1)} %shard_map.68.right_ref), channel_id=1, source_target_pairs={{0,16},{16,0},{1,17},{17,1},{2,18},{18,2},{3,19},{19,3},{4,20},{20... | collective-permute-start | bytes 688136 | tf_op jit(solution)/shard_map/ppermute | solution.py:322
  30.7 5.5 %shard_map.69 = (bf16[2048,1920]{1,0:T(8,128)(2,1)S(1)}, bf16[2048,1920]{1,0:T(8,128)(2,1)S(1)}) custom-call(bf16[2048,1920]{1,0:T(8,128)(2,1)} %bitcast.7, bf16[2048,1920]{1,0:T(8,128)(2,1)} %bitcast.8, bf16[128,256]{1,0:T(8,128)(2,1)S(1)} %get-tuple-element.57.refs_8_._.refs_5_), custom_call_target="tpu_custom_call" | custom-call | bytes 31457280 | tf_op jit(solution)/shard_map/pallas_call | solution.py:26
  36.2 0.0 collective-permute-done.16.left_ref
  36.2 0.6 collective-permute-done.17.right_ref
  36.8 3.7 %shard_map.71 = (bf16[128,1536]{1,0:T(8,128)(2,1)S(1)}, bf16[128,2048]{1,0:T(8,128)(2,1)S(1)}) custom-call(bf16[128,1024]{1,0:T(8,128)(2,1)S(1)} %collective-permute-done.16.left_ref, bf16[128,896]{1,0:T(8,128)(2,1)S(1)} %collective-permute-done.17.right_ref, f32[1,1920]{1,0:T(1,128)S(1)} %get-tuple-element.58.gain_ref, ...), custom_call_target="tpu_custom_call" | custom-call | flops 3019898880 | bytes 983040 | tf_op jit(solution)/shard_map/pallas_call | solution.py:26
  40.5 0.0 copy-start.1
  40.5 1.3 %collective-permute-start.18 = (bf16[128,1536]{1,0:T(8,128)(2,1)S(1)}, bf16[128,1536]{1,0:T(8,128)(2,1)S(1)}, u32[]{:S(2)}, u32[]{:S(2)}) collective-permute-start(bf16[128,1536]{1,0:T(8,128)(2,1)S(1)} %get-tuple-element.62), channel_id=1, source_target_pairs={{16,0},{0,16},{17,1},{1,17},{18,2},{2,18},{19,3},{3,19},{20,4},{4,... | collective-permute-start | bytes 1179656 | tf_op jit(solution)/shard_map/ppermute | solution.py:343
  41.8 0.4 shard_map.72
  42.2 0.0 copy-start
  42.3 0.3 collective-permute-start.19
  42.6 0.0 copy-done.1
  42.6 4.0 %shard_map.70 = (bf16[128,1536]{1,0:T(8,128)(2,1)S(1)}, bf16[128,384]{1,0:T(8,128)(2,1)S(1)}, f32[128,128]{1,0:T(8,128)S(1)}) custom-call(bf16[128,1024]{1,0:T(8,128)(2,1)S(1)} %get-tuple-element.46.left_ref, bf16[128,896]{1,0:T(8,128)(2,1)S(1)} %shard_map.68.right_ref, f32[1,1920]{1,0:T(1,128)S(1)} %get-tuple-element.58.gain_ref, ...), custom_call_target="tpu_custom_call" | custom-call | flops 4026531840 | bytes 983040 | tf_op jit(solution)/shard_map/pallas_call | solution.py:26
  46.6 3.2 %collective-permute-done.19.refs_3_ = bf16[128,384]{1,0:T(8,128)(2,1)S(1)} collective-permute-done((bf16[128,384]{1,0:T(8,128)(2,1)S(1)}, bf16[128,384]{1,0:T(8,128)(2,1)S(1)}, u32[]{:S(2)}, u32[]{:S(2)}) %collective-permute-start.19) | collective-permute-done | bytes 98336 | tf_op jit(solution)/shard_map/ppermute | solution.py:351
  49.8 0.0 collective-permute-done.18.refs_1_
  49.8 0.5 shard_map.73
  50.3 31.6 %all_to_all.11 = bf16[16,16,1920]{2,1,0:T(8,128)(2,1)S(1)} all-to-all(bf16[16,16,1920]{2,1,0:T(8,128)(2,1)S(1)} %bitcast.5), channel_id=1, replica_groups=mesh['dp'=2,'expert'=16] {'expert'}, dimensions={0} | all-to-all | bytes 1966080 | tf_op jit(solution)/shard_map/all_to_all | solution.py:256
  82.0 0.0 copy-done
  82.0 1.1 %shard_map.74 = bf16[128,1920]{1,0:T(8,128)(2,1)} custom-call(bf16[128,1920]{1,0:T(8,128)(2,1)S(1)} %copy-done, bf16[256,1920]{1,0:T(8,128)(2,1)S(1)} %bitcast.6, bf16[256,128]{1,0:T(8,128)(2,1)S(1)} %get-tuple-element.66.place_ref), custom_call_target="tpu_custom_call" | custom-call | flops 125829120 | bytes 1966080 | tf_op jit(solution)/shard_map/pallas_call | solution.py:26
  (2 shorter events, 0.1 us)
Async XLA Ops:
  1.5 1.6 %collective-permute-start = (bf16[128,1024]{1,0:T(8,128)(2,1)S(1)}, bf16[128,1024]{1,0:T(8,128)(2,1)S(1)}, u32[]{:S(2)}, u32[]{:S(2)}) collective-permute-start(bf16[128,1024]{1,0:T(8,128)(2,1)S(1)} %get-tuple-element.37), channel_id=1, source_target_pairs={{0,1},{1,0},{2,3},{3,2},{4,5},{5,4},{6,7},{7,6},{8,9},{9,8},{10,11... | collective-permute-start | bytes 786440 | tf_op jit(solution)/shard_map/ppermute | solution.py:231
  1.6 7.7 %collective-permute-start.8 = (bf16[128,896]{1,0:T(8,128)(2,1)S(1)}, bf16[128,896]{1,0:T(8,128)(2,1)S(1)}, u32[]{:S(2)}, u32[]{:S(2)}) collective-permute-start(bf16[128,896]{1,0:T(8,128)(2,1)S(1)} %get-tuple-element.48), channel_id=1, source_target_pairs={{0,1},{1,0},{2,3},{3,2},{4,5},{5,4},{6,7},{7,6},{8,9},{9,8},{10,11... | collective-permute-start | bytes 688136 | tf_op jit(solution)/shard_map/ppermute | solution.py:231
  3.1 7.2 %collective-permute-start.4 = (bf16[32,1024]{1,0:T(8,128)(2,1)S(1)}, bf16[32,1024]{1,0:T(8,128)(2,1)S(1)}, u32[]{:S(2)}, u32[]{:S(2)}) collective-permute-start(bf16[32,1024]{1,0:T(8,128)(2,1)S(1)} %get-tuple-element.42), channel_id=1, source_target_pairs={{0,8},{1,9},{2,10},{3,11},{4,12},{5,13},{6,14},{7,15},{8,0},{9,1},... | collective-permute-start | bytes 196616 | tf_op jit(solution)/shard_map/ppermute | solution.py:231
  6.6 7.2 %collective-permute-start.1 = (bf16[32,1024]{1,0:T(8,128)(2,1)S(1)}, bf16[32,1024]{1,0:T(8,128)(2,1)S(1)}, u32[]{:S(2)}, u32[]{:S(2)}) collective-permute-start(bf16[32,1024]{1,0:T(8,128)(2,1)S(1)} %get-tuple-element.39), channel_id=1, source_target_pairs={{0,2},{1,3},{2,0},{3,1},{4,6},{5,7},{6,4},{7,5},{8,10},{9,11},{10,... | collective-permute-start | bytes 196616 | tf_op jit(solution)/shard_map/ppermute | solution.py:231
  7.9 7.0 %collective-permute-start.2 = (bf16[32,1024]{1,0:T(8,128)(2,1)S(1)}, bf16[32,1024]{1,0:T(8,128)(2,1)S(1)}, u32[]{:S(2)}, u32[]{:S(2)}) collective-permute-start(bf16[32,1024]{1,0:T(8,128)(2,1)S(1)} %get-tuple-element.40), channel_id=1, source_target_pairs={{0,4},{1,5},{2,6},{3,7},{4,0},{5,1},{6,2},{7,3},{8,12},{9,13},{10,... | collective-permute-start | bytes 196616 | tf_op jit(solution)/shard_map/ppermute | solution.py:231
  9.2 5.8 %collective-permute-start.3 = (bf16[32,1024]{1,0:T(8,128)(2,1)S(1)}, bf16[32,1024]{1,0:T(8,128)(2,1)S(1)}, u32[]{:S(2)}, u32[]{:S(2)}) collective-permute-start(bf16[32,1024]{1,0:T(8,128)(2,1)S(1)} %get-tuple-element.41), channel_id=1, source_target_pairs={{0,6},{1,7},{2,4},{3,5},{4,2},{5,3},{6,0},{7,1},{8,14},{9,15},{10,... | collective-permute-start | bytes 196616 | tf_op jit(solution)/shard_map/ppermute | solution.py:231
  9.3 7.1 %collective-permute-start.5 = (bf16[32,1024]{1,0:T(8,128)(2,1)S(1)}, bf16[32,1024]{1,0:T(8,128)(2,1)S(1)}, u32[]{:S(2)}, u32[]{:S(2)}) collective-permute-start(bf16[32,1024]{1,0:T(8,128)(2,1)S(1)} %get-tuple-element.43), channel_id=1, source_target_pairs={{0,10},{1,11},{2,8},{3,9},{4,14},{5,15},{6,12},{7,13},{8,2},{9,3},... | collective-permute-start | bytes 196616 | tf_op jit(solution)/shard_map/ppermute | solution.py:231
  10.3 8.2 %collective-permute-start.6 = (bf16[32,1024]{1,0:T(8,128)(2,1)S(1)}, bf16[32,1024]{1,0:T(8,128)(2,1)S(1)}, u32[]{:S(2)}, u32[]{:S(2)}) collective-permute-start(bf16[32,1024]{1,0:T(8,128)(2,1)S(1)} %get-tuple-element.44), channel_id=1, source_target_pairs={{0,12},{1,13},{2,14},{3,15},{4,8},{5,9},{6,10},{7,11},{8,4},{9,5},... | collective-permute-start | bytes 196616 | tf_op jit(solution)/shard_map/ppermute | solution.py:231
  13.9 5.9 %collective-permute-start.7 = (bf16[32,1024]{1,0:T(8,128)(2,1)S(1)}, bf16[32,1024]{1,0:T(8,128)(2,1)S(1)}, u32[]{:S(2)}, u32[]{:S(2)}) collective-permute-start(bf16[32,1024]{1,0:T(8,128)(2,1)S(1)} %get-tuple-element.45), channel_id=1, source_target_pairs={{0,14},{1,15},{2,12},{3,13},{4,10},{5,11},{6,8},{7,9},{8,6},{9,7},... | collective-permute-start | bytes 196616 | tf_op jit(solution)/shard_map/ppermute | solution.py:231
  14.9 8.1 %collective-permute-start.10 = (bf16[32,896]{1,0:T(8,128)(2,1)S(1)}, bf16[32,896]{1,0:T(8,128)(2,1)S(1)}, u32[]{:S(2)}, u32[]{:S(2)}) collective-permute-start(bf16[32,896]{1,0:T(8,128)(2,1)S(1)} %get-tuple-element.51), channel_id=1, source_target_pairs={{0,4},{1,5},{2,6},{3,7},{4,0},{5,1},{6,2},{7,3},{8,12},{9,13},{10,... | collective-permute-start | bytes 172040 | tf_op jit(solution)/shard_map/ppermute | solution.py:231
  15.0 9.1 %collective-permute-start.11 = (bf16[32,896]{1,0:T(8,128)(2,1)S(1)}, bf16[32,896]{1,0:T(8,128)(2,1)S(1)}, u32[]{:S(2)}, u32[]{:S(2)}) collective-permute-start(bf16[32,896]{1,0:T(8,128)(2,1)S(1)} %get-tuple-element.52), channel_id=1, source_target_pairs={{0,6},{1,7},{2,4},{3,5},{4,2},{5,3},{6,0},{7,1},{8,14},{9,15},{10,... | collective-permute-start | bytes 172040 | tf_op jit(solution)/shard_map/ppermute | solution.py:231
  16.4 8.3 %collective-permute-start.12 = (bf16[32,896]{1,0:T(8,128)(2,1)S(1)}, bf16[32,896]{1,0:T(8,128)(2,1)S(1)}, u32[]{:S(2)}, u32[]{:S(2)}) collective-permute-start(bf16[32,896]{1,0:T(8,128)(2,1)S(1)} %get-tuple-element.53), channel_id=1, source_target_pairs={{0,8},{1,9},{2,10},{3,11},{4,12},{5,13},{6,14},{7,15},{8,0},{9,1},... | collective-permute-start | bytes 172040 | tf_op jit(solution)/shard_map/ppermute | solution.py:231
  18.6 7.5 %collective-permute-start.13 = (bf16[32,896]{1,0:T(8,128)(2,1)S(1)}, bf16[32,896]{1,0:T(8,128)(2,1)S(1)}, u32[]{:S(2)}, u32[]{:S(2)}) collective-permute-start(bf16[32,896]{1,0:T(8,128)(2,1)S(1)} %get-tuple-element.54), channel_id=1, source_target_pairs={{0,10},{1,11},{2,8},{3,9},{4,14},{5,15},{6,12},{7,13},{8,2},{9,3},... | collective-permute-start | bytes 172040 | tf_op jit(solution)/shard_map/ppermute | solution.py:231
  19.8 6.3 %collective-permute-start.14 = (bf16[32,896]{1,0:T(8,128)(2,1)S(1)}, bf16[32,896]{1,0:T(8,128)(2,1)S(1)}, u32[]{:S(2)}, u32[]{:S(2)}) collective-permute-start(bf16[32,896]{1,0:T(8,128)(2,1)S(1)} %get-tuple-element.55), channel_id=1, source_target_pairs={{0,12},{1,13},{2,14},{3,15},{4,8},{5,9},{6,10},{7,11},{8,4},{9,5},... | collective-permute-start | bytes 172040 | tf_op jit(solution)/shard_map/ppermute | solution.py:231
  22.9 6.2 %collective-permute-start.15 = (bf16[32,896]{1,0:T(8,128)(2,1)S(1)}, bf16[32,896]{1,0:T(8,128)(2,1)S(1)}, u32[]{:S(2)}, u32[]{:S(2)}) collective-permute-start(bf16[32,896]{1,0:T(8,128)(2,1)S(1)} %get-tuple-element.56), channel_id=1, source_target_pairs={{0,14},{1,15},{2,12},{3,13},{4,10},{5,11},{6,8},{7,9},{8,6},{9,7},... | collective-permute-start | bytes 172040 | tf_op jit(solution)/shard_map/ppermute | solution.py:231
  24.1 5.1 %collective-permute-start.9 = (bf16[32,896]{1,0:T(8,128)(2,1)S(1)}, bf16[32,896]{1,0:T(8,128)(2,1)S(1)}, u32[]{:S(2)}, u32[]{:S(2)}) collective-permute-start(bf16[32,896]{1,0:T(8,128)(2,1)S(1)} %get-tuple-element.50), channel_id=1, source_target_pairs={{0,2},{1,3},{2,0},{3,1},{4,6},{5,7},{6,4},{7,5},{8,10},{9,11},{10,... | collective-permute-start | bytes 172040 | tf_op jit(solution)/shard_map/ppermute | solution.py:231
  24.7 11.4 %collective-permute-start.16 = (bf16[128,1024]{1,0:T(8,128)(2,1)S(1)}, bf16[128,1024]{1,0:T(8,128)(2,1)S(1)}, u32[]{:S(2)}, u32[]{:S(2)}) collective-permute-start(bf16[128,1024]{1,0:T(8,128)(2,1)S(1)} %get-tuple-element.46.left_ref), channel_id=1, source_target_pairs={{0,16},{16,0},{1,17},{17,1},{2,18},{18,2},{3,19},{19,3},{4,20},{20... | collective-permute-start | bytes 786440 | tf_op jit(solution)/shard_map/ppermute | solution.py:304
  29.4 7.4 %collective-permute-start.17 = (bf16[128,896]{1,0:T(8,128)(2,1)S(1)}, bf16[128,896]{1,0:T(8,128)(2,1)S(1)}, u32[]{:S(2)}, u32[]{:S(2)}) collective-permute-start(bf16[128,896]{1,0:T(8,128)(2,1)S(1)} %shard_map.68.right_ref), channel_id=1, source_target_pairs={{0,16},{16,0},{1,17},{17,1},{2,18},{18,2},{3,19},{19,3},{4,20},{20... | collective-permute-start | bytes 688136 | tf_op jit(solution)/shard_map/ppermute | solution.py:322
  40.5 2.1 %copy-start.1 = (bf16[1,1920]{1,0:T(2,128)(2,1)S(1)}, bf16[1,1920]{1,0:T(2,128)(2,1)}, u32[]{:S(2)}) copy-start(bf16[1,1920]{1,0:T(2,128)(2,1)} %centroid_ref.1) | copy-start | bytes 11524
  40.5 9.3 %collective-permute-start.18 = (bf16[128,1536]{1,0:T(8,128)(2,1)S(1)}, bf16[128,1536]{1,0:T(8,128)(2,1)S(1)}, u32[]{:S(2)}, u32[]{:S(2)}) collective-permute-start(bf16[128,1536]{1,0:T(8,128)(2,1)S(1)} %get-tuple-element.62), channel_id=1, source_target_pairs={{16,0},{0,16},{17,1},{1,17},{18,2},{2,18},{19,3},{3,19},{20,4},{4,... | collective-permute-start | bytes 1179656 | tf_op jit(solution)/shard_map/ppermute | solution.py:343
  42.2 39.7 %copy-start = (bf16[128,1920]{1,0:T(8,128)(2,1)S(1)}, bf16[128,1920]{1,0:T(8,128)(2,1)}, u32[]{:S(2)}) copy-start(bf16[128,1920]{1,0:T(8,128)(2,1)} %tokens_ref.1) | copy-start | bytes 1474564
  42.3 7.5 %collective-permute-start.19 = (bf16[128,384]{1,0:T(8,128)(2,1)S(1)}, bf16[128,384]{1,0:T(8,128)(2,1)S(1)}, u32[]{:S(2)}, u32[]{:S(2)}) collective-permute-start(bf16[128,384]{1,0:T(8,128)(2,1)S(1)} %shard_map.72), channel_id=1, source_target_pairs={{16,0},{0,16},{17,1},{1,17},{18,2},{2,18},{19,3},{3,19},{20,4},{4,... | collective-permute-start | bytes 294920 | tf_op jit(solution)/shard_map/ppermute | solution.py:351

commit v6 on v5

--- a/solution.py
+++ b/solution.py
@@ -83,12 +83,12 @@
 
 def pack_kernel(targets, experts, capacity, cut, *refs):
     assign_ref, tokens_ref, gain_ref = refs[:3]
-    halves = refs[3 : 3 + targets], refs[3 + targets : 3 + 2 * targets]
-    place_ref, gain_out, assign_buf, tokens_buf, sems = refs[3 + 2 * targets :]
+    left_refs = refs[3 : 3 + targets]
+    place_ref, packing_ref, gain_out, assign_buf, tokens_buf, sems = refs[3 + targets :]
     tok_count = tokens_ref.shape[0]
     slot_total = place_ref.shape[0]
     get_assign, *others = fetch(
-        (assign_ref, tokens_ref, gain_ref),
+        (assign_ref, tokens_ref.at[:, pl.ds(0, cut)], gain_ref),
         (assign_buf, tokens_buf, gain_out),
         sems,
     )
@@ -105,12 +105,21 @@
     place = (rows == assign * capacity + position).astype(F32)
     taken = jnp.sum(place, axis=1, keepdims=True)
     place = place.astype(BF16)
+    packing_ref[...] = place
     for copy in others:
         copy.wait()
     packed = dot(place, tokens_buf[...])
     packed = jnp.where(taken > 0.5, packed, EMPTY).astype(BF16)
-    put_slots(packed[:, :cut], halves[0], capacity)
-    put_slots(packed[:, cut:], halves[1], capacity)
+    put_slots(packed, left_refs, capacity)
+
+
+def pack_rest_kernel(capacity, packing_ref, tokens_ref, *refs):
+    *right_refs, tokens_buf, sems = refs
+    width = tokens_buf.shape[1]
+    cut = tokens_ref.shape[1] - width
+    (copy,) = fetch((tokens_ref.at[:, pl.ds(cut, width)],), (tokens_buf,), sems)
+    copy.wait()
+    put_slots(dot(packing_ref[...], tokens_buf[...]).astype(BF16), right_refs, capacity)
 
 
 def load_kernel(inner_ref, outer_ref, _, inner_out, outer_out, sems):
@@ -270,10 +279,11 @@
     back_widths = (back_cut, features - back_cut)
     move_flops = slot_total * tok_count * features
     half_bytes = 2 * slot_total * features
-    *packed, place, gain = call(
+    *left_packed, place, packing, gain = call(
         functools.partial(pack_kernel, targets, experts, capacity, cut),
-        [shape(slot_total // targets, w) for w in widths for _ in range(targets)]
+        [shape(slot_total // targets, cut) for _ in range(targets)]
         + [
+            shape(slot_total, tok_count),
             shape(slot_total, tok_count),
             pltpu.VMEM((1, features), F32),
         ],
@@ -283,15 +293,24 @@
         [FAR] * 3,
         [
             pltpu.VMEM((1, tok_count), jnp.int32),
-            pltpu.VMEM((tok_count, features), BF16),
+            pltpu.VMEM((tok_count, cut), BF16),
             pltpu.SemaphoreType.DMA((3,)),
         ],
     )
+    right_packed = call(
+        functools.partial(pack_rest_kernel, capacity),
+        [shape(slot_total // targets, widths[1]) for _ in range(targets)],
+        [packing, stay(tokens)],
+        move_flops,
+        half_bytes,
+        [LOCAL, FAR],
+        [pltpu.VMEM((tok_count, widths[1]), BF16), pltpu.SemaphoreType.DMA((1,))],
+    )
     if targets == 2:
-        first = exchange(packed[:targets], experts, capacity)
-        second = exchange(packed[targets:], experts, capacity, first[experts // 4])
+        first = exchange(left_packed, experts, capacity)
+        second = exchange(right_packed, experts, capacity, first[experts // 4])
     else:
-        first, second = [together(packed[0])], [together(packed[1])]
+        first, second = [together(left_packed[0])], [together(right_packed[0])]
     rows, select = call(
         first_kernel,
         [shape(tok_count, cut), shape(tok_count, slot_total)],

time: 83.3 us -> 83.5 us (level)
  waiting for transfers between devices: 8.04 us -> 5.01 us
  blocking collectives: 31.6 us -> 34.1 us
  Pallas kernels: 17.6 us -> 18.6 us
    all_to_all x1, blocking collectives: 31.6 us -> 34.1 us  [together(): lax.all_to_all(rows, 'expert', split_axis=0, concat_axis=0, tiled=True)]
    ppermute x16, waiting for transfers between devices: 4.28 us -> 2.92 us  [swap(): lax.ppermute(array, 'expert', [(i, i ^ axis_mask) for i in range(experts)])]
    ppermute x1, waiting for transfers between devices: 3.18 us -> 2.08 us  [body(): right_parts.append(lax.ppermute(right_part, 'dp', back[k]))]
    pallas_call x11 -> x12, Pallas kernels: 17.6 us -> 18.6 us  [call(): pl.pallas_call(kernel, out_shape=tuple(outs), in_specs=[LOCAL] * len(args...]
  transfers between devices with their start and end apart: 20 -> 20, of which waited for: 5 -> 4; matrix products, arithmetic and copies ran while one was open for 0% -> 0% of each run, Pallas kernels for 13% -> 14%
where the time goes in v6:
time: 83.5 us; the launch traced here: 83.3 us
  blocking collectives  34.1 us (41%)
  starting transfers between devices  25.5 us (31%)
  Pallas kernels  18.6 us (22%)
  waiting for transfers between devices  5.01 us (6%)
    all_to_all x1, blocking collectives, together(): lax.all_to_all(rows, 'expert', split_axis=0, concat_axis=0, tiled=True)  34.1 us
    ppermute x16, starting transfers between devices, swap(): lax.ppermute(array, 'expert', [(i, i ^ axis_mask) for i in range(experts)])  21.3 us
    pallas_call x12, Pallas kernels, call(): pl.pallas_call(kernel, out_shape=tuple(outs), in_specs=[LOCAL] * len(args...  18.6 us
    ppermute x16, waiting for transfers between devices, swap(): lax.ppermute(array, 'expert', [(i, i ^ axis_mask) for i in range(experts)])  2.92 us
    ppermute x1, waiting for transfers between devices, body(): right_parts.append(lax.ppermute(right_part, 'dp', back[k]))  2.08 us
  transfers between devices with their start and end apart: 20, of which 4 were waited for; matrix products, arithmetic and copies ran while one was open for 0% of the time, Pallas kernels for 14%

profile of v6, /device:TPU:1, one launch (start us, length us, event | category | flops | bytes accessed | tf_op | source)
XLA Modules:
  0.0 83.3 jit_solution(2057006034316022240)
XLA Ops:
  0.0 1.3 %shard_map.64 = (bf16[128,1024]{1,0:T(8,128)(2,1)S(1)}, bf16[128,1024]{1,0:T(8,128)(2,1)S(1)}, bf16[256,128]{1,0:T(8,128)(2,1)S(1)}, bf16[256,128]{1,0:T(8,128)(2,1)S(1)}, f32[1,1920]{1,0:T(1,128)S(1)}) custom-call(s32[1,128]{1,0:T(1,128)} %bitcast.9, bf16[128,1920]{1,0:T(8,128)(2,1)} %tokens_ref.3, f32[1,1920]{1,0:T(1,128)} %refs_2_.1), custom_call_target="tpu_custom_call" | custom-call | flops 125829120 | bytes 1966080 | tf_op jit(solution)/shard_map/pallas_call | solution.py:26
  1.3 0.1 collective-permute-start
  1.4 1.2 %shard_map.67 = (bf16[128,896]{1,0:T(8,128)(2,1)S(1)}, bf16[128,896]{1,0:T(8,128)(2,1)S(1)}) custom-call(bf16[256,128]{1,0:T(8,128)(2,1)S(1)} %get-tuple-element.48.packing_ref, bf16[128,1920]{1,0:T(8,128)(2,1)} %tokens_ref.3), custom_call_target="tpu_custom_call" | custom-call | flops 62914560 | bytes 983040 | tf_op jit(solution)/shard_map/pallas_call | solution.py:26
  2.6 0.5 collective-permute-start.8
  3.2 0.0 collective-permute-done.crossed_ref
  3.2 3.4 %collective-permute-start.4 = (bf16[32,1024]{1,0:T(8,128)(2,1)S(1)}, bf16[32,1024]{1,0:T(8,128)(2,1)S(1)}, u32[]{:S(2)}, u32[]{:S(2)}) collective-permute-start(bf16[32,1024]{1,0:T(8,128)(2,1)S(1)} %get-tuple-element.43), channel_id=1, source_target_pairs={{0,8},{1,9},{2,10},{3,11},{4,12},{5,13},{6,14},{7,15},{8,0},{9,1},... | collective-permute-start | bytes 196616 | tf_op jit(solution)/shard_map/ppermute | solution.py:240
  6.6 1.2 %collective-permute-start.1 = (bf16[32,1024]{1,0:T(8,128)(2,1)S(1)}, bf16[32,1024]{1,0:T(8,128)(2,1)S(1)}, u32[]{:S(2)}, u32[]{:S(2)}) collective-permute-start(bf16[32,1024]{1,0:T(8,128)(2,1)S(1)} %get-tuple-element.40), channel_id=1, source_target_pairs={{0,2},{1,3},{2,0},{3,1},{4,6},{5,7},{6,4},{7,5},{8,10},{9,11},{10,... | collective-permute-start | bytes 196616 | tf_op jit(solution)/shard_map/ppermute | solution.py:240
  7.8 1.3 %collective-permute-start.2 = (bf16[32,1024]{1,0:T(8,128)(2,1)S(1)}, bf16[32,1024]{1,0:T(8,128)(2,1)S(1)}, u32[]{:S(2)}, u32[]{:S(2)}) collective-permute-start(bf16[32,1024]{1,0:T(8,128)(2,1)S(1)} %get-tuple-element.41), channel_id=1, source_target_pairs={{0,4},{1,5},{2,6},{3,7},{4,0},{5,1},{6,2},{7,3},{8,12},{9,13},{10,... | collective-permute-start | bytes 196616 | tf_op jit(solution)/shard_map/ppermute | solution.py:240
  9.1 0.1 collective-permute-start.3
  9.2 0.0 collective-permute-done.8.crossed_ref
  9.2 1.0 %collective-permute-start.5 = (bf16[32,1024]{1,0:T(8,128)(2,1)S(1)}, bf16[32,1024]{1,0:T(8,128)(2,1)S(1)}, u32[]{:S(2)}, u32[]{:S(2)}) collective-permute-start(bf16[32,1024]{1,0:T(8,128)(2,1)S(1)} %get-tuple-element.44), channel_id=1, source_target_pairs={{0,10},{1,11},{2,8},{3,9},{4,14},{5,15},{6,12},{7,13},{8,2},{9,3},... | collective-permute-start | bytes 196616 | tf_op jit(solution)/shard_map/ppermute | solution.py:240
  10.3 0.0 collective-permute-done.4.refs_4_._
  10.3 3.4 %collective-permute-start.6 = (bf16[32,1024]{1,0:T(8,128)(2,1)S(1)}, bf16[32,1024]{1,0:T(8,128)(2,1)S(1)}, u32[]{:S(2)}, u32[]{:S(2)}) collective-permute-start(bf16[32,1024]{1,0:T(8,128)(2,1)S(1)} %get-tuple-element.45), channel_id=1, source_target_pairs={{0,12},{1,13},{2,14},{3,15},{4,8},{5,9},{6,10},{7,11},{8,4},{9,5},... | collective-permute-start | bytes 196616 | tf_op jit(solution)/shard_map/ppermute | solution.py:240
  13.7 0.0 collective-permute-done.1.refs_1_
  13.7 0.9 %collective-permute-start.7 = (bf16[32,1024]{1,0:T(8,128)(2,1)S(1)}, bf16[32,1024]{1,0:T(8,128)(2,1)S(1)}, u32[]{:S(2)}, u32[]{:S(2)}) collective-permute-start(bf16[32,1024]{1,0:T(8,128)(2,1)S(1)} %get-tuple-element.46), channel_id=1, source_target_pairs={{0,14},{1,15},{2,12},{3,13},{4,10},{5,11},{6,8},{7,9},{8,6},{9,7},... | collective-permute-start | bytes 196616 | tf_op jit(solution)/shard_map/ppermute | solution.py:240
  14.6 0.0 collective-permute-done.2.refs_2_
  14.7 0.1 collective-permute-start.10
  14.7 0.0 collective-permute-done.3.refs_3_
  14.7 1.4 %collective-permute-start.11 = (bf16[32,896]{1,0:T(8,128)(2,1)S(1)}, bf16[32,896]{1,0:T(8,128)(2,1)S(1)}, u32[]{:S(2)}, u32[]{:S(2)}) collective-permute-start(bf16[32,896]{1,0:T(8,128)(2,1)S(1)} %get-tuple-element.54), channel_id=1, source_target_pairs={{0,6},{1,7},{2,4},{3,5},{4,2},{5,3},{6,0},{7,1},{8,14},{9,15},{10,... | collective-permute-start | bytes 172040 | tf_op jit(solution)/shard_map/ppermute | solution.py:240
  16.2 0.0 collective-permute-done.5.refs_5_
  16.2 2.1 %collective-permute-start.12 = (bf16[32,896]{1,0:T(8,128)(2,1)S(1)}, bf16[32,896]{1,0:T(8,128)(2,1)S(1)}, u32[]{:S(2)}, u32[]{:S(2)}) collective-permute-start(bf16[32,896]{1,0:T(8,128)(2,1)S(1)} %get-tuple-element.55), channel_id=1, source_target_pairs={{0,8},{1,9},{2,10},{3,11},{4,12},{5,13},{6,14},{7,15},{8,0},{9,1},... | collective-permute-start | bytes 172040 | tf_op jit(solution)/shard_map/ppermute | solution.py:240
  18.3 0.0 collective-permute-done.6.refs_6_
  18.3 1.1 %collective-permute-start.13 = (bf16[32,896]{1,0:T(8,128)(2,1)S(1)}, bf16[32,896]{1,0:T(8,128)(2,1)S(1)}, u32[]{:S(2)}, u32[]{:S(2)}) collective-permute-start(bf16[32,896]{1,0:T(8,128)(2,1)S(1)} %get-tuple-element.56), channel_id=1, source_target_pairs={{0,10},{1,11},{2,8},{3,9},{4,14},{5,15},{6,12},{7,13},{8,2},{9,3},... | collective-permute-start | bytes 172040 | tf_op jit(solution)/shard_map/ppermute | solution.py:240
  19.5 0.2 collective-permute-done.7.refs_7_
  19.6 3.1 %collective-permute-start.14 = (bf16[32,896]{1,0:T(8,128)(2,1)S(1)}, bf16[32,896]{1,0:T(8,128)(2,1)S(1)}, u32[]{:S(2)}, u32[]{:S(2)}) collective-permute-start(bf16[32,896]{1,0:T(8,128)(2,1)S(1)} %get-tuple-element.57), channel_id=1, source_target_pairs={{0,12},{1,13},{2,14},{3,15},{4,8},{5,9},{6,10},{7,11},{8,4},{9,5},... | collective-permute-start | bytes 172040 | tf_op jit(solution)/shard_map/ppermute | solution.py:240
  22.7 0.0 collective-permute-done.10.refs_2_
  22.7 1.1 %collective-permute-start.15 = (bf16[32,896]{1,0:T(8,128)(2,1)S(1)}, bf16[32,896]{1,0:T(8,128)(2,1)S(1)}, u32[]{:S(2)}, u32[]{:S(2)}) collective-permute-start(bf16[32,896]{1,0:T(8,128)(2,1)S(1)} %get-tuple-element.58), channel_id=1, source_target_pairs={{0,14},{1,15},{2,12},{3,13},{4,10},{5,11},{6,8},{7,9},{8,6},{9,7},... | collective-permute-start | bytes 172040 | tf_op jit(solution)/shard_map/ppermute | solution.py:240
  23.8 0.0 collective-permute-done.11.refs_3_
  23.8 0.3 collective-permute-start.9
  24.1 0.5 shard_map.66
  24.6 0.0 collective-permute-done.12.refs_4_
  24.6 1.3 %collective-permute-start.16 = (bf16[128,1024]{1,0:T(8,128)(2,1)S(1)}, bf16[128,1024]{1,0:T(8,128)(2,1)S(1)}, u32[]{:S(2)}, u32[]{:S(2)}) collective-permute-start(bf16[128,1024]{1,0:T(8,128)(2,1)S(1)} %get-tuple-element.47.left_ref), channel_id=1, source_target_pairs={{0,16},{16,0},{1,17},{17,1},{2,18},{18,2},{3,19},{19,3},{4,20},{20... | collective-permute-start | bytes 786440 | tf_op jit(solution)/shard_map/ppermute | solution.py:323
  25.9 0.0 collective-permute-done.13.refs_5_
  25.9 0.1 collective-permute-done.14.refs_6_
  26.0 2.6 %collective-permute-done.15.refs_7_ = bf16[32,896]{1,0:T(8,128)(2,1)S(1)} collective-permute-done((bf16[32,896]{1,0:T(8,128)(2,1)S(1)}, bf16[32,896]{1,0:T(8,128)(2,1)S(1)}, u32[]{:S(2)}, u32[]{:S(2)}) %collective-permute-start.15) | collective-permute-done | bytes 57376 | tf_op jit(solution)/shard_map/ppermute | solution.py:240
  28.6 0.0 collective-permute-done.9.refs_1_
  28.6 0.2 shard_map.69.right_ref
  28.8 1.3 %collective-permute-start.17 = (bf16[128,896]{1,0:T(8,128)(2,1)S(1)}, bf16[128,896]{1,0:T(8,128)(2,1)S(1)}, u32[]{:S(2)}, u32[]{:S(2)}) collective-permute-start(bf16[128,896]{1,0:T(8,128)(2,1)S(1)} %shard_map.69.right_ref), channel_id=1, source_target_pairs={{0,16},{16,0},{1,17},{17,1},{2,18},{18,2},{3,19},{19,3},{4,20},{20... | collective-permute-start | bytes 688136 | tf_op jit(solution)/shard_map/ppermute | solution.py:341
  30.2 5.5 %shard_map.70 = (bf16[2048,1920]{1,0:T(8,128)(2,1)S(1)}, bf16[2048,1920]{1,0:T(8,128)(2,1)S(1)}) custom-call(bf16[2048,1920]{1,0:T(8,128)(2,1)} %bitcast.7, bf16[2048,1920]{1,0:T(8,128)(2,1)} %bitcast.8, bf16[128,256]{1,0:T(8,128)(2,1)S(1)} %get-tuple-element.59.refs_8_._.refs_5_), custom_call_target="tpu_custom_call" | custom-call | bytes 31457280 | tf_op jit(solution)/shard_map/pallas_call | solution.py:26
  35.6 0.0 collective-permute-done.16.left_ref
  35.7 0.0 collective-permute-done.17.right_ref
  35.7 3.7 %shard_map.72 = (bf16[128,1536]{1,0:T(8,128)(2,1)S(1)}, bf16[128,2048]{1,0:T(8,128)(2,1)S(1)}) custom-call(bf16[128,1024]{1,0:T(8,128)(2,1)S(1)} %collective-permute-done.16.left_ref, bf16[128,896]{1,0:T(8,128)(2,1)S(1)} %collective-permute-done.17.right_ref, f32[1,1920]{1,0:T(1,128)S(1)} %get-tuple-element.60.gain_ref, ...), custom_call_target="tpu_custom_call" | custom-call | flops 3019898880 | bytes 983040 | tf_op jit(solution)/shard_map/pallas_call | solution.py:26
  39.4 0.0 copy-start.1
  39.4 1.0 %collective-permute-start.18 = (bf16[128,1536]{1,0:T(8,128)(2,1)S(1)}, bf16[128,1536]{1,0:T(8,128)(2,1)S(1)}, u32[]{:S(2)}, u32[]{:S(2)}) collective-permute-start(bf16[128,1536]{1,0:T(8,128)(2,1)S(1)} %get-tuple-element.64), channel_id=1, source_target_pairs={{16,0},{0,16},{17,1},{1,17},{18,2},{2,18},{19,3},{3,19},{20,4},{4,... | collective-permute-start | bytes 1179656 | tf_op jit(solution)/shard_map/ppermute | solution.py:362
  40.4 0.4 shard_map.73
  40.8 0.0 copy-start
  40.8 0.6 collective-permute-start.19
  41.5 0.0 copy-done.1
  41.5 4.0 %shard_map.71 = (bf16[128,1536]{1,0:T(8,128)(2,1)S(1)}, bf16[128,384]{1,0:T(8,128)(2,1)S(1)}, f32[128,128]{1,0:T(8,128)S(1)}) custom-call(bf16[128,1024]{1,0:T(8,128)(2,1)S(1)} %get-tuple-element.47.left_ref, bf16[128,896]{1,0:T(8,128)(2,1)S(1)} %shard_map.69.right_ref, f32[1,1920]{1,0:T(1,128)S(1)} %get-tuple-element.60.gain_ref, ...), custom_call_target="tpu_custom_call" | custom-call | flops 4026531840 | bytes 983040 | tf_op jit(solution)/shard_map/pallas_call | solution.py:26
  45.5 2.1 %collective-permute-done.19.refs_3_ = bf16[128,384]{1,0:T(8,128)(2,1)S(1)} collective-permute-done((bf16[128,384]{1,0:T(8,128)(2,1)S(1)}, bf16[128,384]{1,0:T(8,128)(2,1)S(1)}, u32[]{:S(2)}, u32[]{:S(2)}) %collective-permute-start.19) | collective-permute-done | bytes 98336 | tf_op jit(solution)/shard_map/ppermute | solution.py:370
  47.6 0.0 collective-permute-done.18.refs_1_
  47.6 0.5 shard_map.74
  48.1 34.1 %all_to_all.11 = bf16[16,16,1920]{2,1,0:T(8,128)(2,1)S(1)} all-to-all(bf16[16,16,1920]{2,1,0:T(8,128)(2,1)S(1)} %bitcast.5), channel_id=1, replica_groups=mesh['dp'=2,'expert'=16] {'expert'}, dimensions={0} | all-to-all | bytes 1966080 | tf_op jit(solution)/shard_map/all_to_all | solution.py:265
  82.2 0.0 copy-done
  82.2 1.1 %shard_map.75 = bf16[128,1920]{1,0:T(8,128)(2,1)} custom-call(bf16[128,1920]{1,0:T(8,128)(2,1)S(1)} %copy-done, bf16[256,1920]{1,0:T(8,128)(2,1)S(1)} %bitcast.6, bf16[256,128]{1,0:T(8,128)(2,1)S(1)} %get-tuple-element.68.place_ref), custom_call_target="tpu_custom_call" | custom-call | flops 125829120 | bytes 1966080 | tf_op jit(solution)/shard_map/pallas_call | solution.py:26
  (2 shorter events, 0.1 us)
Async XLA Ops:
  1.3 1.9 %collective-permute-start = (bf16[128,1024]{1,0:T(8,128)(2,1)S(1)}, bf16[128,1024]{1,0:T(8,128)(2,1)S(1)}, u32[]{:S(2)}, u32[]{:S(2)}) collective-permute-start(bf16[128,1024]{1,0:T(8,128)(2,1)S(1)} %get-tuple-element.38), channel_id=1, source_target_pairs={{0,1},{1,0},{2,3},{3,2},{4,5},{5,4},{6,7},{7,6},{8,9},{9,8},{10,11... | collective-permute-start | bytes 786440 | tf_op jit(solution)/shard_map/ppermute | solution.py:240
  2.6 6.6 %collective-permute-start.8 = (bf16[128,896]{1,0:T(8,128)(2,1)S(1)}, bf16[128,896]{1,0:T(8,128)(2,1)S(1)}, u32[]{:S(2)}, u32[]{:S(2)}) collective-permute-start(bf16[128,896]{1,0:T(8,128)(2,1)S(1)} %get-tuple-element.50), channel_id=1, source_target_pairs={{0,1},{1,0},{2,3},{3,2},{4,5},{5,4},{6,7},{7,6},{8,9},{9,8},{10,11... | collective-permute-start | bytes 688136 | tf_op jit(solution)/shard_map/ppermute | solution.py:240
  3.2 7.1 %collective-permute-start.4 = (bf16[32,1024]{1,0:T(8,128)(2,1)S(1)}, bf16[32,1024]{1,0:T(8,128)(2,1)S(1)}, u32[]{:S(2)}, u32[]{:S(2)}) collective-permute-start(bf16[32,1024]{1,0:T(8,128)(2,1)S(1)} %get-tuple-element.43), channel_id=1, source_target_pairs={{0,8},{1,9},{2,10},{3,11},{4,12},{5,13},{6,14},{7,15},{8,0},{9,1},... | collective-permute-start | bytes 196616 | tf_op jit(solution)/shard_map/ppermute | solution.py:240
  6.6 7.1 %collective-permute-start.1 = (bf16[32,1024]{1,0:T(8,128)(2,1)S(1)}, bf16[32,1024]{1,0:T(8,128)(2,1)S(1)}, u32[]{:S(2)}, u32[]{:S(2)}) collective-permute-start(bf16[32,1024]{1,0:T(8,128)(2,1)S(1)} %get-tuple-element.40), channel_id=1, source_target_pairs={{0,2},{1,3},{2,0},{3,1},{4,6},{5,7},{6,4},{7,5},{8,10},{9,11},{10,... | collective-permute-start | bytes 196616 | tf_op jit(solution)/shard_map/ppermute | solution.py:240
  7.8 6.8 %collective-permute-start.2 = (bf16[32,1024]{1,0:T(8,128)(2,1)S(1)}, bf16[32,1024]{1,0:T(8,128)(2,1)S(1)}, u32[]{:S(2)}, u32[]{:S(2)}) collective-permute-start(bf16[32,1024]{1,0:T(8,128)(2,1)S(1)} %get-tuple-element.41), channel_id=1, source_target_pairs={{0,4},{1,5},{2,6},{3,7},{4,0},{5,1},{6,2},{7,3},{8,12},{9,13},{10,... | collective-permute-start | bytes 196616 | tf_op jit(solution)/shard_map/ppermute | solution.py:240
  9.1 5.6 %collective-permute-start.3 = (bf16[32,1024]{1,0:T(8,128)(2,1)S(1)}, bf16[32,1024]{1,0:T(8,128)(2,1)S(1)}, u32[]{:S(2)}, u32[]{:S(2)}) collective-permute-start(bf16[32,1024]{1,0:T(8,128)(2,1)S(1)} %get-tuple-element.42), channel_id=1, source_target_pairs={{0,6},{1,7},{2,4},{3,5},{4,2},{5,3},{6,0},{7,1},{8,14},{9,15},{10,... | collective-permute-start | bytes 196616 | tf_op jit(solution)/shard_map/ppermute | solution.py:240
  9.2 6.9 %collective-permute-start.5 = (bf16[32,1024]{1,0:T(8,128)(2,1)S(1)}, bf16[32,1024]{1,0:T(8,128)(2,1)S(1)}, u32[]{:S(2)}, u32[]{:S(2)}) collective-permute-start(bf16[32,1024]{1,0:T(8,128)(2,1)S(1)} %get-tuple-element.44), channel_id=1, source_target_pairs={{0,10},{1,11},{2,8},{3,9},{4,14},{5,15},{6,12},{7,13},{8,2},{9,3},... | collective-permute-start | bytes 196616 | tf_op jit(solution)/shard_map/ppermute | solution.py:240
  10.3 8.1 %collective-permute-start.6 = (bf16[32,1024]{1,0:T(8,128)(2,1)S(1)}, bf16[32,1024]{1,0:T(8,128)(2,1)S(1)}, u32[]{:S(2)}, u32[]{:S(2)}) collective-permute-start(bf16[32,1024]{1,0:T(8,128)(2,1)S(1)} %get-tuple-element.45), channel_id=1, source_target_pairs={{0,12},{1,13},{2,14},{3,15},{4,8},{5,9},{6,10},{7,11},{8,4},{9,5},... | collective-permute-start | bytes 196616 | tf_op jit(solution)/shard_map/ppermute | solution.py:240
  13.7 6.0 %collective-permute-start.7 = (bf16[32,1024]{1,0:T(8,128)(2,1)S(1)}, bf16[32,1024]{1,0:T(8,128)(2,1)S(1)}, u32[]{:S(2)}, u32[]{:S(2)}) collective-permute-start(bf16[32,1024]{1,0:T(8,128)(2,1)S(1)} %get-tuple-element.46), channel_id=1, source_target_pairs={{0,14},{1,15},{2,12},{3,13},{4,10},{5,11},{6,8},{7,9},{8,6},{9,7},... | collective-permute-start | bytes 196616 | tf_op jit(solution)/shard_map/ppermute | solution.py:240
  14.7 8.1 %collective-permute-start.10 = (bf16[32,896]{1,0:T(8,128)(2,1)S(1)}, bf16[32,896]{1,0:T(8,128)(2,1)S(1)}, u32[]{:S(2)}, u32[]{:S(2)}) collective-permute-start(bf16[32,896]{1,0:T(8,128)(2,1)S(1)} %get-tuple-element.53), channel_id=1, source_target_pairs={{0,4},{1,5},{2,6},{3,7},{4,0},{5,1},{6,2},{7,3},{8,12},{9,13},{10,... | collective-permute-start | bytes 172040 | tf_op jit(solution)/shard_map/ppermute | solution.py:240
  14.7 9.0 %collective-permute-start.11 = (bf16[32,896]{1,0:T(8,128)(2,1)S(1)}, bf16[32,896]{1,0:T(8,128)(2,1)S(1)}, u32[]{:S(2)}, u32[]{:S(2)}) collective-permute-start(bf16[32,896]{1,0:T(8,128)(2,1)S(1)} %get-tuple-element.54), channel_id=1, source_target_pairs={{0,6},{1,7},{2,4},{3,5},{4,2},{5,3},{6,0},{7,1},{8,14},{9,15},{10,... | collective-permute-start | bytes 172040 | tf_op jit(solution)/shard_map/ppermute | solution.py:240
  16.2 8.4 %collective-permute-start.12 = (bf16[32,896]{1,0:T(8,128)(2,1)S(1)}, bf16[32,896]{1,0:T(8,128)(2,1)S(1)}, u32[]{:S(2)}, u32[]{:S(2)}) collective-permute-start(bf16[32,896]{1,0:T(8,128)(2,1)S(1)} %get-tuple-element.55), channel_id=1, source_target_pairs={{0,8},{1,9},{2,10},{3,11},{4,12},{5,13},{6,14},{7,15},{8,0},{9,1},... | collective-permute-start | bytes 172040 | tf_op jit(solution)/shard_map/ppermute | solution.py:240
  18.3 7.5 %collective-permute-start.13 = (bf16[32,896]{1,0:T(8,128)(2,1)S(1)}, bf16[32,896]{1,0:T(8,128)(2,1)S(1)}, u32[]{:S(2)}, u32[]{:S(2)}) collective-permute-start(bf16[32,896]{1,0:T(8,128)(2,1)S(1)} %get-tuple-element.56), channel_id=1, source_target_pairs={{0,10},{1,11},{2,8},{3,9},{4,14},{5,15},{6,12},{7,13},{8,2},{9,3},... | collective-permute-start | bytes 172040 | tf_op jit(solution)/shard_map/ppermute | solution.py:240
  19.6 6.4 %collective-permute-start.14 = (bf16[32,896]{1,0:T(8,128)(2,1)S(1)}, bf16[32,896]{1,0:T(8,128)(2,1)S(1)}, u32[]{:S(2)}, u32[]{:S(2)}) collective-permute-start(bf16[32,896]{1,0:T(8,128)(2,1)S(1)} %get-tuple-element.57), channel_id=1, source_target_pairs={{0,12},{1,13},{2,14},{3,15},{4,8},{5,9},{6,10},{7,11},{8,4},{9,5},... | collective-permute-start | bytes 172040 | tf_op jit(solution)/shard_map/ppermute | solution.py:240
  22.7 5.9 %collective-permute-start.15 = (bf16[32,896]{1,0:T(8,128)(2,1)S(1)}, bf16[32,896]{1,0:T(8,128)(2,1)S(1)}, u32[]{:S(2)}, u32[]{:S(2)}) collective-permute-start(bf16[32,896]{1,0:T(8,128)(2,1)S(1)} %get-tuple-element.58), channel_id=1, source_target_pairs={{0,14},{1,15},{2,12},{3,13},{4,10},{5,11},{6,8},{7,9},{8,6},{9,7},... | collective-permute-start | bytes 172040 | tf_op jit(solution)/shard_map/ppermute | solution.py:240
  23.8 4.8 %collective-permute-start.9 = (bf16[32,896]{1,0:T(8,128)(2,1)S(1)}, bf16[32,896]{1,0:T(8,128)(2,1)S(1)}, u32[]{:S(2)}, u32[]{:S(2)}) collective-permute-start(bf16[32,896]{1,0:T(8,128)(2,1)S(1)} %get-tuple-element.52), channel_id=1, source_target_pairs={{0,2},{1,3},{2,0},{3,1},{4,6},{5,7},{6,4},{7,5},{8,10},{9,11},{10,... | collective-permute-start | bytes 172040 | tf_op jit(solution)/shard_map/ppermute | solution.py:240
  24.6 11.1 %collective-permute-start.16 = (bf16[128,1024]{1,0:T(8,128)(2,1)S(1)}, bf16[128,1024]{1,0:T(8,128)(2,1)S(1)}, u32[]{:S(2)}, u32[]{:S(2)}) collective-permute-start(bf16[128,1024]{1,0:T(8,128)(2,1)S(1)} %get-tuple-element.47.left_ref), channel_id=1, source_target_pairs={{0,16},{16,0},{1,17},{17,1},{2,18},{18,2},{3,19},{19,3},{4,20},{20... | collective-permute-start | bytes 786440 | tf_op jit(solution)/shard_map/ppermute | solution.py:323
  28.8 6.8 %collective-permute-start.17 = (bf16[128,896]{1,0:T(8,128)(2,1)S(1)}, bf16[128,896]{1,0:T(8,128)(2,1)S(1)}, u32[]{:S(2)}, u32[]{:S(2)}) collective-permute-start(bf16[128,896]{1,0:T(8,128)(2,1)S(1)} %shard_map.69.right_ref), channel_id=1, source_target_pairs={{0,16},{16,0},{1,17},{17,1},{2,18},{18,2},{3,19},{19,3},{4,20},{20... | collective-permute-start | bytes 688136 | tf_op jit(solution)/shard_map/ppermute | solution.py:341
  39.4 2.1 %copy-start.1 = (bf16[1,1920]{1,0:T(2,128)(2,1)S(1)}, bf16[1,1920]{1,0:T(2,128)(2,1)}, u32[]{:S(2)}) copy-start(bf16[1,1920]{1,0:T(2,128)(2,1)} %centroid_ref.1) | copy-start | bytes 11524
  39.4 8.2 %collective-permute-start.18 = (bf16[128,1536]{1,0:T(8,128)(2,1)S(1)}, bf16[128,1536]{1,0:T(8,128)(2,1)S(1)}, u32[]{:S(2)}, u32[]{:S(2)}) collective-permute-start(bf16[128,1536]{1,0:T(8,128)(2,1)S(1)} %get-tuple-element.64), channel_id=1, source_target_pairs={{16,0},{0,16},{17,1},{1,17},{18,2},{2,18},{19,3},{3,19},{20,4},{4,... | collective-permute-start | bytes 1179656 | tf_op jit(solution)/shard_map/ppermute | solution.py:362
  40.8 41.4 %copy-start = (bf16[128,1920]{1,0:T(8,128)(2,1)S(1)}, bf16[128,1920]{1,0:T(8,128)(2,1)}, u32[]{:S(2)}) copy-start(bf16[128,1920]{1,0:T(8,128)(2,1)} %tokens_ref.3) | copy-start | bytes 1474564
  40.8 6.8 %collective-permute-start.19 = (bf16[128,384]{1,0:T(8,128)(2,1)S(1)}, bf16[128,384]{1,0:T(8,128)(2,1)S(1)}, u32[]{:S(2)}, u32[]{:S(2)}) collective-permute-start(bf16[128,384]{1,0:T(8,128)(2,1)S(1)} %shard_map.73), channel_id=1, source_target_pairs={{16,0},{0,16},{17,1},{1,17},{18,2},{2,18},{19,3},{3,19},{20,4},{4,... | collective-permute-start | bytes 294920 | tf_op jit(solution)/shard_map/ppermute | solution.py:370
